TPU v7x, 128 devices: a whole 4x4x4 slice. The times are simulated.
128 devices in a mesh: attn: 8 (over y, core), ffn: 16 (over x, z).
Axes of the slice: x: 4, y: 4, z: 4, core: 2. Of those that a mesh axis runs over, the one named last changes fastest.
Arguments:
- queries: bfloat16 [512, 16384], P('ffn', 'attn'), may hold values from -6 to 6
- key_cache: bfloat16 [512, 128, 1024], P('ffn', None, 'attn'), may hold values from -6 to 6
- cached_value_rows: bfloat16 [512, 128, 1024], P('ffn', None, 'attn'), may hold values from -6 to 6
- new_key: bfloat16 [512, 1024], P('ffn', 'attn'), may hold values from -6 to 6
- token_value: bfloat16 [512, 1024], P('ffn', 'attn'), may hold values from -6 to 6
- lengths: int32 [512], P('ffn'), may hold values from 1 to 128, as said below
- residual: float32 [512, 16384], P('ffn', 'attn'), may hold values from -14 to 14
- out_weight: bfloat16 [16384, 16384], P('attn', 'ffn'), may hold values from -0.046875 to 0.046875
- norm_gain: bfloat16 [16384], P('attn'), may hold values from 0.099609375 to 1.8984375
- gate_weight: bfloat16 [16384, 26624], P('attn', 'ffn'), may hold values from -0.046875 to 0.046875
- up_weight: bfloat16 [16384, 26624], P('attn', 'ffn'), may hold values from -0.046875 to 0.046875
- down_weight: bfloat16 [26624, 16384], P('ffn', 'attn'), may hold values from -0.0390625 to 0.0390625
Outputs:
- updated: float32 [512, 16384], P('ffn', 'attn')
Inputs may be any that keep to these rules, and one draw needn't show every extreme that they name: lengths[b] is the number of valid cache positions of request b; some request has exactly 128.
All inputs are finite; a program needn't handle non-finite values.
Results may differ from a plain program's by a relative error of at most 0.023.
Values may be sent and summed in bfloat16 or wider, within the bound.
No kernel may reach another device: no remote copies, remote signals or barrier semaphores. Data moves between devices by JAX's collectives and lax.ppermute only.
A program may use at most 128 MiB of HBM per device.

v0:
```python
import jax
import jax.numpy as jnp
from jax import lax
from jax.sharding import PartitionSpec as P

D = 16384
QUERY_HEADS = 128
KEY_VALUE_HEADS = 8
HEAD_SIZE = 128


def attend(queries, key_cache, cached_value_rows, new_key, token_value, lengths):
    count_of_rows = queries.shape[0]
    key_value_heads = new_key.shape[1] // HEAD_SIZE
    cache_len = key_cache.shape[1]
    score_scale = HEAD_SIZE ** (-0.5)
    grouped_query = queries.reshape(
        count_of_rows, key_value_heads, QUERY_HEADS // KEY_VALUE_HEADS, HEAD_SIZE
    )
    cache_keys = key_cache.reshape(count_of_rows, cache_len, key_value_heads, HEAD_SIZE)
    cache_values = cached_value_rows.reshape(count_of_rows, cache_len, key_value_heads, HEAD_SIZE)
    own_keys = new_key.reshape(count_of_rows, key_value_heads, HEAD_SIZE)
    own_values = token_value.reshape(count_of_rows, key_value_heads, 1, HEAD_SIZE).astype(
        jnp.float32
    )
    scores = (
        jnp.einsum("rkgd,rlkd->rkgl", grouped_query, cache_keys, preferred_element_type=jnp.float32)
        * score_scale
    )
    own_score = (
        jnp.einsum("rkgd,rkd->rkg", grouped_query, own_keys, preferred_element_type=jnp.float32)
        * score_scale
    )
    visible = jnp.arange(cache_len, dtype=jnp.int32)[None, :] < lengths[:, None]
    scores = jnp.where(visible[:, None, None, :], scores, -jnp.inf)
    peak_score = jnp.maximum(jnp.max(scores, axis=-1), own_score)
    weights = jnp.exp(scores - peak_score[..., None])
    own_weight = jnp.exp(own_score - peak_score)
    denom_sum = jnp.sum(weights, axis=-1) + own_weight
    weights = (weights / denom_sum[..., None]).astype(jnp.bfloat16)
    own_weight = (own_weight / denom_sum).astype(jnp.bfloat16)
    attended_output = jnp.einsum(
        "rkgl,rlkd->rkgd", weights, cache_values, preferred_element_type=jnp.float32
    )
    attended_output = attended_output + own_weight.astype(jnp.float32)[..., None] * own_values
    return attended_output.astype(jnp.bfloat16).reshape(
        count_of_rows, key_value_heads * (QUERY_HEADS // KEY_VALUE_HEADS) * HEAD_SIZE
    )


def local(
    queries,
    key_cache,
    cached_value_rows,
    new_key,
    token_value,
    lengths,
    residual,
    out_weight,
    norm_gain,
    gate_weight,
    up_weight,
    down_weight,
):
    attended_output = attend(queries, key_cache, cached_value_rows, new_key, token_value, lengths)
    projected = jnp.dot(
        lax.all_gather(attended_output, "ffn", axis=0, tiled=True),
        out_weight,
        preferred_element_type=jnp.float32,
    )
    regrouped = lax.all_to_all(
        projected.astype(jnp.bfloat16), "ffn", split_axis=0, concat_axis=1, tiled=True
    ).astype(projected.dtype)
    summed = lax.psum_scatter(
        regrouped.astype(jnp.bfloat16), "attn", scatter_dimension=1, tiled=True
    ).astype(jnp.float32)
    middle = residual + summed
    local_rows = residual.shape[0]
    total_rows = local_rows * lax.axis_size("ffn")
    row_squares = jnp.sum(middle * middle, axis=1)
    placed = lax.dynamic_update_slice_in_dim(
        jnp.zeros((total_rows,), jnp.float32), row_squares, lax.axis_index("ffn") * local_rows, 0
    )
    squares = lax.psum(placed, ("attn", "ffn"))
    inv_rms = lax.rsqrt(squares / D + 1e-05)
    scaled = (middle * norm_gain.astype(jnp.float32)).astype(jnp.bfloat16)
    hidden_cols = gate_weight.shape[1]
    block_rows = lax.all_gather(scaled, "ffn", axis=0, tiled=True)
    gate_part = jnp.dot(block_rows, gate_weight, preferred_element_type=jnp.float32)
    up_part = jnp.dot(block_rows, up_weight, preferred_element_type=jnp.float32)
    products = jnp.concatenate([gate_part, up_part], axis=1)
    totals = lax.psum(products.astype(jnp.bfloat16), "attn").astype(jnp.float32)
    gate_act = inv_rms[:, None] * totals[:, :hidden_cols]
    up_act = inv_rms[:, None] * totals[:, hidden_cols:]
    hidden = (jax.nn.silu(gate_act) * up_act).astype(jnp.bfloat16)
    block_rows = hidden
    down_out = lax.psum_scatter(
        jnp.dot(block_rows, down_weight, preferred_element_type=jnp.float32).astype(jnp.bfloat16),
        "ffn",
        scatter_dimension=0,
        tiled=True,
    ).astype(jnp.float32)
    return middle + down_out


def solution(mesh):
    placed = (
        P("ffn", "attn"),
        P("ffn", None, "attn"),
        P("ffn", None, "attn"),
        P("ffn", "attn"),
        P("ffn", "attn"),
        P("ffn"),
        P("ffn", "attn"),
        P("attn", "ffn"),
        P("attn"),
        P("attn", "ffn"),
        P("attn", "ffn"),
        P("ffn", "attn"),
    )
    return jax.shard_map(
        local, mesh=mesh, in_specs=placed, out_specs=P("ffn", "attn"), check_vma=False
    )
```

profile of v0, /device:TPU:0, one launch (start us, length us, event | category | flops | bytes accessed | tf_op | source)
XLA Modules:
  0.0 344.6 jit_solution(7711178090769700917)
XLA Ops:
  6.5 0.0 copy-start
  6.5 0.0 all-gather.3.cloned.1.call-start
  6.5 1.0 copy.17
  7.6 0.7 iota_compare_fusion
  8.3 0.9 fusion.10
  9.1 0.0 copy-done
  9.2 0.7 fusion.15
  9.9 0.3 fusion.7
  10.2 0.7 convert_element_type.50
  10.9 1.7 fusion.6
  12.6 0.7 copy.22
  13.3 0.0 all-gather.3.cloned.1.call-update
  13.3 0.0 reduce-scatter.3.cloned.1.call-start
  13.3 47.8 %all-gather.3.cloned.1.call-done = bf16[512,2048]{1,0:T(8,128)(2,1)} async-done(((bf16[32,2048]{1,0:T(8,128)(2,1)}), bf16[512,2048]{1,0:T(8,128)(2,1)}) %all-gather.3.cloned.1.call-update) | async-done | bytes 2097168 | tf_op jit(solution)/shard_map/all_gather | solution.py:67
  61.2 5.2 %convolution_convert_fusion.3 = bf16[512,1024]{1,0:T(8,128)(2,1)S(1)} fusion(bf16[512,2048]{1,0:T(8,128)(2,1)} %all-gather.3.cloned.1.call-done, bf16[2048,1024]{1,0:T(8,128)(2,1)} %param.19), kind=kOutput, calls=%fused_computation.10 | convolution fusion | flops 2148007936 | bytes 7340032 | tf_op jit(solution)/shard_map/dot_general | solution.py:66
  66.3 0.0 copy-start.3
  66.3 0.0 copy-start.1
  66.4 20.9 %all_to_all.19 = bf16[16,32,1024]{2,1,0:T(8,128)(2,1)S(1)} all-to-all(bf16[16,32,1024]{2,1,0:T(8,128)(2,1)S(1)} %bitcast.26), channel_id=1, replica_groups=mesh['attn'=8,'ffn'=16] {'ffn'}, dimensions={0} | all-to-all | bytes 2097152 | tf_op jit(solution)/shard_map/all_to_all | solution.py:71
  87.3 1.1 copy.16
  88.3 0.0 reduce-scatter.3.cloned.1.call-update
  88.4 0.0 all-gather.5.cloned.1.call-start
  88.4 0.0 copy-done.3
  88.4 29.7 %reduce-scatter.3.cloned.1.call-done = bf16[32,2048]{1,0:T(8,128)(2,1)} async-done(((bf16[32,16384]{1,0:T(8,128)(2,1)}), bf16[32,2048]{1,0:T(8,128)(2,1)}) %reduce-scatter.3.cloned.1.call-update) | async-done | bytes 131088 | tf_op jit(solution)/shard_map/reduce_scatter | solution.py:74
  118.1 0.0 copy-done.1
  118.1 1.7 multiply_reduce_fusion
  119.8 0.0 all-gather.5.cloned.1.call-update
  119.9 0.0 all-reduce.2.cloned.1.call-start
  119.9 44.5 %all-gather.5.cloned.1.call-done = bf16[512,2048]{1,0:T(8,128)(2,1)} async-done(((bf16[32,2048]{1,0:T(8,128)(2,1)}), bf16[512,2048]{1,0:T(8,128)(2,1)}) %all-gather.5.cloned.1.call-update) | async-done | bytes 2097168 | tf_op jit(solution)/shard_map/all_gather | solution.py:88
  164.5 0.0 copy-start.4
  164.5 7.7 %convolution_convert_fusion.1 = bf16[512,1664]{1,0:T(8,128)(2,1)S(1)} fusion(bf16[512,2048]{1,0:T(8,128)(2,1)} %all-gather.5.cloned.1.call-done, bf16[2048,1664]{1,0:T(8,128)(2,1)} %param.22), kind=kOutput, calls=%fused_computation.6 | convolution fusion | flops 3490512896 | bytes 10616832 | tf_op jit(solution)/shard_map/dot_general | solution.py:90
  172.1 0.0 copy-done.4
  172.2 6.9 %convolution_convert_fusion.2 = bf16[512,1664]{1,0:T(8,128)(2,1)S(1)} fusion(bf16[512,2048]{1,0:T(8,128)(2,1)S(1)} %copy-done.4, bf16[2048,1664]{1,0:T(8,128)(2,1)} %param.21), kind=kOutput, calls=%fused_computation.7 | convolution fusion | flops 3490512896 | bytes 10616832 | tf_op jit(solution)/shard_map/dot_general | solution.py:89
  179.0 2.0 pad_maximum_fusion
  181.0 0.0 all-reduce.2.cloned.1.call-update
  181.1 0.0 reduce-scatter.5.cloned.1.call-start
  181.1 0.2 dynamic_update_slice.3
  181.4 65.1 %psum.14 = f32[512]{0:T(512)S(1)} all-reduce(f32[512]{0:T(512)S(1)} %dynamic_update_slice.3), channel_id=1, replica_groups=mesh['attn'=8,'ffn'=16] {'attn','ffn'}, use_global_device_ids=true, to_apply=%region_4.5 | all-reduce | flops 512 | bytes 4096 | tf_op jit(solution)/shard_map/psum | solution.py:84
  246.5 4.4 %all-reduce.2.cloned.1.call-done = bf16[512,3328]{1,0:T(8,128)(2,1)} async-done(((bf16[512,3328]{1,0:T(8,128)(2,1)}), bf16[512,3328]{1,0:T(8,128)(2,1)}) %all-reduce.2.cloned.1.call-update) | async-done | bytes 3407888 | tf_op jit(solution)/shard_map/psum | solution.py:92
  250.9 2.4 convert_element_type.56
  253.4 0.0 copy-start.2
  253.4 8.7 %convolution_convert_fusion = bf16[512,2048]{1,0:T(8,128)(2,1)} fusion(bf16[1664,2048]{1,0:T(8,128)(2,1)} %param.23, f32[512,3328]{1,0:T(8,128)S(1)} %convert_element_type.56, f32[512]{0:T(512)S(1)} %add_rsqrt_fusion), kind=kOutput, calls=%fused_computation.5 | convolution fusion | flops 3497525248 | bytes 15730688 | tf_op jit(solution)/shard_map/dot_general | solution.py:98
  262.1 0.0 reduce-scatter.5.cloned.1.call-update
  262.1 74.3 %reduce-scatter.5.cloned.1.call-done = bf16[32,2048]{1,0:T(8,128)(2,1)} async-done(((bf16[512,2048]{1,0:T(8,128)(2,1)}), bf16[32,2048]{1,0:T(8,128)(2,1)}) %reduce-scatter.5.cloned.1.call-update) | async-done | bytes 131088 | tf_op jit(solution)/shard_map/reduce_scatter | solution.py:97
  336.4 0.0 copy-done.2
  336.4 1.6 convert_add_fusion
  (5 shorter events, 0.0 us)
Async XLA Ops:
  6.5 2.6 copy-start
  6.5 54.6 %all-gather.3.cloned.1.call-start = ((), (), s32[]{:S(2)}) async-start(), calls=%async_computation.3 | async-start | bytes 2228224 | tf_op jit(solution)/shard_map/all_gather | solution.py:67
  13.3 104.8 %reduce-scatter.3.cloned.1.call-start = ((), (), s32[]{:S(2)}) async-start(), calls=%async_computation.4 | async-start | bytes 1179648 | tf_op jit(solution)/shard_map/reduce_scatter | solution.py:74
  66.3 22.1 %copy-start.3 = (bf16[2048]{0:T(1024)(128)(2,1)S(1)}, bf16[2048]{0:T(1024)(128)(2,1)}, u32[]{:S(2)}) copy-start(bf16[2048]{0:T(1024)(128)(2,1)} %param.20) | copy-start | bytes 12292
  66.3 51.8 %copy-start.1 = (f32[32,2048]{1,0:T(8,128)S(1)}, f32[32,2048]{1,0:T(8,128)}, u32[]{:S(2)}) copy-start(f32[32,2048]{1,0:T(8,128)} %param.18) | copy-start | bytes 786436
  88.4 76.1 %all-gather.5.cloned.1.call-start = ((), (), s32[]{:S(2)}) async-start(), calls=%async_computation.5 | async-start | bytes 2228224 | tf_op jit(solution)/shard_map/all_gather | solution.py:88
  119.9 131.1 %all-reduce.2.cloned.1.call-start = ((), (), s32[]{:S(2)}) async-start(), calls=%async_computation.6 | async-start | bytes 6815744 | tf_op jit(solution)/shard_map/psum | solution.py:92
  164.5 7.7 %copy-start.4 = (bf16[512,2048]{1,0:T(8,128)(2,1)S(1)}, bf16[512,2048]{1,0:T(8,128)(2,1)}, u32[]{:S(2)}) copy-start(bf16[512,2048]{1,0:T(8,128)(2,1)} %all-gather.5.cloned.1.call-done) | copy-start | bytes 6291460
  181.1 155.4 %reduce-scatter.5.cloned.1.call-start = ((), (), s32[]{:S(2)}) async-start(), calls=%async_computation.7 | async-start | bytes 2228224 | tf_op jit(solution)/shard_map/reduce_scatter | solution.py:97
  253.4 83.0 %copy-start.2 = (bf16[32,2048]{1,0:T(8,128)(2,1)S(1)}, bf16[32,2048]{1,0:T(8,128)(2,1)}, u32[]{:S(2)}) copy-start(bf16[32,2048]{1,0:T(8,128)(2,1)} %reduce-scatter.3.cloned.1.call-done) | copy-start | bytes 393220
Sparse Core Ops, SparseCore 0:
  13.4 47.7 all-gather.2
  88.5 29.5 reduce-scatter.2
  120.3 44.1 all-gather.4
  181.2 69.7 all-reduce.1
  262.3 74.1 reduce-scatter.4
where the time goes:
time: 345 us
  waiting for transfers between devices  201 us (58%)
  blocking collectives  86 us (25%)
  matrix products  31.7 us (9%)
  between operations  13.3 us (4%)
  other arithmetic  9.53 us (3%)
    reduce_scatter x1, waiting for transfers between devices, local(): lax.psum_scatter(jnp.dot(block_rows, down_weight, preferred_element_type=...  74.3 us
    psum x1, blocking collectives, local(): squares = lax.psum(placed, ('attn', 'ffn'))  65.1 us
    all_gather x1, waiting for transfers between devices, local(): lax.all_gather(attended_output, 'ffn', axis=0, tiled=True)  47.8 us
    all_gather x1, waiting for transfers between devices, local(): block_rows = lax.all_gather(scaled, 'ffn', axis=0, tiled=True)  44.5 us
    reduce_scatter x1, waiting for transfers between devices, local(): lax.psum_scatter(regrouped.astype(jnp.bfloat16), 'attn', scatter_dimensio...  29.7 us
    all_to_all x1, blocking collectives, local(): lax.all_to_all(projected.astype(jnp.bfloat16), 'ffn', split_axis=0, conca...  20.9 us
    dot_general x1, matrix products, local(): jnp.dot(block_rows, down_weight, preferred_element_type=jnp.float32)  8.7 us
    dot_general x1, matrix products, local(): up_part = jnp.dot(block_rows, up_weight, preferred_element_type=jnp.float32)  7.66 us
  transfers between devices with their start and end apart: 5, of which 5 were waited for; matrix products, arithmetic and copies ran while one was open for 0% of the time, Pallas kernels for 0%

commit v1 on v0

v1 whole, which is shorter than its diff:
```python
import functools

import jax
import jax.numpy as jnp
from jax import lax
from jax.experimental import pallas as pl
from jax.experimental.pallas import tpu as pltpu
from jax.sharding import PartitionSpec as P

D = 16384
QUERY_HEADS = 128
KEY_VALUE_HEADS = 8
HEAD_SIZE = 128
AXES = ("attn", "ffn")
BF16 = jnp.bfloat16
F32 = jnp.float32


def place_of(device):
    attn, ffn = divmod(device, 16)
    return ffn // 4, attn // 2, ffn % 4, attn % 2


def index_of(x, y, z, core):
    return ((y % 4) * 2 + core) * 16 + (x % 4) * 4 + z % 4


def send(value, target):
    pairs = [(device, index_of(*target(*place_of(device)))) for device in range(128)]
    return lax.ppermute(value, AXES, pairs)


def to_other_core(value):
    return send(value, lambda x, y, z, core: (x, y, z, 1 - core))


def along_y(value, step):
    return send(value, lambda x, y, z, core: (x, y + step, z, core))


def along_first(value, step):
    return send(
        value,
        lambda x, y, z, core: (x + step, y, z, core) if core == 0 else (x, y, z + step, core),
    )


def along_second(value, step):
    return send(
        value,
        lambda x, y, z, core: (x, y, z + step, core) if core == 0 else (x + step, y, z, core),
    )


def my_place():
    attn, ffn = lax.axis_index("attn"), lax.axis_index("ffn")
    return ffn // 4, attn // 2, ffn % 4, attn % 2


def gather_rows(block):
    near = [block] + [along_first(block, i) for i in (1, 3, 2)]
    chunk = jnp.concatenate([near[0], near[1], near[3], near[2]], axis=0)
    far = [chunk] + [along_second(chunk, j) for j in (1, 3, 2)]
    return [far[0], far[1], far[3], far[2]]


def offsets(core, j, i):
    return jnp.where(core == 0, i, j), jnp.where(core == 0, j, i)


def place_in_projected(x, y, z, core, j, i):
    x_off, z_off = offsets(core, j, i)
    owner_x, owner_z = (x - x_off) & 3, (z - z_off) & 3
    return ((owner_z >> 1) ^ core) * 8 + ((owner_x - y) & 3) * 2 + ((owner_z ^ z) & 1)


def place_in_terms(x, y, z, core, j, i):
    x_off, z_off = offsets(core, j, i)
    return ((z_off >> 1) ^ core) * 8 + ((x_off - y) & 3) * 2 + (z_off & 1)


def arrange_kernel(place, rows, width, *refs):
    chunks, out, rest = refs[:4], refs[4], refs[5:]
    x, y, z, core = my_place()
    for j in range(4):
        for i in range(4):
            start = pl.multiple_of(place(x, y, z, core, j, i) * rows, rows)
            block = chunks[j].at[pl.ds(i * rows, rows), :]
            out[pl.ds(start, rows), :] = block[:, :width]
            if rest:
                rest[0][pl.ds(start, rows), :] = block[:, width:]


def arrange(chunks, place, width):
    rows = chunks[0].shape[0] // 4
    extra = chunks[0].shape[1] - width
    shapes = [jax.ShapeDtypeStruct((16 * rows, width), chunks[0].dtype)]
    if extra:
        shapes.append(jax.ShapeDtypeStruct((16 * rows, extra), chunks[0].dtype))
    outs = pl.pallas_call(
        functools.partial(arrange_kernel, place, rows, width),
        out_shape=shapes,
        compiler_params=pltpu.CompilerParams(vmem_limit_bytes=12 << 20),
        cost_estimate=pl.CostEstimate(
            flops=0, bytes_accessed=64 * rows * (width + extra), transcendentals=0
        ),
    )(*chunks)
    return outs if extra else outs[0]


def hidden_order_kernel(rows, mine, theirs, *refs):
    parts, out = refs[:8], refs[8]
    x, y, z, core = my_place()
    for half in range(2):
        owner = core if half == 0 else 1 - core
        for d in range(4):
            for s in range(2):
                x_off, z_off = (y - d) & 3, owner * 2 + s
                spot = jnp.where(core == 0, z_off * 4 + x_off, x_off * 4 + z_off)
                start = pl.multiple_of(spot * rows, rows)
                out[pl.ds(start, rows), :] = parts[half * 4 + d][s * rows : (s + 1) * rows, :]


def order_hidden(mine, theirs):
    rows, width = mine[0].shape[0] // 2, mine[0].shape[1]
    return pl.pallas_call(
        lambda *refs: hidden_order_kernel(rows, None, None, *refs),
        out_shape=jax.ShapeDtypeStruct((16 * rows, width), mine[0].dtype),
        compiler_params=pltpu.CompilerParams(vmem_limit_bytes=12 << 20),
        cost_estimate=pl.CostEstimate(flops=0, bytes_accessed=64 * rows * width, transcendentals=0),
    )(*mine, *theirs)


def attend(queries, key_cache, cached_value_rows, new_key, token_value, lengths):
    count_of_rows = queries.shape[0]
    key_value_heads = new_key.shape[1] // HEAD_SIZE
    cache_len = key_cache.shape[1]
    score_scale = HEAD_SIZE ** (-0.5)
    grouped_query = queries.reshape(
        count_of_rows, key_value_heads, QUERY_HEADS // KEY_VALUE_HEADS, HEAD_SIZE
    )
    cache_keys = key_cache.reshape(count_of_rows, cache_len, key_value_heads, HEAD_SIZE)
    cache_values = cached_value_rows.reshape(count_of_rows, cache_len, key_value_heads, HEAD_SIZE)
    own_keys = new_key.reshape(count_of_rows, key_value_heads, HEAD_SIZE)
    own_values = token_value.reshape(count_of_rows, key_value_heads, 1, HEAD_SIZE).astype(F32)
    scores = (
        jnp.einsum("rkgd,rlkd->rkgl", grouped_query, cache_keys, preferred_element_type=F32)
        * score_scale
    )
    own_score = (
        jnp.einsum("rkgd,rkd->rkg", grouped_query, own_keys, preferred_element_type=F32)
        * score_scale
    )
    visible = jnp.arange(cache_len, dtype=jnp.int32)[None, :] < lengths[:, None]
    scores = jnp.where(visible[:, None, None, :], scores, -jnp.inf)
    peak_score = jnp.maximum(jnp.max(scores, axis=-1), own_score)
    weights = jnp.exp(scores - peak_score[..., None])
    own_weight = jnp.exp(own_score - peak_score)
    denom_sum = jnp.sum(weights, axis=-1) + own_weight
    weights = (weights / denom_sum[..., None]).astype(BF16)
    own_weight = (own_weight / denom_sum).astype(BF16)
    attended_output = jnp.einsum(
        "rkgl,rlkd->rkgd", weights, cache_values, preferred_element_type=F32
    )
    attended_output = attended_output + own_weight.astype(F32)[..., None] * own_values
    return attended_output.astype(BF16).reshape(
        count_of_rows, key_value_heads * (QUERY_HEADS // KEY_VALUE_HEADS) * HEAD_SIZE
    )


def dot(left, right):
    return jnp.dot(left, right, preferred_element_type=F32).astype(BF16)


def add(*terms):
    total = terms[0].astype(F32)
    for term in terms[1:]:
        total = total + term.astype(F32)
    return total


def in_three(value):
    high = value.astype(BF16)
    rest = value - high.astype(F32)
    middle = rest.astype(BF16)
    low = (rest - middle.astype(F32)).astype(BF16)
    column = lax.broadcasted_iota(jnp.int32, (value.shape[0], 128), 1)
    parts = jnp.where(
        column == 0, high[:, None], jnp.where(column == 1, middle[:, None], low[:, None])
    )
    return jnp.where(column < 3, parts, jnp.zeros_like(parts))


def local(
    queries,
    key_cache,
    cached_value_rows,
    new_key,
    token_value,
    lengths,
    residual,
    out_weight,
    norm_gain,
    gate_weight,
    up_weight,
    down_weight,
):
    rows, width = residual.shape
    x, y, z, core = my_place()
    with jax.named_scope("attention"):
        attended = attend(queries, key_cache, cached_value_rows, new_key, token_value, lengths)
    with jax.named_scope("gather_attended"):
        chunks = gather_rows(attended)
    with jax.named_scope("projection"):
        placed = arrange(chunks, place_in_projected, width)
        half = placed.shape[0] // 2
        away = dot(placed[half:], out_weight)
        away = to_other_core(away)
        own = dot(placed[:half], out_weight)
    with jax.named_scope("sum_projected"):
        part = half // 4
        pieces = [
            add(own[d * part : (d + 1) * part], away[d * part : (d + 1) * part]) for d in range(4)
        ]
        moved = [along_y(pieces[d].astype(BF16), d) for d in (1, 3, 2)]
        summed = add(pieces[0], *moved).astype(BF16)
        blocks = [
            send(
                summed[s * rows : (s + 1) * rows],
                lambda x, y, z, core, s=s: (y, x, core * 2 + (s ^ (z & 1)), z >> 1),
            )
            for s in range(2)
        ]
    with jax.named_scope("norm"):
        odd = (z & 1) == 1
        projected = jnp.concatenate(
            [jnp.where(odd, blocks[1], blocks[0]), jnp.where(odd, blocks[0], blocks[1])], axis=1
        )
        middle = residual + projected.astype(F32)
        squares = jnp.sum(middle * middle, axis=1)
        scaled = (middle * norm_gain.astype(F32)).astype(BF16)
        message = jnp.concatenate([scaled, in_three(squares)], axis=1)
    with jax.named_scope("gather_scaled"):
        chunks = gather_rows(message)
    with jax.named_scope("gate_up"):
        placed, square_parts = arrange(chunks, place_in_terms, width)
        square_away = to_other_core(square_parts[half:])
        gate_away = to_other_core(dot(placed[half:], gate_weight))
        up_away = to_other_core(dot(placed[half:], up_weight))
        gate_own = dot(placed[:half], gate_weight)
        up_own = dot(placed[:half], up_weight)
    with jax.named_scope("sum_terms"):

        def piece(d):
            cut = slice(d * part, (d + 1) * part)
            total = add(square_parts[cut], square_away[cut])
            return (
                add(gate_own[cut], gate_away[cut]),
                add(up_own[cut], up_away[cut]),
                jnp.sum(total, axis=1),
            )

        def packed(d):
            gate, up, square = piece(d)
            return jnp.concatenate([gate.astype(BF16), up.astype(BF16), in_three(square)], axis=1)

        moved = [along_y(packed(d), d) for d in (1, 3, 2)]
        gate, up, square = piece(0)
        cols = gate.shape[1]
        gate = add(gate, *[m[:, :cols] for m in moved])
        up = add(up, *[m[:, cols : 2 * cols] for m in moved])
        square = square + jnp.sum(add(*[m[:, 2 * cols :] for m in moved]), axis=1)
    with jax.named_scope("hidden"):
        inv_rms = lax.rsqrt(square / D + 1e-05)[:, None]
        hidden = (jax.nn.silu(inv_rms * gate) * (inv_rms * up)).astype(BF16)
    with jax.named_scope("gather_hidden"):
        got = [along_y(hidden, d) for d in (1, 3, 2)]
        mine = [hidden, got[0], got[2], got[1]]
        theirs = [to_other_core(m) for m in mine]
        hidden_all = order_hidden(mine, theirs)
    with jax.named_scope("down"):
        chunk = 4 * rows
        down = dot(hidden_all, down_weight)
        away = [along_second(down[j * chunk : (j + 1) * chunk], -j) for j in (1, 3, 2)]
    with jax.named_scope("sum_down"):

        def block(i):
            cut = slice(i * rows, (i + 1) * rows)
            return add(down[cut], *[a[cut] for a in away])

        last = [along_first(block(i).astype(BF16), -i) for i in (1, 3, 2)]
        return middle + add(block(0), *last)


def solution(mesh):
    placed = (
        P("ffn", "attn"),
        P("ffn", None, "attn"),
        P("ffn", None, "attn"),
        P("ffn", "attn"),
        P("ffn", "attn"),
        P("ffn"),
        P("ffn", "attn"),
        P("attn", "ffn"),
        P("attn"),
        P("attn", "ffn"),
        P("attn", "ffn"),
        P("ffn", "attn"),
    )
    return jax.shard_map(
        local, mesh=mesh, in_specs=placed, out_specs=P("ffn", "attn"), check_vma=False
    )
```

time: 345 us -> 182 us (0.53)
  waiting for transfers between devices: 201 us -> 110 us
  blocking collectives: 86 us -> 0 us
  starting transfers between devices: 0.17 us -> 44.2 us
  between operations: 13.3 us -> 0.51 us
  matrix products: 31.7 us -> 20.1 us
  other arithmetic: 9.53 us -> 4.72 us
    ppermute x0 -> x37, waiting for transfers between devices: none -> 110 us  [send(): return lax.ppermute(value, AXES, pairs)]
    reduce_scatter x2 -> x0, waiting for transfers between devices: 104 us -> none  [the longest x1 74.3 us: local(): lax.psum_scatter(jnp.dot(block_rows, down_weight, preferred_element_type=...]
    all_gather x2 -> x0, waiting for transfers between devices: 92.4 us -> none  [the longest x1 47.8 us: local(): lax.all_gather(attended_output, 'ffn', axis=0, tiled=True)]
    psum x1 -> x0, blocking collectives: 65.1 us -> none  [local(): squares = lax.psum(placed, ('attn', 'ffn'))]
    ppermute x0 -> x37, starting transfers between devices: none -> 44.2 us  [send(): return lax.ppermute(value, AXES, pairs)]
    all_to_all x1 -> x0, blocking collectives: 20.9 us -> none  [local(): lax.all_to_all(projected.astype(jnp.bfloat16), 'ffn', split_axis=0, conca...]
    dot_general x4 -> x7, matrix products: 28.4 us -> 18 us  [dot(): return jnp.dot(left, right, preferred_element_type=F32).astype(BF16)]
    psum x1 -> x0, waiting for transfers between devices: 4.45 us -> none  [local(): totals = lax.psum(products.astype(jnp.bfloat16), 'attn').astype(jnp.float32)]
  transfers between devices with their start and end apart: 5 -> 37, of which waited for: 5 -> 27; matrix products, arithmetic and copies ran while one was open for 0% -> 3% of each run, Pallas kernels for 0% -> 0%
where the time goes in v1:
time: 182 us; the launch traced here: 181 us
  waiting for transfers between devices  110 us (60%)
  starting transfers between devices  44.2 us (24%)
  matrix products  20.1 us (11%)
  other arithmetic  4.72 us (3%)
    ppermute x37, waiting for transfers between devices, send(): return lax.ppermute(value, AXES, pairs)  110 us
    ppermute x37, starting transfers between devices, send(): return lax.ppermute(value, AXES, pairs)  44.2 us
    dot_general x7, matrix products, dot(): return jnp.dot(left, right, preferred_element_type=F32).astype(BF16)  18 us
  transfers between devices with their start and end apart: 37, of which 27 were waited for; matrix products, arithmetic and copies ran while one was open for 3% of the time, Pallas kernels for 0%

profile of v1, /device:TPU:0, one launch (start us, length us, event | category | flops | bytes accessed | tf_op | source)
XLA Modules:
  0.0 181.4 jit_solution(13715679961057146673)
XLA Ops:
  1.6 0.9 copy.15
  4.9 2.9 %collective-permute-start.2 = (bf16[32,2048]{1,0:T(8,128)(2,1)S(1)}, bf16[32,2048]{1,0:T(8,128)(2,1)S(1)}, u32[]{:S(2)}, u32[]{:S(2)}) collective-permute-start(bf16[32,2048]{1,0:T(8,128)(2,1)S(1)} %bitcast.28), channel_id=1, source_target_pairs={{0,12},{1,13},{2,14},{3,15},{4,0},{5,1},{6,2},{7,3},{8,4},{9,5},{1... | collective-permute-start | bytes 393224 | tf_op jit(solution)/shard_map/gather_attended/ppermute | solution.py:30
  9.6 6.2 %collective-permute-done = bf16[32,2048]{1,0:T(8,128)(2,1)S(1)} collective-permute-done((bf16[32,2048]{1,0:T(8,128)(2,1)S(1)}, bf16[32,2048]{1,0:T(8,128)(2,1)S(1)}, u32[]{:S(2)}, u32[]{:S(2)}) %collective-permute-start) | collective-permute-done | bytes 131104 | tf_op jit(solution)/shard_map/gather_attended/ppermute | solution.py:30
  15.8 4.1 %collective-permute-start.5 = (bf16[128,2048]{1,0:T(8,128)(2,1)S(1)}, bf16[128,2048]{1,0:T(8,128)(2,1)S(1)}, u32[]{:S(2)}, u32[]{:S(2)}) collective-permute-start(bf16[128,2048]{1,0:T(8,128)(2,1)S(1)} %constant_dynamic-update-slice_fusion.refs_0_), channel_id=1, source_target_pairs={{0,3},{1,0},{2,1},{3,2},{4,7},{5,4},{6,5},{7,6},{8,11},{9,8},{10,9... | collective-permute-start | bytes 1572872 | tf_op jit(solution)/shard_map/gather_attended/ppermute | solution.py:30
  19.9 1.3 collective-permute-start.3
  21.2 11.1 %collective-permute-done.5.refs_3_ = bf16[128,2048]{1,0:T(8,128)(2,1)S(1)} collective-permute-done((bf16[128,2048]{1,0:T(8,128)(2,1)S(1)}, bf16[128,2048]{1,0:T(8,128)(2,1)S(1)}, u32[]{:S(2)}, u32[]{:S(2)}) %collective-permute-start.5) | collective-permute-done | bytes 524320 | tf_op jit(solution)/shard_map/gather_attended/ppermute | solution.py:30
  32.2 3.7 %collective-permute-done.3.refs_1_ = bf16[128,2048]{1,0:T(8,128)(2,1)S(1)} collective-permute-done((bf16[128,2048]{1,0:T(8,128)(2,1)S(1)}, bf16[128,2048]{1,0:T(8,128)(2,1)S(1)}, u32[]{:S(2)}, u32[]{:S(2)}) %collective-permute-start.3) | collective-permute-done | bytes 524320 | tf_op jit(solution)/shard_map/gather_attended/ppermute | solution.py:30
  36.1 1.3 convolution_convert_fusion.5
  37.5 1.3 convolution_convert_fusion.6
  39.5 1.6 collective-permute-start.7
  41.2 2.9 %collective-permute-start.9 = (bf16[64,1024]{1,0:T(8,128)(2,1)S(1)}, bf16[64,1024]{1,0:T(8,128)(2,1)S(1)}, u32[]{:S(2)}, u32[]{:S(2)}) collective-permute-start(bf16[64,1024]{1,0:T(8,128)(2,1)S(1)} %get-tuple-element.26), channel_id=1, source_target_pairs={{0,64},{1,65},{2,66},{3,67},{4,68},{5,69},{6,70},{7,71},{8,72},{9,... | collective-permute-start | bytes 393224 | tf_op jit(solution)/shard_map/sum_projected/ppermute | solution.py:30
  44.1 1.3 collective-permute-start.8
  45.4 1.0 collective-permute-done.7
  46.4 4.0 %collective-permute-done.9 = bf16[64,1024]{1,0:T(8,128)(2,1)S(1)} collective-permute-done((bf16[64,1024]{1,0:T(8,128)(2,1)S(1)}, bf16[64,1024]{1,0:T(8,128)(2,1)S(1)}, u32[]{:S(2)}, u32[]{:S(2)}) %collective-permute-start.9) | collective-permute-done | bytes 131104 | tf_op jit(solution)/shard_map/sum_projected/ppermute | solution.py:30
  51.3 3.6 %collective-permute-done.10 = bf16[32,1024]{1,0:T(8,128)(2,1)S(1)} collective-permute-done((bf16[32,1024]{1,0:T(8,128)(2,1)S(1)}, bf16[32,1024]{1,0:T(8,128)(2,1)S(1)}, u32[]{:S(2)}, u32[]{:S(2)}) %collective-permute-start.10) | collective-permute-done | bytes 65568 | tf_op jit(solution)/shard_map/sum_projected/ppermute | solution.py:30
  55.2 9.7 %collective-permute-start.14 = (bf16[32,2176]{1,0:T(8,128)(2,1)S(1)}, bf16[32,2176]{1,0:T(8,128)(2,1)S(1)}, u32[]{:S(2)}, u32[]{:S(2)}) collective-permute-start(bf16[32,2176]{1,0:T(8,128)(2,1)S(1)} %pad_maximum_fusion.4), channel_id=1, source_target_pairs={{0,12},{1,13},{2,14},{3,15},{4,0},{5,1},{6,2},{7,3},{8,4},{9,5},{1... | collective-permute-start | bytes 417800 | tf_op jit(solution)/shard_map/gather_scaled/ppermute | solution.py:30
  65.2 1.3 collective-permute-start.12
  66.5 2.5 %collective-permute-done.14 = bf16[32,2176]{1,0:T(8,128)(2,1)S(1)} collective-permute-done((bf16[32,2176]{1,0:T(8,128)(2,1)S(1)}, bf16[32,2176]{1,0:T(8,128)(2,1)S(1)}, u32[]{:S(2)}, u32[]{:S(2)}) %collective-permute-start.14) | collective-permute-done | bytes 139296 | tf_op jit(solution)/shard_map/gather_scaled/ppermute | solution.py:30
  69.0 2.6 %collective-permute-done.13 = bf16[32,2176]{1,0:T(8,128)(2,1)S(1)} collective-permute-done((bf16[32,2176]{1,0:T(8,128)(2,1)S(1)}, bf16[32,2176]{1,0:T(8,128)(2,1)S(1)}, u32[]{:S(2)}, u32[]{:S(2)}) %collective-permute-start.13) | collective-permute-done | bytes 139296 | tf_op jit(solution)/shard_map/gather_scaled/ppermute | solution.py:30
  71.6 1.4 collective-permute-done.12
  73.0 5.1 %collective-permute-start.17 = (bf16[128,2176]{1,0:T(8,128)(2,1)S(1)}, bf16[128,2176]{1,0:T(8,128)(2,1)S(1)}, u32[]{:S(2)}, u32[]{:S(2)}) collective-permute-start(bf16[128,2176]{1,0:T(8,128)(2,1)S(1)} %pad_maximum_fusion.refs_0_), channel_id=1, source_target_pairs={{0,3},{1,0},{2,1},{3,2},{4,7},{5,4},{6,5},{7,6},{8,11},{9,8},{10,9... | collective-permute-start | bytes 1671176 | tf_op jit(solution)/shard_map/gather_scaled/ppermute | solution.py:30
  79.0 12.1 %collective-permute-done.17.refs_3_ = bf16[128,2176]{1,0:T(8,128)(2,1)S(1)} collective-permute-done((bf16[128,2176]{1,0:T(8,128)(2,1)S(1)}, bf16[128,2176]{1,0:T(8,128)(2,1)S(1)}, u32[]{:S(2)}, u32[]{:S(2)}) %collective-permute-start.17) | collective-permute-done | bytes 557088 | tf_op jit(solution)/shard_map/gather_scaled/ppermute | solution.py:30
  91.1 3.9 %collective-permute-done.15.refs_1_ = bf16[128,2176]{1,0:T(8,128)(2,1)S(1)} collective-permute-done((bf16[128,2176]{1,0:T(8,128)(2,1)S(1)}, bf16[128,2176]{1,0:T(8,128)(2,1)S(1)}, u32[]{:S(2)}, u32[]{:S(2)}) %collective-permute-start.15) | collective-permute-done | bytes 557088 | tf_op jit(solution)/shard_map/gather_scaled/ppermute | solution.py:30
  95.3 5.1 %convolution_convert_fusion.2 = bf16[256,1664]{1,0:T(8,128)(2,1)S(1)} fusion(bf16[2048,1664]{1,0:T(8,128)(2,1)} %param.22, bf16[512,2048]{1,0:T(8,128)(2,1)S(1)} %get-tuple-element.8), kind=kOutput, calls=%fused_computation.2 | convolution fusion | flops 1745256448 | bytes 8716288 | tf_op jit(solution)/shard_map/gate_up/dot_general | solution.py:172
  100.5 2.1 %convolution_convert_fusion.1 = bf16[256,1664]{1,0:T(8,128)(2,1)S(1)} fusion(bf16[2048,1664]{1,0:T(8,128)(2,1)S(1)} %bitcast.34, bf16[512,2048]{1,0:T(8,128)(2,1)S(1)} %get-tuple-element.8), kind=kOutput, calls=%fused_computation.1 | convolution fusion | flops 1745256448 | bytes 8716288 | tf_op jit(solution)/shard_map/gate_up/dot_general | solution.py:172
  102.7 2.1 %convolution_convert_fusion.4 = bf16[256,1664]{1,0:T(8,128)(2,1)S(1)} fusion(bf16[2048,1664]{1,0:T(8,128)(2,1)S(1)} %bitcast.36, bf16[512,2048]{1,0:T(8,128)(2,1)S(1)} %get-tuple-element.8), kind=kOutput, calls=%fused_computation.4 | convolution fusion | flops 1745256448 | bytes 8716288 | tf_op jit(solution)/shard_map/gate_up/dot_general | solution.py:172
  104.8 2.1 %convolution_convert_fusion.3 = bf16[256,1664]{1,0:T(8,128)(2,1)S(1)} fusion(bf16[2048,1664]{1,0:T(8,128)(2,1)S(1)} %bitcast.36, bf16[512,2048]{1,0:T(8,128)(2,1)S(1)} %get-tuple-element.8), kind=kOutput, calls=%fused_computation.3 | convolution fusion | flops 1745256448 | bytes 8716288 | tf_op jit(solution)/shard_map/gate_up/dot_general | solution.py:172
  107.8 1.6 collective-permute-done.19
  109.5 1.1 collective-permute-done.20
  110.9 1.4 collective-permute-start.23
  113.1 10.7 %collective-permute-done.22 = bf16[64,3456]{1,0:T(8,128)(2,1)S(1)} collective-permute-done((bf16[64,3456]{1,0:T(8,128)(2,1)S(1)}, bf16[64,3456]{1,0:T(8,128)(2,1)S(1)}, u32[]{:S(2)}, u32[]{:S(2)}) %collective-permute-start.22) | collective-permute-done | bytes 442400 | tf_op jit(solution)/shard_map/sum_terms/ppermute | solution.py:30
  123.9 1.7 collective-permute-done.23
  125.5 8.9 %collective-permute-done.21 = bf16[64,3456]{1,0:T(8,128)(2,1)S(1)} collective-permute-done((bf16[64,3456]{1,0:T(8,128)(2,1)S(1)}, bf16[64,3456]{1,0:T(8,128)(2,1)S(1)}, u32[]{:S(2)}, u32[]{:S(2)}) %collective-permute-start.21) | collective-permute-done | bytes 442400 | tf_op jit(solution)/shard_map/sum_terms/ppermute | solution.py:30
  134.9 1.1 collective-permute-start.26
  137.5 5.7 %collective-permute-done.26.refs_3_ = bf16[64,1664]{1,0:T(8,128)(2,1)S(1)} collective-permute-done((bf16[64,1664]{1,0:T(8,128)(2,1)S(1)}, bf16[64,1664]{1,0:T(8,128)(2,1)S(1)}, u32[]{:S(2)}, u32[]{:S(2)}) %collective-permute-start.26) | collective-permute-done | bytes 213024 | tf_op jit(solution)/shard_map/gather_hidden/ppermute | solution.py:30
  143.1 2.7 %collective-permute-done.25.refs_2_ = bf16[64,1664]{1,0:T(8,128)(2,1)S(1)} collective-permute-done((bf16[64,1664]{1,0:T(8,128)(2,1)S(1)}, bf16[64,1664]{1,0:T(8,128)(2,1)S(1)}, u32[]{:S(2)}, u32[]{:S(2)}) %collective-permute-start.25) | collective-permute-done | bytes 213024 | tf_op jit(solution)/shard_map/gather_hidden/ppermute | solution.py:30
  145.8 2.8 %collective-permute-done.24.refs_1_ = bf16[64,1664]{1,0:T(8,128)(2,1)S(1)} collective-permute-done((bf16[64,1664]{1,0:T(8,128)(2,1)S(1)}, bf16[64,1664]{1,0:T(8,128)(2,1)S(1)}, u32[]{:S(2)}, u32[]{:S(2)}) %collective-permute-start.24) | collective-permute-done | bytes 213024 | tf_op jit(solution)/shard_map/gather_hidden/ppermute | solution.py:30
  148.6 1.4 collective-permute-done.28.refs_5_
  150.2 4.2 %convolution_convert_fusion = bf16[512,2048]{1,0:T(8,128)(2,1)S(1)} fusion(bf16[512,1664]{1,0:T(8,128)(2,1)S(1)} %gather_hidden.1, bf16[1664,2048]{1,0:T(8,128)(2,1)S(1)} %bitcast.38), kind=kOutput, calls=%fused_computation | convolution fusion | flops 3490709504 | bytes 10616832 | tf_op jit(solution)/shard_map/down/dot_general | solution.py:172
  155.4 1.1 collective-permute-start.32
  156.6 7.2 %collective-permute-done.31 = bf16[128,2048]{1,0:T(8,128)(2,1)S(1)} collective-permute-done((bf16[128,2048]{1,0:T(8,128)(2,1)S(1)}, bf16[128,2048]{1,0:T(8,128)(2,1)S(1)}, u32[]{:S(2)}, u32[]{:S(2)}) %collective-permute-start.31) | collective-permute-done | bytes 524320 | tf_op jit(solution)/shard_map/down/ppermute | solution.py:30
  163.7 2.3 %collective-permute-done.33 = bf16[128,2048]{1,0:T(8,128)(2,1)S(1)} collective-permute-done((bf16[128,2048]{1,0:T(8,128)(2,1)S(1)}, bf16[128,2048]{1,0:T(8,128)(2,1)S(1)}, u32[]{:S(2)}, u32[]{:S(2)}) %collective-permute-start.33) | collective-permute-done | bytes 524320 | tf_op jit(solution)/shard_map/down/ppermute | solution.py:30
  166.0 5.5 %collective-permute-done.32 = bf16[128,2048]{1,0:T(8,128)(2,1)S(1)} collective-permute-done((bf16[128,2048]{1,0:T(8,128)(2,1)S(1)}, bf16[128,2048]{1,0:T(8,128)(2,1)S(1)}, u32[]{:S(2)}, u32[]{:S(2)}) %collective-permute-start.32) | collective-permute-done | bytes 524320 | tf_op jit(solution)/shard_map/down/ppermute | solution.py:30
  171.7 1.0 collective-permute-start.34
  172.7 1.5 collective-permute-start.36
  174.2 2.6 %collective-permute-done.34 = bf16[32,2048]{1,0:T(8,128)(2,1)S(1)} collective-permute-done((bf16[32,2048]{1,0:T(8,128)(2,1)S(1)}, bf16[32,2048]{1,0:T(8,128)(2,1)S(1)}, u32[]{:S(2)}, u32[]{:S(2)}) %collective-permute-start.34) | collective-permute-done | bytes 131104 | tf_op jit(solution)/shard_map/sum_down/ppermute | solution.py:30
  176.8 2.4 %collective-permute-done.36 = bf16[32,2048]{1,0:T(8,128)(2,1)S(1)} collective-permute-done((bf16[32,2048]{1,0:T(8,128)(2,1)S(1)}, bf16[32,2048]{1,0:T(8,128)(2,1)S(1)}, u32[]{:S(2)}, u32[]{:S(2)}) %collective-permute-start.36) | collective-permute-done | bytes 131104 | tf_op jit(solution)/shard_map/sum_down/ppermute | solution.py:30
  179.2 1.4 collective-permute-done.35
  (104 shorter events, 16.0 us)
Async XLA Ops:
  0.0 3.4 %copy-start = (bf16[32,128,128]{2,1,0:T(8,128)(2,1)S(1)}, bf16[32,128,128]{2,1,0:T(8,128)(2,1)}, u32[]{:S(2)}) copy-start(bf16[32,128,128]{2,1,0:T(8,128)(2,1)} %param.13) | copy-start | bytes 3145732
  0.0 4.4 %copy-start.4 = (bf16[32,128,128]{2,1,0:T(8,128)(2,1)S(1)}, bf16[32,128,128]{2,1,0:T(8,128)(2,1)}, u32[]{:S(2)}) copy-start(bf16[32,128,128]{2,1,0:T(8,128)(2,1)} %param.14) | copy-start | bytes 3145732
  4.9 10.8 %collective-permute-start.2 = (bf16[32,2048]{1,0:T(8,128)(2,1)S(1)}, bf16[32,2048]{1,0:T(8,128)(2,1)S(1)}, u32[]{:S(2)}, u32[]{:S(2)}) collective-permute-start(bf16[32,2048]{1,0:T(8,128)(2,1)S(1)} %bitcast.28), channel_id=1, source_target_pairs={{0,12},{1,13},{2,14},{3,15},{4,0},{5,1},{6,2},{7,3},{8,4},{9,5},{1... | collective-permute-start | bytes 393224 | tf_op jit(solution)/shard_map/gather_attended/ppermute | solution.py:30
  7.8 7.9 %collective-permute-start.1 = (bf16[32,2048]{1,0:T(8,128)(2,1)S(1)}, bf16[32,2048]{1,0:T(8,128)(2,1)S(1)}, u32[]{:S(2)}, u32[]{:S(2)}) collective-permute-start(bf16[32,2048]{1,0:T(8,128)(2,1)S(1)} %bitcast.29), channel_id=1, source_target_pairs={{0,8},{1,9},{2,10},{3,11},{4,12},{5,13},{6,14},{7,15},{8,0},{9,1},... | collective-permute-start | bytes 393224 | tf_op jit(solution)/shard_map/gather_attended/ppermute | solution.py:30
  8.6 7.1 %collective-permute-start = (bf16[32,2048]{1,0:T(8,128)(2,1)S(1)}, bf16[32,2048]{1,0:T(8,128)(2,1)S(1)}, u32[]{:S(2)}, u32[]{:S(2)}) collective-permute-start(bf16[32,2048]{1,0:T(8,128)(2,1)S(1)} %bitcast.30), channel_id=1, source_target_pairs={{0,4},{1,5},{2,6},{3,7},{4,8},{5,9},{6,10},{7,11},{8,12},{9,13},{1... | collective-permute-start | bytes 393224 | tf_op jit(solution)/shard_map/gather_attended/ppermute | solution.py:30
  15.8 20.3 %copy-start.3 = (bf16[2048,1024]{1,0:T(8,128)(2,1)S(1)}, bf16[2048,1024]{1,0:T(8,128)(2,1)}, u32[]{:S(2)}) copy-start(bf16[2048,1024]{1,0:T(8,128)(2,1)} %param.19) | copy-start | bytes 12582916
  15.8 16.4 %collective-permute-start.5 = (bf16[128,2048]{1,0:T(8,128)(2,1)S(1)}, bf16[128,2048]{1,0:T(8,128)(2,1)S(1)}, u32[]{:S(2)}, u32[]{:S(2)}) collective-permute-start(bf16[128,2048]{1,0:T(8,128)(2,1)S(1)} %constant_dynamic-update-slice_fusion.refs_0_), channel_id=1, source_target_pairs={{0,3},{1,0},{2,1},{3,2},{4,7},{5,4},{6,5},{7,6},{8,11},{9,8},{10,9... | collective-permute-start | bytes 1572872 | tf_op jit(solution)/shard_map/gather_attended/ppermute | solution.py:30
  19.9 12.3 %collective-permute-start.4 = (bf16[128,2048]{1,0:T(8,128)(2,1)S(1)}, bf16[128,2048]{1,0:T(8,128)(2,1)S(1)}, u32[]{:S(2)}, u32[]{:S(2)}) collective-permute-start(bf16[128,2048]{1,0:T(8,128)(2,1)S(1)} %constant_dynamic-update-slice_fusion.refs_0_), channel_id=1, source_target_pairs={{0,2},{1,3},{2,0},{3,1},{4,6},{5,7},{6,4},{7,5},{8,10},{9,11},{10,... | collective-permute-start | bytes 1572872 | tf_op jit(solution)/shard_map/gather_attended/ppermute | solution.py:30
  19.9 16.0 %collective-permute-start.3 = (bf16[128,2048]{1,0:T(8,128)(2,1)S(1)}, bf16[128,2048]{1,0:T(8,128)(2,1)S(1)}, u32[]{:S(2)}, u32[]{:S(2)}) collective-permute-start(bf16[128,2048]{1,0:T(8,128)(2,1)S(1)} %constant_dynamic-update-slice_fusion.refs_0_), channel_id=1, source_target_pairs={{0,1},{1,2},{2,3},{3,0},{4,5},{5,6},{6,7},{7,4},{8,9},{9,10},{10,1... | collective-permute-start | bytes 1572872 | tf_op jit(solution)/shard_map/gather_attended/ppermute | solution.py:30
  37.4 8.0 %copy-start.2 = (bf16[2048]{0:T(1024)(128)(2,1)S(1)}, bf16[2048]{0:T(1024)(128)(2,1)}, u32[]{:S(2)}) copy-start(bf16[2048]{0:T(1024)(128)(2,1)} %param.20) | copy-start | bytes 12292
  37.4 2.0 %collective-permute-start.6 = (bf16[256,1024]{1,0:T(8,128)(2,1)S(1)}, bf16[256,1024]{1,0:T(8,128)(2,1)S(1)}, u32[]{:S(2)}, u32[]{:S(2)}) collective-permute-start(bf16[256,1024]{1,0:T(8,128)(2,1)S(1)} %convolution_convert_fusion.5), channel_id=1, source_target_pairs={{0,16},{1,17},{2,18},{3,19},{4,20},{5,21},{6,22},{7,23},{8,24},{9,... | collective-permute-start | bytes 1572872 | tf_op jit(solution)/shard_map/projection/ppermute | solution.py:30
  38.8 16.1 %copy-start.1 = (f32[32,2048]{1,0:T(8,128)S(1)}, f32[32,2048]{1,0:T(8,128)}, u32[]{:S(2)}) copy-start(f32[32,2048]{1,0:T(8,128)} %param.18) | copy-start | bytes 786436
  39.5 6.9 %collective-permute-start.7 = (bf16[64,1024]{1,0:T(8,128)(2,1)S(1)}, bf16[64,1024]{1,0:T(8,128)(2,1)S(1)}, u32[]{:S(2)}, u32[]{:S(2)}) collective-permute-start(bf16[64,1024]{1,0:T(8,128)(2,1)S(1)} %get-tuple-element.25), channel_id=1, source_target_pairs={{0,32},{1,33},{2,34},{3,35},{4,36},{5,37},{6,38},{7,39},{8,40},{9,... | collective-permute-start | bytes 393224 | tf_op jit(solution)/shard_map/sum_projected/ppermute | solution.py:30
  41.2 9.2 %collective-permute-start.9 = (bf16[64,1024]{1,0:T(8,128)(2,1)S(1)}, bf16[64,1024]{1,0:T(8,128)(2,1)S(1)}, u32[]{:S(2)}, u32[]{:S(2)}) collective-permute-start(bf16[64,1024]{1,0:T(8,128)(2,1)S(1)} %get-tuple-element.26), channel_id=1, source_target_pairs={{0,64},{1,65},{2,66},{3,67},{4,68},{5,69},{6,70},{7,71},{8,72},{9,... | collective-permute-start | bytes 393224 | tf_op jit(solution)/shard_map/sum_projected/ppermute | solution.py:30
  44.1 6.3 %collective-permute-start.8 = (bf16[64,1024]{1,0:T(8,128)(2,1)S(1)}, bf16[64,1024]{1,0:T(8,128)(2,1)S(1)}, u32[]{:S(2)}, u32[]{:S(2)}) collective-permute-start(bf16[64,1024]{1,0:T(8,128)(2,1)S(1)} %get-tuple-element.27), channel_id=1, source_target_pairs={{0,96},{1,97},{2,98},{3,99},{4,100},{5,101},{6,102},{7,103},{8,104... | collective-permute-start | bytes 393224 | tf_op jit(solution)/shard_map/sum_projected/ppermute | solution.py:30
  50.5 4.3 %collective-permute-start.10 = (bf16[32,1024]{1,0:T(8,128)(2,1)S(1)}, bf16[32,1024]{1,0:T(8,128)(2,1)S(1)}, u32[]{:S(2)}, u32[]{:S(2)}) collective-permute-start(bf16[32,1024]{1,0:T(8,128)(2,1)S(1)} %get-tuple-element.32), channel_id=1, source_target_pairs={{0,1},{1,0},{2,17},{3,16},{4,33},{5,32},{6,49},{7,48},{8,65},{9,64... | collective-permute-start | bytes 196616 | tf_op jit(solution)/shard_map/sum_projected/ppermute | solution.py:30
  50.6 4.3 %collective-permute-start.11 = (bf16[32,1024]{1,0:T(8,128)(2,1)S(1)}, bf16[32,1024]{1,0:T(8,128)(2,1)S(1)}, u32[]{:S(2)}, u32[]{:S(2)}) collective-permute-start(bf16[32,1024]{1,0:T(8,128)(2,1)S(1)} %get-tuple-element.33), channel_id=1, source_target_pairs={{0,0},{1,1},{2,16},{3,17},{4,32},{5,33},{6,48},{7,49},{8,64},{9,65... | collective-permute-start | bytes 196616 | tf_op jit(solution)/shard_map/sum_projected/ppermute | solution.py:30
  55.2 13.8 %collective-permute-start.14 = (bf16[32,2176]{1,0:T(8,128)(2,1)S(1)}, bf16[32,2176]{1,0:T(8,128)(2,1)S(1)}, u32[]{:S(2)}, u32[]{:S(2)}) collective-permute-start(bf16[32,2176]{1,0:T(8,128)(2,1)S(1)} %pad_maximum_fusion.4), channel_id=1, source_target_pairs={{0,12},{1,13},{2,14},{3,15},{4,0},{5,1},{6,2},{7,3},{8,4},{9,5},{1... | collective-permute-start | bytes 417800 | tf_op jit(solution)/shard_map/gather_scaled/ppermute | solution.py:30
  64.9 6.7 %collective-permute-start.13 = (bf16[32,2176]{1,0:T(8,128)(2,1)S(1)}, bf16[32,2176]{1,0:T(8,128)(2,1)S(1)}, u32[]{:S(2)}, u32[]{:S(2)}) collective-permute-start(bf16[32,2176]{1,0:T(8,128)(2,1)S(1)} %pad_maximum_fusion.4), channel_id=1, source_target_pairs={{0,8},{1,9},{2,10},{3,11},{4,12},{5,13},{6,14},{7,15},{8,0},{9,1},... | collective-permute-start | bytes 417800 | tf_op jit(solution)/shard_map/gather_scaled/ppermute | solution.py:30
  65.2 7.8 %collective-permute-start.12 = (bf16[32,2176]{1,0:T(8,128)(2,1)S(1)}, bf16[32,2176]{1,0:T(8,128)(2,1)S(1)}, u32[]{:S(2)}, u32[]{:S(2)}) collective-permute-start(bf16[32,2176]{1,0:T(8,128)(2,1)S(1)} %pad_maximum_fusion.4), channel_id=1, source_target_pairs={{0,4},{1,5},{2,6},{3,7},{4,8},{5,9},{6,10},{7,11},{8,12},{9,13},{1... | collective-permute-start | bytes 417800 | tf_op jit(solution)/shard_map/gather_scaled/ppermute | solution.py:30
  73.0 18.1 %collective-permute-start.17 = (bf16[128,2176]{1,0:T(8,128)(2,1)S(1)}, bf16[128,2176]{1,0:T(8,128)(2,1)S(1)}, u32[]{:S(2)}, u32[]{:S(2)}) collective-permute-start(bf16[128,2176]{1,0:T(8,128)(2,1)S(1)} %pad_maximum_fusion.refs_0_), channel_id=1, source_target_pairs={{0,3},{1,0},{2,1},{3,2},{4,7},{5,4},{6,5},{7,6},{8,11},{9,8},{10,9... | collective-permute-start | bytes 1671176 | tf_op jit(solution)/shard_map/gather_scaled/ppermute | solution.py:30
  78.1 13.0 %collective-permute-start.16 = (bf16[128,2176]{1,0:T(8,128)(2,1)S(1)}, bf16[128,2176]{1,0:T(8,128)(2,1)S(1)}, u32[]{:S(2)}, u32[]{:S(2)}) collective-permute-start(bf16[128,2176]{1,0:T(8,128)(2,1)S(1)} %pad_maximum_fusion.refs_0_), channel_id=1, source_target_pairs={{0,2},{1,3},{2,0},{3,1},{4,6},{5,7},{6,4},{7,5},{8,10},{9,11},{10,... | collective-permute-start | bytes 1671176 | tf_op jit(solution)/shard_map/gather_scaled/ppermute | solution.py:30
  78.3 16.7 %collective-permute-start.15 = (bf16[128,2176]{1,0:T(8,128)(2,1)S(1)}, bf16[128,2176]{1,0:T(8,128)(2,1)S(1)}, u32[]{:S(2)}, u32[]{:S(2)}) collective-permute-start(bf16[128,2176]{1,0:T(8,128)(2,1)S(1)} %pad_maximum_fusion.refs_0_), channel_id=1, source_target_pairs={{0,1},{1,2},{2,3},{3,0},{4,5},{5,6},{6,7},{7,4},{8,9},{9,10},{10,1... | collective-permute-start | bytes 1671176 | tf_op jit(solution)/shard_map/gather_scaled/ppermute | solution.py:30
  95.1 5.4 %slice-start = ((s8[6815744]{0:T(1024)(128)(4,1)}), s8[4194304]{0:T(1024)(128)(4,1)S(1)}, s32[]{:S(2)}) async-start(s8[6815744]{0:T(1024)(128)(4,1)} %bitcast.33), calls=%async_computation | async-start | bytes 8388608
  95.2 5.2 %slice-start.1 = ((s8[6815744]{0:T(1024)(128)(4,1)}), s8[2621440]{0:T(1024)(128)(4,1)S(1)}, s32[]{:S(2)}) async-start(s8[6815744]{0:T(1024)(128)(4,1)} %bitcast.33), calls=%async_computation.1 | async-start | bytes 5242880
  95.3 7.4 %slice-start.2 = ((s8[6815744]{0:T(1024)(128)(4,1)}), s8[4194304]{0:T(1024)(128)(4,1)S(1)}, s32[]{:S(2)}) async-start(s8[6815744]{0:T(1024)(128)(4,1)} %bitcast.35), calls=%async_computation.2 | async-start | bytes 8388608
  100.4 2.2 %slice-start.3 = ((s8[6815744]{0:T(1024)(128)(4,1)}), s8[2621440]{0:T(1024)(128)(4,1)S(1)}, s32[]{:S(2)}) async-start(s8[6815744]{0:T(1024)(128)(4,1)} %bitcast.35), calls=%async_computation.3 | async-start | bytes 5242880
  102.5 4.9 %collective-permute-start.18 = (bf16[256,128]{1,0:T(8,128)(2,1)S(1)}, bf16[256,128]{1,0:T(8,128)(2,1)S(1)}, u32[]{:S(2)}, u32[]{:S(2)}) collective-permute-start(bf16[256,128]{1,0:T(8,128)(2,1)S(1)} %slice.216), channel_id=1, source_target_pairs={{0,16},{1,17},{2,18},{3,19},{4,20},{5,21},{6,22},{7,23},{8,24},{9,... | collective-permute-start | bytes 196616 | tf_op jit(solution)/shard_map/gate_up/ppermute | solution.py:30
  102.7 47.5 %slice-start.4 = ((s8[6815744]{0:T(1024)(128)(4,1)}), s8[4194304]{0:T(1024)(128)(4,1)S(1)}, s32[]{:S(2)}) async-start(s8[6815744]{0:T(1024)(128)(4,1)} %bitcast.37), calls=%async_computation.4 | async-start | bytes 8388608
  104.7 45.4 %slice-start.5 = ((s8[6815744]{0:T(1024)(128)(4,1)}), s8[2621440]{0:T(1024)(128)(4,1)S(1)}, s32[]{:S(2)}) async-start(s8[6815744]{0:T(1024)(128)(4,1)} %bitcast.37), calls=%async_computation.5 | async-start | bytes 5242880
  106.8 2.6 %collective-permute-start.19 = (bf16[256,1664]{1,0:T(8,128)(2,1)S(1)}, bf16[256,1664]{1,0:T(8,128)(2,1)S(1)}, u32[]{:S(2)}, u32[]{:S(2)}) collective-permute-start(bf16[256,1664]{1,0:T(8,128)(2,1)S(1)} %convolution_convert_fusion.3), channel_id=1, source_target_pairs={{0,16},{1,17},{2,18},{3,19},{4,20},{5,21},{6,22},{7,23},{8,24},{9,... | collective-permute-start | bytes 2555912 | tf_op jit(solution)/shard_map/gate_up/ppermute | solution.py:30
  107.4 3.2 %collective-permute-start.20 = (bf16[256,1664]{1,0:T(8,128)(2,1)S(1)}, bf16[256,1664]{1,0:T(8,128)(2,1)S(1)}, u32[]{:S(2)}, u32[]{:S(2)}) collective-permute-start(bf16[256,1664]{1,0:T(8,128)(2,1)S(1)} %convolution_convert_fusion.1), channel_id=1, source_target_pairs={{0,16},{1,17},{2,18},{3,19},{4,20},{5,21},{6,22},{7,23},{8,24},{9,... | collective-permute-start | bytes 2555912 | tf_op jit(solution)/shard_map/gate_up/ppermute | solution.py:30
  110.8 13.1 %collective-permute-start.22 = (bf16[64,3456]{1,0:T(8,128)(2,1)S(1)}, bf16[64,3456]{1,0:T(8,128)(2,1)S(1)}, u32[]{:S(2)}, u32[]{:S(2)}) collective-permute-start(bf16[64,3456]{1,0:T(8,128)(2,1)S(1)} %pad_maximum_fusion.2), channel_id=1, source_target_pairs={{0,96},{1,97},{2,98},{3,99},{4,100},{5,101},{6,102},{7,103},{8,104... | collective-permute-start | bytes 1327112 | tf_op jit(solution)/shard_map/sum_terms/ppermute | solution.py:30
  110.9 14.6 %collective-permute-start.23 = (bf16[64,3456]{1,0:T(8,128)(2,1)S(1)}, bf16[64,3456]{1,0:T(8,128)(2,1)S(1)}, u32[]{:S(2)}, u32[]{:S(2)}) collective-permute-start(bf16[64,3456]{1,0:T(8,128)(2,1)S(1)} %pad_maximum_fusion.3), channel_id=1, source_target_pairs={{0,64},{1,65},{2,66},{3,67},{4,68},{5,69},{6,70},{7,71},{8,72},{9,... | collective-permute-start | bytes 1327112 | tf_op jit(solution)/shard_map/sum_terms/ppermute | solution.py:30
  112.3 22.1 %collective-permute-start.21 = (bf16[64,3456]{1,0:T(8,128)(2,1)S(1)}, bf16[64,3456]{1,0:T(8,128)(2,1)S(1)}, u32[]{:S(2)}, u32[]{:S(2)}) collective-permute-start(bf16[64,3456]{1,0:T(8,128)(2,1)S(1)} %pad_maximum_fusion.1), channel_id=1, source_target_pairs={{0,32},{1,33},{2,34},{3,35},{4,36},{5,37},{6,38},{7,39},{8,40},{9,... | collective-permute-start | bytes 1327112 | tf_op jit(solution)/shard_map/sum_terms/ppermute | solution.py:30
  134.9 8.2 %collective-permute-start.26 = (bf16[64,1664]{1,0:T(8,128)(2,1)S(1)}, bf16[64,1664]{1,0:T(8,128)(2,1)S(1)}, u32[]{:S(2)}, u32[]{:S(2)}) collective-permute-start(bf16[64,1664]{1,0:T(8,128)(2,1)S(1)} %multiply_convert_fusion.refs_0_), channel_id=1, source_target_pairs={{0,96},{1,97},{2,98},{3,99},{4,100},{5,101},{6,102},{7,103},{8,104... | collective-permute-start | bytes 638984 | tf_op jit(solution)/shard_map/gather_hidden/ppermute | solution.py:30
  136.1 9.7 %collective-permute-start.25 = (bf16[64,1664]{1,0:T(8,128)(2,1)S(1)}, bf16[64,1664]{1,0:T(8,128)(2,1)S(1)}, u32[]{:S(2)}, u32[]{:S(2)}) collective-permute-start(bf16[64,1664]{1,0:T(8,128)(2,1)S(1)} %multiply_convert_fusion.refs_0_), channel_id=1, source_target_pairs={{0,64},{1,65},{2,66},{3,67},{4,68},{5,69},{6,70},{7,71},{8,72},{9,... | collective-permute-start | bytes 638984 | tf_op jit(solution)/shard_map/gather_hidden/ppermute | solution.py:30
  136.6 11.9 %collective-permute-start.24 = (bf16[64,1664]{1,0:T(8,128)(2,1)S(1)}, bf16[64,1664]{1,0:T(8,128)(2,1)S(1)}, u32[]{:S(2)}, u32[]{:S(2)}) collective-permute-start(bf16[64,1664]{1,0:T(8,128)(2,1)S(1)} %multiply_convert_fusion.refs_0_), channel_id=1, source_target_pairs={{0,32},{1,33},{2,34},{3,35},{4,36},{5,37},{6,38},{7,39},{8,40},{9,... | collective-permute-start | bytes 638984 | tf_op jit(solution)/shard_map/gather_hidden/ppermute | solution.py:30
  137.5 11.1 %collective-permute-start.27 = (bf16[64,1664]{1,0:T(8,128)(2,1)S(1)}, bf16[64,1664]{1,0:T(8,128)(2,1)S(1)}, u32[]{:S(2)}, u32[]{:S(2)}) collective-permute-start(bf16[64,1664]{1,0:T(8,128)(2,1)S(1)} %multiply_convert_fusion.refs_0_), channel_id=1, source_target_pairs={{0,16},{1,17},{2,18},{3,19},{4,20},{5,21},{6,22},{7,23},{8,24},{9,... | collective-permute-start | bytes 638984 | tf_op jit(solution)/shard_map/gather_hidden/ppermute | solution.py:30
  143.1 5.5 %collective-permute-start.30 = (bf16[64,1664]{1,0:T(8,128)(2,1)S(1)}, bf16[64,1664]{1,0:T(8,128)(2,1)S(1)}, u32[]{:S(2)}, u32[]{:S(2)}) collective-permute-start(bf16[64,1664]{1,0:T(8,128)(2,1)S(1)} %collective-permute-done.26.refs_3_), channel_id=1, source_target_pairs={{0,16},{1,17},{2,18},{3,19},{4,20},{5,21},{6,22},{7,23},{8,24},{9,... | collective-permute-start | bytes 638984 | tf_op jit(solution)/shard_map/gather_hidden/ppermute | solution.py:30
  145.8 2.8 %collective-permute-start.29 = (bf16[64,1664]{1,0:T(8,128)(2,1)S(1)}, bf16[64,1664]{1,0:T(8,128)(2,1)S(1)}, u32[]{:S(2)}, u32[]{:S(2)}) collective-permute-start(bf16[64,1664]{1,0:T(8,128)(2,1)S(1)} %collective-permute-done.25.refs_2_), channel_id=1, source_target_pairs={{0,16},{1,17},{2,18},{3,19},{4,20},{5,21},{6,22},{7,23},{8,24},{9,... | collective-permute-start | bytes 638984 | tf_op jit(solution)/shard_map/gather_hidden/ppermute | solution.py:30
  148.6 1.5 collective-permute-start.28
  154.5 9.3 %collective-permute-start.31 = (bf16[128,2048]{1,0:T(8,128)(2,1)S(1)}, bf16[128,2048]{1,0:T(8,128)(2,1)S(1)}, u32[]{:S(2)}, u32[]{:S(2)}) collective-permute-start(bf16[128,2048]{1,0:T(8,128)(2,1)S(1)} %get-tuple-element.16), channel_id=1, source_target_pairs={{0,3},{1,0},{2,1},{3,2},{4,7},{5,4},{6,5},{7,6},{8,11},{9,8},{10,9... | collective-permute-start | bytes 1572872 | tf_op jit(solution)/shard_map/down/ppermute | solution.py:30
  155.2 10.8 %collective-permute-start.33 = (bf16[128,2048]{1,0:T(8,128)(2,1)S(1)}, bf16[128,2048]{1,0:T(8,128)(2,1)S(1)}, u32[]{:S(2)}, u32[]{:S(2)}) collective-permute-start(bf16[128,2048]{1,0:T(8,128)(2,1)S(1)} %get-tuple-element.17), channel_id=1, source_target_pairs={{0,2},{1,3},{2,0},{3,1},{4,6},{5,7},{6,4},{7,5},{8,10},{9,11},{10,... | collective-permute-start | bytes 1572872 | tf_op jit(solution)/shard_map/down/ppermute | solution.py:30
  155.4 16.1 %collective-permute-start.32 = (bf16[128,2048]{1,0:T(8,128)(2,1)S(1)}, bf16[128,2048]{1,0:T(8,128)(2,1)S(1)}, u32[]{:S(2)}, u32[]{:S(2)}) collective-permute-start(bf16[128,2048]{1,0:T(8,128)(2,1)S(1)} %get-tuple-element.18), channel_id=1, source_target_pairs={{0,1},{1,2},{2,3},{3,0},{4,5},{5,6},{6,7},{7,4},{8,9},{9,10},{10,1... | collective-permute-start | bytes 1572872 | tf_op jit(solution)/shard_map/down/ppermute | solution.py:30
  171.7 5.0 %collective-permute-start.34 = (bf16[32,2048]{1,0:T(8,128)(2,1)S(1)}, bf16[32,2048]{1,0:T(8,128)(2,1)S(1)}, u32[]{:S(2)}, u32[]{:S(2)}) collective-permute-start(bf16[32,2048]{1,0:T(8,128)(2,1)S(1)} %get-tuple-element.13), channel_id=1, source_target_pairs={{0,12},{1,13},{2,14},{3,15},{4,0},{5,1},{6,2},{7,3},{8,4},{9,5},{1... | collective-permute-start | bytes 393224 | tf_op jit(solution)/shard_map/sum_down/ppermute | solution.py:30
  172.7 6.5 %collective-permute-start.36 = (bf16[32,2048]{1,0:T(8,128)(2,1)S(1)}, bf16[32,2048]{1,0:T(8,128)(2,1)S(1)}, u32[]{:S(2)}, u32[]{:S(2)}) collective-permute-start(bf16[32,2048]{1,0:T(8,128)(2,1)S(1)} %get-tuple-element.14), channel_id=1, source_target_pairs={{0,8},{1,9},{2,10},{3,11},{4,12},{5,13},{6,14},{7,15},{8,0},{9,1},... | collective-permute-start | bytes 393224 | tf_op jit(solution)/shard_map/sum_down/ppermute | solution.py:30
  174.2 6.4 %collective-permute-start.35 = (bf16[32,2048]{1,0:T(8,128)(2,1)S(1)}, bf16[32,2048]{1,0:T(8,128)(2,1)S(1)}, u32[]{:S(2)}, u32[]{:S(2)}) collective-permute-start(bf16[32,2048]{1,0:T(8,128)(2,1)S(1)} %get-tuple-element.15), channel_id=1, source_target_pairs={{0,4},{1,5},{2,6},{3,7},{4,8},{5,9},{6,10},{7,11},{8,12},{9,13},{1... | collective-permute-start | bytes 393224 | tf_op jit(solution)/shard_map/sum_down/ppermute | solution.py:30

commit v2 on v0

v2 whole, which is shorter than its diff:
```python
import functools

import jax
import jax.numpy as jnp
from jax import lax
from jax.experimental import pallas as pl
from jax.experimental.pallas import tpu as pltpu
from jax.sharding import PartitionSpec as P

D = 16384
HEAD_SIZE = 128
ATTEND_VMEM = 62 << 20
AXES = ("attn", "ffn")
BF16 = jnp.bfloat16
F32 = jnp.float32


def place_of(device):
    attn, ffn = divmod(device, 16)
    return ffn // 4, attn // 2, ffn % 4, attn % 2


def index_of(x, y, z, core):
    return ((y % 4) * 2 + core) * 16 + (x % 4) * 4 + z % 4


def send(value, target):
    pairs = [(device, index_of(*target(*place_of(device)))) for device in range(128)]
    return lax.ppermute(value, AXES, pairs)


def to_other_core(value):
    return send(value, lambda x, y, z, core: (x, y, z, 1 - core))


def along_y(value, step):
    return send(value, lambda x, y, z, core: (x, y + step, z, core))


def across_y(value, bits):
    return send(value, lambda x, y, z, core: (x, y ^ bits, z, core))


def along_first(value, step):
    return send(
        value,
        lambda x, y, z, core: (x + step, y, z, core) if core == 0 else (x, y, z + step, core),
    )


def along_second(value, step):
    return send(
        value,
        lambda x, y, z, core: (x, y, z + step, core) if core == 0 else (x + step, y, z, core),
    )


def my_place():
    attn, ffn = lax.axis_index("attn"), lax.axis_index("ffn")
    return ffn // 4, attn // 2, ffn % 4, attn % 2


def after(value, *others):
    return lax.optimization_barrier((value, *others))[0]


def gather_rows(block):
    near = {i: along_first(block, i) for i in (1, 3, 2)}
    chunk = jnp.concatenate([block, near[1], near[2], near[3]], axis=0)
    far = {j: along_second(chunk, j) for j in (1, 3, 2)}
    return [chunk, far[1], far[2], far[3]]


def offsets_of(projected, x, y, z, core, half, low, j):
    which = (core ^ half) * 2 + low
    delta = (x - z - which) & 3 if projected else which
    i = jnp.where(core == 0, j + delta, j - delta) & 3
    x_off = jnp.where(core == 0, i, j)
    if projected:
        return i, ((x - x_off - y) & 3) * 2 + (low ^ (z & 1))
    return i, low * 4 + (-(x_off ^ y) & 3)


COPY = dict(
    compiler_params=pltpu.CompilerParams(vmem_limit_bytes=12 << 20),
    cost_estimate=pl.CostEstimate(flops=0, bytes_accessed=0, transcendentals=0),
)


def split_kernel(projected, width, *refs):
    chunks, rest, extra = refs[:4], refs[4:6], refs[6:]
    rows = chunks[0].shape[0] // 4
    place = my_place()
    for half in range(2):
        for j in range(4):
            for low in range(2):
                i, spot = offsets_of(projected, *place, half, low, j)
                block = chunks[j].at[pl.ds(pl.multiple_of(i * rows, rows), rows), :]
                if j:
                    at = ((j - 1) * 2 + low) * rows
                    rest[half][at : at + rows, :] = block[:, :width]
                if extra:
                    start = pl.multiple_of(spot * rows, rows)
                    extra[half][pl.ds(start, rows), :] = block[:, width:]


def split(chunks, projected, width):
    rows, extra = chunks[0].shape[0] // 4, chunks[0].shape[1] - width
    kind = chunks[0].dtype
    shapes = [jax.ShapeDtypeStruct((6 * rows, width), kind)] * 2
    if extra:
        shapes += [jax.ShapeDtypeStruct((8 * rows, extra), kind)] * 2
    return pl.pallas_call(
        functools.partial(split_kernel, projected, width),
        out_shape=shapes,
        **COPY,
    )(*chunks)


def place_kernel(projected, half, first, rest, out):
    rows = first.shape[0] // 4
    place = my_place()
    for j in range(4):
        for low in range(2):
            i, spot = offsets_of(projected, *place, half, low, j)
            start = pl.multiple_of(spot * rows, rows)
            at = ((j - 1) * 2 + low) * rows
            if j:
                out[pl.ds(start, rows), :] = rest[at : at + rows, :]
            else:
                out[pl.ds(start, rows), :] = first[pl.ds(pl.multiple_of(i * rows, rows), rows), :]


def in_place(first, rest, projected, half):
    rows, width = first.shape[0] // 4, first.shape[1]
    return pl.pallas_call(
        functools.partial(place_kernel, projected, half),
        out_shape=jax.ShapeDtypeStruct((8 * rows, width), first.dtype),
        **COPY,
    )(first, rest)


def products(chunks, weight, projected):
    first = dot(chunks[0], weight)
    own_rows, away_rows = split(chunks, projected, weight.shape[0])
    return shares(first, own_rows, away_rows, weight, projected)


def shares(first, own_rows, away_rows, weight, projected):
    away = in_place(first, dot(away_rows, weight), projected, 1)
    own = in_place(first, dot(after(own_rows, away), weight), projected, 0)
    return own, to_other_core(away)


def order_down_kernel(first, rest, out):
    rows = out.shape[0] // 16
    x, y, z, core = my_place()
    for d in range(4):
        source, base = (rest, (d - 1) * 4) if d else (first, 0)
        for half in range(2):
            for low in range(2):
                x_off = (y - d) & 3
                z_off = (x_off - ((core ^ half) * 2 + low)) & 3
                spot = jnp.where(core == 0, z_off * 4 + x_off, x_off * 4 + z_off)
                start = pl.multiple_of(spot * rows, rows)
                at = (base + half * 2 + low) * rows
                out[pl.ds(start, rows), :] = source[at : at + rows, :]


def order_down(first, rest):
    shape = (4 * first.shape[0], first.shape[1])
    return pl.pallas_call(
        order_down_kernel,
        out_shape=jax.ShapeDtypeStruct(shape, first.dtype),
        **COPY,
    )(first, rest)


def attend_kernel(lengths, *refs):
    sources, out, buffers, sems = refs[:5], refs[5], refs[6:11], refs[11]
    copies = [
        pltpu.make_async_copy(source, buffer, sems.at[n])
        for n, (source, buffer) in enumerate(zip(sources, buffers))
    ]
    for copy in copies:
        copy.start()
    queries, new_key, keys, token_value, values = buffers
    rows, heads = queries.shape[0], queries.shape[1] // HEAD_SIZE
    score_scale = HEAD_SIZE ** (-0.5)
    copies[0].wait()
    copies[1].wait()
    grouped = queries[...].reshape(rows, heads, HEAD_SIZE)
    own_key = new_key[...].astype(F32)[:, None, :]
    own = jnp.sum(grouped.astype(F32) * own_key, axis=2, keepdims=True) * score_scale
    copies[2].wait()
    scores = (
        lax.dot_general(
            grouped, keys[...], (((2,), (2,)), ((0,), (0,))), preferred_element_type=F32
        )
        * score_scale
    )
    position = lax.broadcasted_iota(jnp.int32, scores.shape[1:], 1)
    visible = jnp.stack([position < lengths[row] for row in range(rows)])
    scores = jnp.where(visible, scores, -jnp.inf)
    peak = jnp.maximum(jnp.max(scores, axis=2, keepdims=True), own)
    weights, own_weight = jnp.exp(scores - peak), jnp.exp(own - peak)
    total = jnp.sum(weights, axis=2, keepdims=True) + own_weight
    weights, own_weight = (weights / total).astype(BF16), (own_weight / total).astype(BF16)
    copies[3].wait()
    copies[4].wait()
    attended = lax.dot_general(
        weights, values[...], (((2,), (1,)), ((0,), (0,))), preferred_element_type=F32
    )
    attended = attended + own_weight.astype(F32) * token_value[...].astype(F32)[:, None, :]
    out[...] = attended.astype(BF16).reshape(rows, heads * HEAD_SIZE)


def attend(queries, key_cache, cached_value_rows, new_key, token_value, lengths):
    sources = (queries, new_key, key_cache, token_value, cached_value_rows)
    return pl.pallas_call(
        attend_kernel,
        out_shape=jax.ShapeDtypeStruct(queries.shape, BF16),
        in_specs=[pl.BlockSpec(memory_space=pltpu.SMEM)]
        + [pl.BlockSpec(memory_space=pl.ANY)] * 5,
        out_specs=pl.BlockSpec(memory_space=pltpu.VMEM),
        scratch_shapes=[pltpu.VMEM(s.shape, BF16) for s in sources]
        + [pltpu.SemaphoreType.DMA((5,))],
        compiler_params=pltpu.CompilerParams(vmem_limit_bytes=ATTEND_VMEM),
    )(lengths, *sources)


def dot(left, right):
    return jnp.dot(left, right, preferred_element_type=F32).astype(BF16)


def add(*terms):
    total = terms[0].astype(F32)
    for term in terms[1:]:
        total = total + term.astype(F32)
    return total


def in_three(value):
    high = value.astype(BF16)
    rest = value - high.astype(F32)
    middle = rest.astype(BF16)
    low = (rest - middle.astype(F32)).astype(BF16)
    column = lax.broadcasted_iota(jnp.int32, (value.shape[0], 128), 1)
    parts = jnp.where(
        column == 0, high[:, None], jnp.where(column == 1, middle[:, None], low[:, None])
    )
    return jnp.where(column < 3, parts, jnp.zeros_like(parts))


def project(chunks, out_weight):
    with jax.named_scope("projection"):
        return products(chunks, out_weight, True)


def sum_projected(own, away):
    with jax.named_scope("sum_projected"):
        part = own.shape[0] // 4
        pieces = [
            add(own[d * part : (d + 1) * part], away[d * part : (d + 1) * part]) for d in range(4)
        ]
        moved = [along_y(pieces[d].astype(BF16), d) for d in (1, 3, 2)]
        return add(pieces[0], *moved).astype(BF16)


def to_owners(summed):
    with jax.named_scope("to_owners"):
        rows = summed.shape[0] // 2
        blocks = [
            send(
                summed[s * rows : (s + 1) * rows],
                lambda x, y, z, core, s=s: (y, x, (y - core * 2 - (s ^ (z & 1))) & 3, z >> 1),
            )
            for s in range(2)
        ]
        x, _, z, _ = my_place()
        odd = ((x - z) & 1) == 1
        return jnp.concatenate(
            [jnp.where(odd, blocks[1], blocks[0]), jnp.where(odd, blocks[0], blocks[1])], axis=1
        )


def norm(residual, projected, norm_gain):
    with jax.named_scope("norm"):
        middle = residual + projected.astype(F32)
        squares = jnp.sum(middle * middle, axis=1)
        scaled = (middle * norm_gain.astype(F32)).astype(BF16)
        return middle, jnp.concatenate([scaled, in_three(squares)], axis=1)


def make_hidden(chunks, gate_weight, up_weight):
    width, cols = gate_weight.shape
    rows = chunks[0].shape[0] // 4
    with jax.named_scope("gate_up"):
        first_gate, first_up = [dot(chunks[0][:, :width], w) for w in (gate_weight, up_weight)]
        own_rows, away_rows, own_squares, away_squares = split(chunks, False, width)
        away_gate = in_place(first_gate, dot(away_rows, gate_weight), False, 1)
        away_up = in_place(first_up, dot(away_rows, up_weight), False, 1)
        away = [to_other_core(t) for t in (away_gate, away_up, away_squares)]
        own_rows = after(own_rows, away_gate, away_up)
        own_gate = in_place(first_gate, dot(own_rows, gate_weight), False, 0)
        own_rows = after(own_rows, away[0])
        own_up = in_place(first_up, dot(own_rows, up_weight), False, 0)
        own = [own_gate, own_up, own_squares]

    def piece(low, xor):
        at = (low * 4 + (-xor & 3)) * rows
        gate, up, square = [add(o[at : at + rows], a[at : at + rows]) for o, a in zip(own, away)]
        return gate, up, jnp.sum(square, axis=1)

    def plus(total, message):
        gate, up, square = total
        more = jnp.sum(message[:, 2 * cols :].astype(F32), axis=1)
        return add(gate, message[:, :cols]), add(up, message[:, cols : 2 * cols]), square + more

    def message(*totals):
        gate, up, square = [jnp.concatenate(t, axis=0) for t in zip(*totals)]
        return jnp.concatenate([gate.astype(BF16), up.astype(BF16), in_three(square)], axis=1)

    with jax.named_scope("sum_terms"):
        low = across_y(message(piece(0, 2), piece(0, 1)), 1)
        high = across_y(message(piece(1, 3), piece(1, 2)), 3)
        low, high = lax.optimization_barrier((low, high))
        low_last = across_y(message(plus(piece(0, 3), low[:rows])), 3)
        high_last = across_y(message(plus(piece(1, 1), high[rows:])), 1)
        low_last, high_last = lax.optimization_barrier((low_last, high_last))
        sums = [
            plus(plus(piece(0, 0), low[rows:]), low_last),
            plus(plus(piece(1, 0), high[:rows]), high_last),
        ]
        gate, up, square = [jnp.concatenate(t, axis=0) for t in zip(*sums)]
        inv_rms = lax.rsqrt(square / D + 1e-05)[:, None]
        return (jax.nn.silu(inv_rms * gate) * (inv_rms * up)).astype(BF16)


def down_product(hidden, down_weight):
    with jax.named_scope("gather_hidden"):
        theirs = to_other_core(hidden)
        got = {d: along_y(hidden, d) for d in (2, 1, 3)}
    with jax.named_scope("down"):
        first = dot(jnp.concatenate([hidden, theirs], axis=0), down_weight)
        rest = [half for d in (1, 2, 3) for half in (got[d], to_other_core(got[d]))]
        return order_down(first, dot(jnp.concatenate(rest, axis=0), down_weight))


def sum_down(down):
    with jax.named_scope("sum_down"):
        rows, chunk = down.shape[0] // 16, down.shape[0] // 4
        far = {j: along_second(down[j * chunk + rows : (j + 1) * chunk], -j) for j in (1, 3, 2)}
        near = []
        for i in (1, 3, 2):
            cut = slice((i - 1) * rows, i * rows)
            total = add(down[i * rows : (i + 1) * rows], *[far[j][cut] for j in (1, 2, 3)])
            near.append(along_first(total.astype(BF16), -i))
        side = [
            along_second(after(down[j * chunk : j * chunk + rows], far[1]), -j) for j in (1, 3, 2)
        ]
        return add(down[:rows], *side, *near)


def local(
    queries,
    key_cache,
    cached_value_rows,
    new_key,
    token_value,
    lengths,
    residual,
    out_weight,
    norm_gain,
    gate_weight,
    up_weight,
    down_weight,
):
    with jax.named_scope("attention"):
        attended = attend(queries, key_cache, cached_value_rows, new_key, token_value, lengths)
    with jax.named_scope("gather_attended"):
        gathered = gather_rows(attended)
    summed = sum_projected(*project(gathered, out_weight))
    middle, message = norm(residual, to_owners(summed), norm_gain)
    with jax.named_scope("gather_scaled"):
        gathered = gather_rows(message)
    hidden = make_hidden(gathered, gate_weight, up_weight)
    return middle + sum_down(down_product(hidden, down_weight))


def solution(mesh):
    placed = (
        P("ffn", "attn"),
        P("ffn", None, "attn"),
        P("ffn", None, "attn"),
        P("ffn", "attn"),
        P("ffn", "attn"),
        P("ffn"),
        P("ffn", "attn"),
        P("attn", "ffn"),
        P("attn"),
        P("attn", "ffn"),
        P("attn", "ffn"),
        P("ffn", "attn"),
    )
    return jax.shard_map(
        local, mesh=mesh, in_specs=placed, out_specs=P("ffn", "attn"), check_vma=False
    )
```

time: 345 us -> 171 us (0.50)
  waiting for transfers between devices: 201 us -> 75.5 us
  blocking collectives: 86 us -> 0 us
  starting transfers between devices: 0.17 us -> 62.7 us
  between operations: 13.3 us -> 0.6 us
  matrix products: 31.7 us -> 21.2 us
  other arithmetic: 9.53 us -> 4.69 us
  Pallas kernels: 0 us -> 4.79 us
    reduce_scatter x2 -> x0, waiting for transfers between devices: 104 us -> none  [the longest x1 74.3 us: local(): lax.psum_scatter(jnp.dot(block_rows, down_weight, preferred_element_type=...]
    all_gather x2 -> x0, waiting for transfers between devices: 92.4 us -> none  [the longest x1 47.8 us: local(): lax.all_gather(attended_output, 'ffn', axis=0, tiled=True)]
    ppermute x0 -> x41, waiting for transfers between devices: none -> 75.5 us  [send(): return lax.ppermute(value, AXES, pairs)]
    psum x1 -> x0, blocking collectives: 65.1 us -> none  [local(): squares = lax.psum(placed, ('attn', 'ffn'))]
    ppermute x0 -> x41, starting transfers between devices: none -> 62.7 us  [send(): return lax.ppermute(value, AXES, pairs)]
    all_to_all x1 -> x0, blocking collectives: 20.9 us -> none  [local(): lax.all_to_all(projected.astype(jnp.bfloat16), 'ffn', split_axis=0, conca...]
    dot_general x7 -> x11, matrix products: 31.7 us -> 21.2 us  [dot(): return jnp.dot(left, right, preferred_element_type=F32).astype(BF16)]
    pallas_call x0 -> x10, Pallas kernels: none -> 4.79 us  [the longest x1 3.92 us: attend(): pl.pallas_call(attend_kernel, out_shape=jax.ShapeDtypeStruct(queries.shap...]
  transfers between devices with their start and end apart: 5 -> 41, of which waited for: 5 -> 25; matrix products, arithmetic and copies ran while one was open for 0% -> 9% of each run, Pallas kernels for 0% -> 0%
where the time goes in v2:
time: 171 us; the launch traced here: 170 us
  waiting for transfers between devices  75.5 us (44%)
  starting transfers between devices  62.7 us (37%)
  matrix products  21.2 us (12%)
  Pallas kernels  4.79 us (3%)
  other arithmetic  4.69 us (3%)
    ppermute x41, waiting for transfers between devices, send(): return lax.ppermute(value, AXES, pairs)  75.5 us
    ppermute x41, starting transfers between devices, send(): return lax.ppermute(value, AXES, pairs)  62.7 us
    dot_general x11, matrix products, dot(): return jnp.dot(left, right, preferred_element_type=F32).astype(BF16)  21.2 us
    pallas_call x1, Pallas kernels, attend(): pl.pallas_call(attend_kernel, out_shape=jax.ShapeDtypeStruct(queries.shap...  3.92 us
  transfers between devices with their start and end apart: 41, of which 25 were waited for; matrix products, arithmetic and copies ran while one was open for 9% of the time, Pallas kernels for 0%

profile of v2, /device:TPU:0, one launch (start us, length us, event | category | flops | bytes accessed | tf_op | source)
XLA Modules:
  0.0 169.8 jit_solution(8328843252900123559)
XLA Ops:
  0.0 3.9 %attention.1 = bf16[32,2048]{1,0:T(8,128)(2,1)} custom-call(s32[32]{0:T(128)} %lengths.1, bf16[32,2048]{1,0:T(8,128)(2,1)} %refs_0_.1, bf16[32,128]{1,0:T(8,128)(2,1)} %refs_1_.1, bf16[32,128,128]{2,1,0:T(8,128)(2,1)} %refs_2_.1, bf16[32,128]{1,0:T(8,128)(2,1)} %refs_3_.1, bf16[32,128,128]{2,1,0:T(8,128)(2,1)} %refs_4_.1), custom_call_target="tpu_custom_call" | custom-call | tf_op jit(solution)/shard_map/attention/pallas_call | solution.py:220
  3.9 1.6 collective-permute-start
  5.6 2.7 %collective-permute-start.1 = (bf16[32,2048]{1,0:T(8,128)(2,1)}, bf16[32,2048]{1,0:T(8,128)(2,1)S(1)}, u32[]{:S(2)}, u32[]{:S(2)}) collective-permute-start(bf16[32,2048]{1,0:T(8,128)(2,1)} %attention.1), channel_id=1, source_target_pairs={{0,8},{1,9},{2,10},{3,11},{4,12},{5,13},{6,14},{7,15},{8,0},{9,1},... | collective-permute-start | bytes 393224 | tf_op jit(solution)/shard_map/gather_attended/ppermute | solution.py:29
  8.3 1.4 collective-permute-start.2
  10.4 2.5 %collective-permute-done.1 = bf16[32,2048]{1,0:T(8,128)(2,1)S(1)} collective-permute-done((bf16[32,2048]{1,0:T(8,128)(2,1)}, bf16[32,2048]{1,0:T(8,128)(2,1)S(1)}, u32[]{:S(2)}, u32[]{:S(2)}) %collective-permute-start.1) | collective-permute-done | bytes 131104 | tf_op jit(solution)/shard_map/gather_attended/ppermute | solution.py:29
  14.4 2.0 %collective-permute-start.3 = (bf16[128,2048]{1,0:T(8,128)(2,1)S(1)}, bf16[128,2048]{1,0:T(8,128)(2,1)S(1)}, u32[]{:S(2)}, u32[]{:S(2)}) collective-permute-start(bf16[128,2048]{1,0:T(8,128)(2,1)S(1)} %pad_maximum_fusion.1.refs_0_), channel_id=1, source_target_pairs={{0,1},{1,2},{2,3},{3,0},{4,5},{5,6},{6,7},{7,4},{8,9},{9,10},{10,1... | collective-permute-start | bytes 1572872 | tf_op jit(solution)/shard_map/gather_attended/ppermute | solution.py:29
  16.4 3.6 %collective-permute-start.4 = (bf16[128,2048]{1,0:T(8,128)(2,1)S(1)}, bf16[128,2048]{1,0:T(8,128)(2,1)S(1)}, u32[]{:S(2)}, u32[]{:S(2)}) collective-permute-start(bf16[128,2048]{1,0:T(8,128)(2,1)S(1)} %pad_maximum_fusion.1.refs_0_), channel_id=1, source_target_pairs={{0,2},{1,3},{2,0},{3,1},{4,6},{5,7},{6,4},{7,5},{8,10},{9,11},{10,... | collective-permute-start | bytes 1572872 | tf_op jit(solution)/shard_map/gather_attended/ppermute | solution.py:29
  21.0 3.1 %convolution_convert_fusion.10.first = bf16[128,1024]{1,0:T(8,128)(2,1)S(1)} fusion(bf16[2048,1024]{1,0:T(8,128)(2,1)} %param.19, bf16[32,2048]{1,0:T(8,128)(2,1)S(1)} %collective-permute-done.2, bf16[32,2048]{1,0:T(8,128)(2,1)S(1)} %collective-permute-done.1, bf16[32,2048]{1,0:T(8,128)(2,1)S(1)} %collective-permute-done, bf16[32,2048]{1,0:T(8,128)(2,1)} %attention.1), kind=kOutput, calls=%fused_computation.10 | convolution fusion | flops 539099136 | bytes 4980736 | tf_op jit(solution)/shard_map/projection/dot_general | solution.py:233
  24.1 1.6 collective-permute-done.3.refs_1_
  25.7 7.1 %collective-permute-done.4.refs_2_ = bf16[128,2048]{1,0:T(8,128)(2,1)S(1)} collective-permute-done((bf16[128,2048]{1,0:T(8,128)(2,1)S(1)}, bf16[128,2048]{1,0:T(8,128)(2,1)S(1)}, u32[]{:S(2)}, u32[]{:S(2)}) %collective-permute-start.4) | collective-permute-done | bytes 524320 | tf_op jit(solution)/shard_map/gather_attended/ppermute | solution.py:29
  36.1 1.6 collective-permute-start.7
  37.8 1.7 collective-permute-start.8
  39.4 2.0 %collective-permute-start.9 = (bf16[64,1024]{1,0:T(8,128)(2,1)S(1)}, bf16[64,1024]{1,0:T(8,128)(2,1)S(1)}, u32[]{:S(2)}, u32[]{:S(2)}) collective-permute-start(bf16[64,1024]{1,0:T(8,128)(2,1)S(1)} %get-tuple-element.81), channel_id=1, source_target_pairs={{0,64},{1,65},{2,66},{3,67},{4,68},{5,69},{6,70},{7,71},{8,72},{9,... | collective-permute-start | bytes 393224 | tf_op jit(solution)/shard_map/sum_projected/ppermute | solution.py:29
  41.4 1.6 collective-permute-done.7
  43.0 2.2 %collective-permute-done.8 = bf16[64,1024]{1,0:T(8,128)(2,1)S(1)} collective-permute-done((bf16[64,1024]{1,0:T(8,128)(2,1)S(1)}, bf16[64,1024]{1,0:T(8,128)(2,1)S(1)}, u32[]{:S(2)}, u32[]{:S(2)}) %collective-permute-start.8) | collective-permute-done | bytes 131104 | tf_op jit(solution)/shard_map/sum_projected/ppermute | solution.py:29
  45.2 1.8 %collective-permute-done.9 = bf16[64,1024]{1,0:T(8,128)(2,1)S(1)} collective-permute-done((bf16[64,1024]{1,0:T(8,128)(2,1)S(1)}, bf16[64,1024]{1,0:T(8,128)(2,1)S(1)}, u32[]{:S(2)}, u32[]{:S(2)}) %collective-permute-start.9) | collective-permute-done | bytes 131104 | tf_op jit(solution)/shard_map/sum_projected/ppermute | solution.py:29
  47.1 4.1 %collective-permute-start.10 = (bf16[32,1024]{1,0:T(8,128)(2,1)S(1)}, bf16[32,1024]{1,0:T(8,128)(2,1)S(1)}, u32[]{:S(2)}, u32[]{:S(2)}) collective-permute-start(bf16[32,1024]{1,0:T(8,128)(2,1)S(1)} %get-tuple-element.89), channel_id=1, source_target_pairs={{0,3},{1,0},{2,19},{3,16},{4,35},{5,32},{6,51},{7,48},{8,67},{9,64... | collective-permute-start | bytes 196616 | tf_op jit(solution)/shard_map/to_owners/ppermute | solution.py:29
  51.8 1.4 collective-permute-done.10
  53.6 8.0 %collective-permute-start.12 = (bf16[32,2176]{1,0:T(8,128)(2,1)S(1)}, bf16[32,2176]{1,0:T(8,128)(2,1)S(1)}, u32[]{:S(2)}, u32[]{:S(2)}) collective-permute-start(bf16[32,2176]{1,0:T(8,128)(2,1)S(1)} %pad_maximum_fusion.6), channel_id=1, source_target_pairs={{0,4},{1,5},{2,6},{3,7},{4,8},{5,9},{6,10},{7,11},{8,12},{9,13},{1... | collective-permute-start | bytes 417800 | tf_op jit(solution)/shard_map/gather_scaled/ppermute | solution.py:29
  61.5 6.4 %collective-permute-start.13 = (bf16[32,2176]{1,0:T(8,128)(2,1)S(1)}, bf16[32,2176]{1,0:T(8,128)(2,1)S(1)}, u32[]{:S(2)}, u32[]{:S(2)}) collective-permute-start(bf16[32,2176]{1,0:T(8,128)(2,1)S(1)} %pad_maximum_fusion.6), channel_id=1, source_target_pairs={{0,8},{1,9},{2,10},{3,11},{4,12},{5,13},{6,14},{7,15},{8,0},{9,1},... | collective-permute-start | bytes 417800 | tf_op jit(solution)/shard_map/gather_scaled/ppermute | solution.py:29
  67.9 1.6 collective-permute-done.12
  69.5 2.9 %collective-permute-done.13 = bf16[32,2176]{1,0:T(8,128)(2,1)S(1)} collective-permute-done((bf16[32,2176]{1,0:T(8,128)(2,1)S(1)}, bf16[32,2176]{1,0:T(8,128)(2,1)S(1)}, u32[]{:S(2)}, u32[]{:S(2)}) %collective-permute-start.13) | collective-permute-done | bytes 139296 | tf_op jit(solution)/shard_map/gather_scaled/ppermute | solution.py:29
  73.1 2.1 %collective-permute-start.16 = (bf16[128,2176]{1,0:T(8,128)(2,1)S(1)}, bf16[128,2176]{1,0:T(8,128)(2,1)S(1)}, u32[]{:S(2)}, u32[]{:S(2)}) collective-permute-start(bf16[128,2176]{1,0:T(8,128)(2,1)S(1)} %pad_maximum_fusion.refs_0_), channel_id=1, source_target_pairs={{0,2},{1,3},{2,0},{3,1},{4,6},{5,7},{6,4},{7,5},{8,10},{9,11},{10,... | collective-permute-start | bytes 1671176 | tf_op jit(solution)/shard_map/gather_scaled/ppermute | solution.py:29
  76.3 4.2 %convolution_convert_fusion.7.first = bf16[128,1664]{1,0:T(8,128)(2,1)S(1)} fusion(bf16[2048,1664]{1,0:T(8,128)(2,1)} %param.21, bf16[128,2176]{1,0:T(8,128)(2,1)S(1)} %pad_maximum_fusion.refs_0_), kind=kOutput, calls=%fused_computation.7 | convolution fusion | flops 872628224 | bytes 7766016 | tf_op jit(solution)/shard_map/gate_up/dot_general | solution.py:233
  80.6 1.2 convolution_convert_fusion.6.first
  81.8 8.0 %collective-permute-done.15.refs_1_ = bf16[128,2176]{1,0:T(8,128)(2,1)S(1)} collective-permute-done((bf16[128,2176]{1,0:T(8,128)(2,1)S(1)}, bf16[128,2176]{1,0:T(8,128)(2,1)S(1)}, u32[]{:S(2)}, u32[]{:S(2)}) %collective-permute-start.15) | collective-permute-done | bytes 557088 | tf_op jit(solution)/shard_map/gather_scaled/ppermute | solution.py:29
  90.9 1.6 convolution_convert_fusion.4.rest
  92.5 1.6 convolution_convert_fusion.3.rest
  95.0 1.6 convolution_convert_fusion.2.rest
  96.7 1.2 collective-permute-done.18
  98.5 1.6 convolution_convert_fusion.1.rest
  100.5 4.3 %collective-permute-start.22 = (bf16[64,3456]{1,0:T(8,128)(2,1)S(1)}, bf16[64,3456]{1,0:T(8,128)(2,1)S(1)}, u32[]{:S(2)}, u32[]{:S(2)}) collective-permute-start(bf16[64,3456]{1,0:T(8,128)(2,1)S(1)} %pad_maximum_fusion.3), channel_id=1, source_target_pairs={{0,96},{1,97},{2,98},{3,99},{4,100},{5,101},{6,102},{7,103},{8,104... | collective-permute-start | bytes 1327112 | tf_op jit(solution)/shard_map/sum_terms/ppermute | solution.py:29
  104.9 10.3 %collective-permute-done.22 = bf16[64,3456]{1,0:T(8,128)(2,1)S(1)} collective-permute-done((bf16[64,3456]{1,0:T(8,128)(2,1)S(1)}, bf16[64,3456]{1,0:T(8,128)(2,1)S(1)}, u32[]{:S(2)}, u32[]{:S(2)}) %collective-permute-start.22) | collective-permute-done | bytes 442400 | tf_op jit(solution)/shard_map/sum_terms/ppermute | solution.py:29
  115.3 1.6 collective-permute-done.21
  117.8 1.2 collective-permute-start.23
  119.0 4.8 %collective-permute-done.24 = bf16[32,3456]{1,0:T(8,128)(2,1)S(1)} collective-permute-done((bf16[32,3456]{1,0:T(8,128)(2,1)S(1)}, bf16[32,3456]{1,0:T(8,128)(2,1)S(1)}, u32[]{:S(2)}, u32[]{:S(2)}) %collective-permute-start.24) | collective-permute-done | bytes 221216 | tf_op jit(solution)/shard_map/sum_terms/ppermute | solution.py:29
  123.8 1.6 collective-permute-done.23
  126.5 2.6 %collective-permute-start.28 = (bf16[64,1664]{1,0:T(8,128)(2,1)S(1)}, bf16[64,1664]{1,0:T(8,128)(2,1)S(1)}, u32[]{:S(2)}, u32[]{:S(2)}) collective-permute-start(bf16[64,1664]{1,0:T(8,128)(2,1)S(1)} %fusion.3), channel_id=1, source_target_pairs={{0,64},{1,65},{2,66},{3,67},{4,68},{5,69},{6,70},{7,71},{8,72},{9,... | collective-permute-start | bytes 638984 | tf_op jit(solution)/shard_map/gather_hidden/ppermute | solution.py:29
  129.2 1.1 collective-permute-start.30
  130.3 7.1 %collective-permute-done.26 = bf16[64,1664]{1,0:T(8,128)(2,1)S(1)} collective-permute-done((bf16[64,1664]{1,0:T(8,128)(2,1)S(1)}, bf16[64,1664]{1,0:T(8,128)(2,1)S(1)}, u32[]{:S(2)}, u32[]{:S(2)}) %collective-permute-start.26) | collective-permute-done | bytes 213024 | tf_op jit(solution)/shard_map/gather_hidden/ppermute | solution.py:29
  138.0 1.2 convolution_convert_fusion.5.first
  139.5 3.0 %convolution_convert_fusion.rest = bf16[384,2048]{1,0:T(8,128)(2,1)S(1)} fusion(bf16[384,1664]{1,0:T(8,128)(2,1)S(1)} %constant_dynamic-update-slice_fusion, bf16[1664,2048]{1,0:T(8,128)(2,1)S(1)} %bitcast.23), kind=kOutput, calls=%fused_computation | convolution fusion | flops 2618032128 | bytes 9666560 | tf_op jit(solution)/shard_map/down/dot_general | solution.py:233
  142.8 2.4 %collective-permute-start.32 = (bf16[96,2048]{1,0:T(8,128)(2,1)S(1)}, bf16[96,2048]{1,0:T(8,128)(2,1)S(1)}, u32[]{:S(2)}, u32[]{:S(2)}) collective-permute-start(bf16[96,2048]{1,0:T(8,128)(2,1)S(1)} %get-tuple-element.59), channel_id=1, source_target_pairs={{0,3},{1,0},{2,1},{3,2},{4,7},{5,4},{6,5},{7,6},{8,11},{9,8},{10,9... | collective-permute-start | bytes 1179656 | tf_op jit(solution)/shard_map/sum_down/ppermute | solution.py:29
  146.2 8.6 %collective-permute-done.32 = bf16[96,2048]{1,0:T(8,128)(2,1)S(1)} collective-permute-done((bf16[96,2048]{1,0:T(8,128)(2,1)S(1)}, bf16[96,2048]{1,0:T(8,128)(2,1)S(1)}, u32[]{:S(2)}, u32[]{:S(2)}) %collective-permute-start.32) | collective-permute-done | bytes 393248 | tf_op jit(solution)/shard_map/sum_down/ppermute | solution.py:29
  154.8 3.7 %collective-permute-start.33 = (bf16[32,2048]{1,0:T(8,128)(2,1)S(1)}, bf16[32,2048]{1,0:T(8,128)(2,1)S(1)}, u32[]{:S(2)}, u32[]{:S(2)}) collective-permute-start(bf16[32,2048]{1,0:T(8,128)(2,1)S(1)} %get-tuple-element.34), channel_id=1, source_target_pairs={{0,3},{1,0},{2,1},{3,2},{4,7},{5,4},{6,5},{7,6},{8,11},{9,8},{10,9... | collective-permute-start | bytes 393224 | tf_op jit(solution)/shard_map/sum_down/ppermute | solution.py:29
  158.4 1.5 collective-permute-start.35
  160.1 1.2 collective-permute-start.38
  162.9 5.4 %collective-permute-done.34 = bf16[32,2048]{1,0:T(8,128)(2,1)S(1)} collective-permute-done((bf16[32,2048]{1,0:T(8,128)(2,1)S(1)}, bf16[32,2048]{1,0:T(8,128)(2,1)S(1)}, u32[]{:S(2)}, u32[]{:S(2)}) %collective-permute-start.34) | collective-permute-done | bytes 131104 | tf_op jit(solution)/shard_map/sum_down/ppermute | solution.py:29
  (124 shorter events, 19.6 us)
Async XLA Ops:
  3.9 6.5 %collective-permute-start = (bf16[32,2048]{1,0:T(8,128)(2,1)}, bf16[32,2048]{1,0:T(8,128)(2,1)S(1)}, u32[]{:S(2)}, u32[]{:S(2)}) collective-permute-start(bf16[32,2048]{1,0:T(8,128)(2,1)} %attention.1), channel_id=1, source_target_pairs={{0,4},{1,5},{2,6},{3,7},{4,8},{5,9},{6,10},{7,11},{8,12},{9,13},{1... | collective-permute-start | bytes 393224 | tf_op jit(solution)/shard_map/gather_attended/ppermute | solution.py:29
  5.6 7.3 %collective-permute-start.1 = (bf16[32,2048]{1,0:T(8,128)(2,1)}, bf16[32,2048]{1,0:T(8,128)(2,1)S(1)}, u32[]{:S(2)}, u32[]{:S(2)}) collective-permute-start(bf16[32,2048]{1,0:T(8,128)(2,1)} %attention.1), channel_id=1, source_target_pairs={{0,8},{1,9},{2,10},{3,11},{4,12},{5,13},{6,14},{7,15},{8,0},{9,1},... | collective-permute-start | bytes 393224 | tf_op jit(solution)/shard_map/gather_attended/ppermute | solution.py:29
  8.3 5.2 %collective-permute-start.2 = (bf16[32,2048]{1,0:T(8,128)(2,1)}, bf16[32,2048]{1,0:T(8,128)(2,1)S(1)}, u32[]{:S(2)}, u32[]{:S(2)}) collective-permute-start(bf16[32,2048]{1,0:T(8,128)(2,1)} %attention.1), channel_id=1, source_target_pairs={{0,12},{1,13},{2,14},{3,15},{4,0},{5,1},{6,2},{7,3},{8,4},{9,5},{1... | collective-permute-start | bytes 393224 | tf_op jit(solution)/shard_map/gather_attended/ppermute | solution.py:29
  14.4 11.3 %collective-permute-start.3 = (bf16[128,2048]{1,0:T(8,128)(2,1)S(1)}, bf16[128,2048]{1,0:T(8,128)(2,1)S(1)}, u32[]{:S(2)}, u32[]{:S(2)}) collective-permute-start(bf16[128,2048]{1,0:T(8,128)(2,1)S(1)} %pad_maximum_fusion.1.refs_0_), channel_id=1, source_target_pairs={{0,1},{1,2},{2,3},{3,0},{4,5},{5,6},{6,7},{7,4},{8,9},{9,10},{10,1... | collective-permute-start | bytes 1572872 | tf_op jit(solution)/shard_map/gather_attended/ppermute | solution.py:29
  16.4 16.4 %collective-permute-start.4 = (bf16[128,2048]{1,0:T(8,128)(2,1)S(1)}, bf16[128,2048]{1,0:T(8,128)(2,1)S(1)}, u32[]{:S(2)}, u32[]{:S(2)}) collective-permute-start(bf16[128,2048]{1,0:T(8,128)(2,1)S(1)} %pad_maximum_fusion.1.refs_0_), channel_id=1, source_target_pairs={{0,2},{1,3},{2,0},{3,1},{4,6},{5,7},{6,4},{7,5},{8,10},{9,11},{10,... | collective-permute-start | bytes 1572872 | tf_op jit(solution)/shard_map/gather_attended/ppermute | solution.py:29
  20.0 12.8 %collective-permute-start.5 = (bf16[128,2048]{1,0:T(8,128)(2,1)S(1)}, bf16[128,2048]{1,0:T(8,128)(2,1)S(1)}, u32[]{:S(2)}, u32[]{:S(2)}) collective-permute-start(bf16[128,2048]{1,0:T(8,128)(2,1)S(1)} %pad_maximum_fusion.1.refs_0_), channel_id=1, source_target_pairs={{0,3},{1,0},{2,1},{3,2},{4,7},{5,4},{6,5},{7,6},{8,11},{9,8},{10,9... | collective-permute-start | bytes 1572872 | tf_op jit(solution)/shard_map/gather_attended/ppermute | solution.py:29
  21.0 11.9 %copy-start.2 = (bf16[2048,1024]{1,0:T(8,128)(2,1)S(1)}, bf16[2048,1024]{1,0:T(8,128)(2,1)}, u32[]{:S(2)}) copy-start(bf16[2048,1024]{1,0:T(8,128)(2,1)} %param.19) | copy-start | bytes 12582916
  34.0 2.0 %collective-permute-start.6 = (bf16[256,1024]{1,0:T(8,128)(2,1)S(1)}, bf16[256,1024]{1,0:T(8,128)(2,1)S(1)}, u32[]{:S(2)}, u32[]{:S(2)}) collective-permute-start(bf16[256,1024]{1,0:T(8,128)(2,1)S(1)} %projection.4), channel_id=1, source_target_pairs={{0,16},{1,17},{2,18},{3,19},{4,20},{5,21},{6,22},{7,23},{8,24},{9,... | collective-permute-start | bytes 1572872 | tf_op jit(solution)/shard_map/projection/ppermute | solution.py:29
  35.1 18.2 %copy-start = (f32[32,2048]{1,0:T(8,128)S(1)}, f32[32,2048]{1,0:T(8,128)}, u32[]{:S(2)}) copy-start(f32[32,2048]{1,0:T(8,128)} %param.18) | copy-start | bytes 786436
  36.1 6.9 %collective-permute-start.7 = (bf16[64,1024]{1,0:T(8,128)(2,1)S(1)}, bf16[64,1024]{1,0:T(8,128)(2,1)S(1)}, u32[]{:S(2)}, u32[]{:S(2)}) collective-permute-start(bf16[64,1024]{1,0:T(8,128)(2,1)S(1)} %get-tuple-element.80), channel_id=1, source_target_pairs={{0,32},{1,33},{2,34},{3,35},{4,36},{5,37},{6,38},{7,39},{8,40},{9,... | collective-permute-start | bytes 393224 | tf_op jit(solution)/shard_map/sum_projected/ppermute | solution.py:29
  37.8 7.4 %collective-permute-start.8 = (bf16[64,1024]{1,0:T(8,128)(2,1)S(1)}, bf16[64,1024]{1,0:T(8,128)(2,1)S(1)}, u32[]{:S(2)}, u32[]{:S(2)}) collective-permute-start(bf16[64,1024]{1,0:T(8,128)(2,1)S(1)} %get-tuple-element.82), channel_id=1, source_target_pairs={{0,96},{1,97},{2,98},{3,99},{4,100},{5,101},{6,102},{7,103},{8,104... | collective-permute-start | bytes 393224 | tf_op jit(solution)/shard_map/sum_projected/ppermute | solution.py:29
  39.4 7.6 %collective-permute-start.9 = (bf16[64,1024]{1,0:T(8,128)(2,1)S(1)}, bf16[64,1024]{1,0:T(8,128)(2,1)S(1)}, u32[]{:S(2)}, u32[]{:S(2)}) collective-permute-start(bf16[64,1024]{1,0:T(8,128)(2,1)S(1)} %get-tuple-element.81), channel_id=1, source_target_pairs={{0,64},{1,65},{2,66},{3,67},{4,68},{5,69},{6,70},{7,71},{8,72},{9,... | collective-permute-start | bytes 393224 | tf_op jit(solution)/shard_map/sum_projected/ppermute | solution.py:29
  47.1 6.2 %collective-permute-start.10 = (bf16[32,1024]{1,0:T(8,128)(2,1)S(1)}, bf16[32,1024]{1,0:T(8,128)(2,1)S(1)}, u32[]{:S(2)}, u32[]{:S(2)}) collective-permute-start(bf16[32,1024]{1,0:T(8,128)(2,1)S(1)} %get-tuple-element.89), channel_id=1, source_target_pairs={{0,3},{1,0},{2,19},{3,16},{4,35},{5,32},{6,51},{7,48},{8,67},{9,64... | collective-permute-start | bytes 196616 | tf_op jit(solution)/shard_map/to_owners/ppermute | solution.py:29
  51.2 2.1 %collective-permute-start.11 = (bf16[32,1024]{1,0:T(8,128)(2,1)S(1)}, bf16[32,1024]{1,0:T(8,128)(2,1)S(1)}, u32[]{:S(2)}, u32[]{:S(2)}) collective-permute-start(bf16[32,1024]{1,0:T(8,128)(2,1)S(1)} %get-tuple-element.90), channel_id=1, source_target_pairs={{0,0},{1,3},{2,16},{3,19},{4,32},{5,35},{6,48},{7,51},{8,64},{9,67... | collective-permute-start | bytes 196616 | tf_op jit(solution)/shard_map/to_owners/ppermute | solution.py:29
  53.6 15.9 %collective-permute-start.12 = (bf16[32,2176]{1,0:T(8,128)(2,1)S(1)}, bf16[32,2176]{1,0:T(8,128)(2,1)S(1)}, u32[]{:S(2)}, u32[]{:S(2)}) collective-permute-start(bf16[32,2176]{1,0:T(8,128)(2,1)S(1)} %pad_maximum_fusion.6), channel_id=1, source_target_pairs={{0,4},{1,5},{2,6},{3,7},{4,8},{5,9},{6,10},{7,11},{8,12},{9,13},{1... | collective-permute-start | bytes 417800 | tf_op jit(solution)/shard_map/gather_scaled/ppermute | solution.py:29
  61.5 10.9 %collective-permute-start.13 = (bf16[32,2176]{1,0:T(8,128)(2,1)S(1)}, bf16[32,2176]{1,0:T(8,128)(2,1)S(1)}, u32[]{:S(2)}, u32[]{:S(2)}) collective-permute-start(bf16[32,2176]{1,0:T(8,128)(2,1)S(1)} %pad_maximum_fusion.6), channel_id=1, source_target_pairs={{0,8},{1,9},{2,10},{3,11},{4,12},{5,13},{6,14},{7,15},{8,0},{9,1},... | collective-permute-start | bytes 417800 | tf_op jit(solution)/shard_map/gather_scaled/ppermute | solution.py:29
  67.9 5.1 %collective-permute-start.14 = (bf16[32,2176]{1,0:T(8,128)(2,1)S(1)}, bf16[32,2176]{1,0:T(8,128)(2,1)S(1)}, u32[]{:S(2)}, u32[]{:S(2)}) collective-permute-start(bf16[32,2176]{1,0:T(8,128)(2,1)S(1)} %pad_maximum_fusion.6), channel_id=1, source_target_pairs={{0,12},{1,13},{2,14},{3,15},{4,0},{5,1},{6,2},{7,3},{8,4},{9,5},{1... | collective-permute-start | bytes 417800 | tf_op jit(solution)/shard_map/gather_scaled/ppermute | solution.py:29
  72.9 7.6 %slice-start.2 = ((s8[6815744]{0:T(1024)(128)(4,1)}), s8[4194304]{0:T(1024)(128)(4,1)S(1)}, s32[]{:S(2)}) async-start(s8[6815744]{0:T(1024)(128)(4,1)} %bitcast.20), calls=%async_computation.2 | async-start | bytes 8388608
  73.0 16.8 %collective-permute-start.15 = (bf16[128,2176]{1,0:T(8,128)(2,1)S(1)}, bf16[128,2176]{1,0:T(8,128)(2,1)S(1)}, u32[]{:S(2)}, u32[]{:S(2)}) collective-permute-start(bf16[128,2176]{1,0:T(8,128)(2,1)S(1)} %pad_maximum_fusion.refs_0_), channel_id=1, source_target_pairs={{0,1},{1,2},{2,3},{3,0},{4,5},{5,6},{6,7},{7,4},{8,9},{9,10},{10,1... | collective-permute-start | bytes 1671176 | tf_op jit(solution)/shard_map/gather_scaled/ppermute | solution.py:29
  73.1 16.7 %collective-permute-start.16 = (bf16[128,2176]{1,0:T(8,128)(2,1)S(1)}, bf16[128,2176]{1,0:T(8,128)(2,1)S(1)}, u32[]{:S(2)}, u32[]{:S(2)}) collective-permute-start(bf16[128,2176]{1,0:T(8,128)(2,1)S(1)} %pad_maximum_fusion.refs_0_), channel_id=1, source_target_pairs={{0,2},{1,3},{2,0},{3,1},{4,6},{5,7},{6,4},{7,5},{8,10},{9,11},{10,... | collective-permute-start | bytes 1671176 | tf_op jit(solution)/shard_map/gather_scaled/ppermute | solution.py:29
  75.2 15.5 %collective-permute-start.17 = (bf16[128,2176]{1,0:T(8,128)(2,1)S(1)}, bf16[128,2176]{1,0:T(8,128)(2,1)S(1)}, u32[]{:S(2)}, u32[]{:S(2)}) collective-permute-start(bf16[128,2176]{1,0:T(8,128)(2,1)S(1)} %pad_maximum_fusion.refs_0_), channel_id=1, source_target_pairs={{0,3},{1,0},{2,1},{3,2},{4,7},{5,4},{6,5},{7,6},{8,11},{9,8},{10,9... | collective-permute-start | bytes 1671176 | tf_op jit(solution)/shard_map/gather_scaled/ppermute | solution.py:29
  76.3 14.5 %slice-start = ((s8[6815744]{0:T(1024)(128)(4,1)}), s8[4194304]{0:T(1024)(128)(4,1)S(1)}, s32[]{:S(2)}) async-start(s8[6815744]{0:T(1024)(128)(4,1)} %bitcast.18), calls=%async_computation | async-start | bytes 8388608
  80.6 10.3 %slice-start.1 = ((s8[6815744]{0:T(1024)(128)(4,1)}), s8[2621440]{0:T(1024)(128)(4,1)S(1)}, s32[]{:S(2)}) async-start(s8[6815744]{0:T(1024)(128)(4,1)} %bitcast.18), calls=%async_computation.1 | async-start | bytes 5242880
  94.2 4.3 %collective-permute-start.19 = (bf16[256,1664]{1,0:T(8,128)(2,1)S(1)}, bf16[256,1664]{1,0:T(8,128)(2,1)S(1)}, u32[]{:S(2)}, u32[]{:S(2)}) collective-permute-start(bf16[256,1664]{1,0:T(8,128)(2,1)S(1)} %gate_up.6), channel_id=1, source_target_pairs={{0,16},{1,17},{2,18},{3,19},{4,20},{5,21},{6,22},{7,23},{8,24},{9,... | collective-permute-start | bytes 2555912 | tf_op jit(solution)/shard_map/gate_up/ppermute | solution.py:29
  94.4 6.0 %collective-permute-start.20 = (bf16[256,1664]{1,0:T(8,128)(2,1)S(1)}, bf16[256,1664]{1,0:T(8,128)(2,1)S(1)}, u32[]{:S(2)}, u32[]{:S(2)}) collective-permute-start(bf16[256,1664]{1,0:T(8,128)(2,1)S(1)} %gate_up.7), channel_id=1, source_target_pairs={{0,16},{1,17},{2,18},{3,19},{4,20},{5,21},{6,22},{7,23},{8,24},{9,... | collective-permute-start | bytes 2555912 | tf_op jit(solution)/shard_map/gate_up/ppermute | solution.py:29
  94.9 3.0 %collective-permute-start.18 = (bf16[256,128]{1,0:T(8,128)(2,1)S(1)}, bf16[256,128]{1,0:T(8,128)(2,1)S(1)}, u32[]{:S(2)}, u32[]{:S(2)}) collective-permute-start(bf16[256,128]{1,0:T(8,128)(2,1)S(1)} %get-tuple-element.25), channel_id=1, source_target_pairs={{0,16},{1,17},{2,18},{3,19},{4,20},{5,21},{6,22},{7,23},{8,24},{9,... | collective-permute-start | bytes 196616 | tf_op jit(solution)/shard_map/gate_up/ppermute | solution.py:29
  96.6 41.4 %slice-start.4 = ((s8[6815744]{0:T(1024)(128)(4,1)}), s8[4194304]{0:T(1024)(128)(4,1)S(1)}, s32[]{:S(2)}) async-start(s8[6815744]{0:T(1024)(128)(4,1)} %bitcast.22), calls=%async_computation.4 | async-start | bytes 8388608
  98.5 39.5 %slice-start.5 = ((s8[6815744]{0:T(1024)(128)(4,1)}), s8[2621440]{0:T(1024)(128)(4,1)S(1)}, s32[]{:S(2)}) async-start(s8[6815744]{0:T(1024)(128)(4,1)} %bitcast.22), calls=%async_computation.5 | async-start | bytes 5242880
  100.5 14.8 %collective-permute-start.22 = (bf16[64,3456]{1,0:T(8,128)(2,1)S(1)}, bf16[64,3456]{1,0:T(8,128)(2,1)S(1)}, u32[]{:S(2)}, u32[]{:S(2)}) collective-permute-start(bf16[64,3456]{1,0:T(8,128)(2,1)S(1)} %pad_maximum_fusion.3), channel_id=1, source_target_pairs={{0,96},{1,97},{2,98},{3,99},{4,100},{5,101},{6,102},{7,103},{8,104... | collective-permute-start | bytes 1327112 | tf_op jit(solution)/shard_map/sum_terms/ppermute | solution.py:29
  104.8 12.0 %collective-permute-start.21 = (bf16[64,3456]{1,0:T(8,128)(2,1)S(1)}, bf16[64,3456]{1,0:T(8,128)(2,1)S(1)}, u32[]{:S(2)}, u32[]{:S(2)}) collective-permute-start(bf16[64,3456]{1,0:T(8,128)(2,1)S(1)} %pad_maximum_fusion.2), channel_id=1, source_target_pairs={{0,32},{1,33},{2,34},{3,35},{4,36},{5,37},{6,38},{7,39},{8,40},{9,... | collective-permute-start | bytes 1327112 | tf_op jit(solution)/shard_map/sum_terms/ppermute | solution.py:29
  117.4 6.4 %collective-permute-start.24 = (bf16[32,3456]{1,0:T(8,128)(2,1)S(1)}, bf16[32,3456]{1,0:T(8,128)(2,1)S(1)}, u32[]{:S(2)}, u32[]{:S(2)}) collective-permute-start(bf16[32,3456]{1,0:T(8,128)(2,1)S(1)} %pad_maximum_fusion.5), channel_id=1, source_target_pairs={{0,32},{1,33},{2,34},{3,35},{4,36},{5,37},{6,38},{7,39},{8,40},{9,... | collective-permute-start | bytes 663560 | tf_op jit(solution)/shard_map/sum_terms/ppermute | solution.py:29
  117.8 7.7 %collective-permute-start.23 = (bf16[32,3456]{1,0:T(8,128)(2,1)S(1)}, bf16[32,3456]{1,0:T(8,128)(2,1)S(1)}, u32[]{:S(2)}, u32[]{:S(2)}) collective-permute-start(bf16[32,3456]{1,0:T(8,128)(2,1)S(1)} %pad_maximum_fusion.4), channel_id=1, source_target_pairs={{0,96},{1,97},{2,98},{3,99},{4,100},{5,101},{6,102},{7,103},{8,104... | collective-permute-start | bytes 663560 | tf_op jit(solution)/shard_map/sum_terms/ppermute | solution.py:29
  126.2 11.2 %collective-permute-start.26 = (bf16[64,1664]{1,0:T(8,128)(2,1)S(1)}, bf16[64,1664]{1,0:T(8,128)(2,1)S(1)}, u32[]{:S(2)}, u32[]{:S(2)}) collective-permute-start(bf16[64,1664]{1,0:T(8,128)(2,1)S(1)} %fusion.3), channel_id=1, source_target_pairs={{0,32},{1,33},{2,34},{3,35},{4,36},{5,37},{6,38},{7,39},{8,40},{9,... | collective-permute-start | bytes 638984 | tf_op jit(solution)/shard_map/gather_hidden/ppermute | solution.py:29
  126.5 10.9 %collective-permute-start.28 = (bf16[64,1664]{1,0:T(8,128)(2,1)S(1)}, bf16[64,1664]{1,0:T(8,128)(2,1)S(1)}, u32[]{:S(2)}, u32[]{:S(2)}) collective-permute-start(bf16[64,1664]{1,0:T(8,128)(2,1)S(1)} %fusion.3), channel_id=1, source_target_pairs={{0,64},{1,65},{2,66},{3,67},{4,68},{5,69},{6,70},{7,71},{8,72},{9,... | collective-permute-start | bytes 638984 | tf_op jit(solution)/shard_map/gather_hidden/ppermute | solution.py:29
  129.2 8.8 %collective-permute-start.30 = (bf16[64,1664]{1,0:T(8,128)(2,1)S(1)}, bf16[64,1664]{1,0:T(8,128)(2,1)S(1)}, u32[]{:S(2)}, u32[]{:S(2)}) collective-permute-start(bf16[64,1664]{1,0:T(8,128)(2,1)S(1)} %fusion.3), channel_id=1, source_target_pairs={{0,96},{1,97},{2,98},{3,99},{4,100},{5,101},{6,102},{7,103},{8,104... | collective-permute-start | bytes 638984 | tf_op jit(solution)/shard_map/gather_hidden/ppermute | solution.py:29
  130.3 7.7 %collective-permute-start.25 = (bf16[64,1664]{1,0:T(8,128)(2,1)S(1)}, bf16[64,1664]{1,0:T(8,128)(2,1)S(1)}, u32[]{:S(2)}, u32[]{:S(2)}) collective-permute-start(bf16[64,1664]{1,0:T(8,128)(2,1)S(1)} %fusion.3), channel_id=1, source_target_pairs={{0,16},{1,17},{2,18},{3,19},{4,20},{5,21},{6,22},{7,23},{8,24},{9,... | collective-permute-start | bytes 638984 | tf_op jit(solution)/shard_map/gather_hidden/ppermute | solution.py:29
  137.4 1.9 %collective-permute-start.27 = (bf16[64,1664]{1,0:T(8,128)(2,1)S(1)}, bf16[64,1664]{1,0:T(8,128)(2,1)S(1)}, u32[]{:S(2)}, u32[]{:S(2)}) collective-permute-start(bf16[64,1664]{1,0:T(8,128)(2,1)S(1)} %collective-permute-done.26), channel_id=1, source_target_pairs={{0,16},{1,17},{2,18},{3,19},{4,20},{5,21},{6,22},{7,23},{8,24},{9,... | collective-permute-start | bytes 638984 | tf_op jit(solution)/shard_map/down/ppermute | solution.py:29
  137.4 1.9 %collective-permute-start.29 = (bf16[64,1664]{1,0:T(8,128)(2,1)S(1)}, bf16[64,1664]{1,0:T(8,128)(2,1)S(1)}, u32[]{:S(2)}, u32[]{:S(2)}) collective-permute-start(bf16[64,1664]{1,0:T(8,128)(2,1)S(1)} %collective-permute-done.28), channel_id=1, source_target_pairs={{0,16},{1,17},{2,18},{3,19},{4,20},{5,21},{6,22},{7,23},{8,24},{9,... | collective-permute-start | bytes 638984 | tf_op jit(solution)/shard_map/down/ppermute | solution.py:29
  138.0 1.5 collective-permute-start.31
  142.8 12.0 %collective-permute-start.32 = (bf16[96,2048]{1,0:T(8,128)(2,1)S(1)}, bf16[96,2048]{1,0:T(8,128)(2,1)S(1)}, u32[]{:S(2)}, u32[]{:S(2)}) collective-permute-start(bf16[96,2048]{1,0:T(8,128)(2,1)S(1)} %get-tuple-element.59), channel_id=1, source_target_pairs={{0,3},{1,0},{2,1},{3,2},{4,7},{5,4},{6,5},{7,6},{8,11},{9,8},{10,9... | collective-permute-start | bytes 1179656 | tf_op jit(solution)/shard_map/sum_down/ppermute | solution.py:29
  145.2 14.7 %collective-permute-start.36 = (bf16[96,2048]{1,0:T(8,128)(2,1)S(1)}, bf16[96,2048]{1,0:T(8,128)(2,1)S(1)}, u32[]{:S(2)}, u32[]{:S(2)}) collective-permute-start(bf16[96,2048]{1,0:T(8,128)(2,1)S(1)} %get-tuple-element.61), channel_id=1, source_target_pairs={{0,2},{1,3},{2,0},{3,1},{4,6},{5,7},{6,4},{7,5},{8,10},{9,11},{10,... | collective-permute-start | bytes 1179656 | tf_op jit(solution)/shard_map/sum_down/ppermute | solution.py:29
  145.2 14.7 %collective-permute-start.37 = (bf16[96,2048]{1,0:T(8,128)(2,1)S(1)}, bf16[96,2048]{1,0:T(8,128)(2,1)S(1)}, u32[]{:S(2)}, u32[]{:S(2)}) collective-permute-start(bf16[96,2048]{1,0:T(8,128)(2,1)S(1)} %get-tuple-element.60), channel_id=1, source_target_pairs={{0,1},{1,2},{2,3},{3,0},{4,5},{5,6},{6,7},{7,4},{8,9},{9,10},{10,1... | collective-permute-start | bytes 1179656 | tf_op jit(solution)/shard_map/sum_down/ppermute | solution.py:29
  154.8 7.5 %collective-permute-start.33 = (bf16[32,2048]{1,0:T(8,128)(2,1)S(1)}, bf16[32,2048]{1,0:T(8,128)(2,1)S(1)}, u32[]{:S(2)}, u32[]{:S(2)}) collective-permute-start(bf16[32,2048]{1,0:T(8,128)(2,1)S(1)} %get-tuple-element.34), channel_id=1, source_target_pairs={{0,3},{1,0},{2,1},{3,2},{4,7},{5,4},{6,5},{7,6},{8,11},{9,8},{10,9... | collective-permute-start | bytes 393224 | tf_op jit(solution)/shard_map/sum_down/ppermute | solution.py:29
  158.4 9.9 %collective-permute-start.34 = (bf16[32,2048]{1,0:T(8,128)(2,1)S(1)}, bf16[32,2048]{1,0:T(8,128)(2,1)S(1)}, u32[]{:S(2)}, u32[]{:S(2)}) collective-permute-start(bf16[32,2048]{1,0:T(8,128)(2,1)S(1)} %get-tuple-element.35), channel_id=1, source_target_pairs={{0,1},{1,2},{2,3},{3,0},{4,5},{5,6},{6,7},{7,4},{8,9},{9,10},{10,1... | collective-permute-start | bytes 393224 | tf_op jit(solution)/shard_map/sum_down/ppermute | solution.py:29
  158.4 9.9 %collective-permute-start.35 = (bf16[32,2048]{1,0:T(8,128)(2,1)S(1)}, bf16[32,2048]{1,0:T(8,128)(2,1)S(1)}, u32[]{:S(2)}, u32[]{:S(2)}) collective-permute-start(bf16[32,2048]{1,0:T(8,128)(2,1)S(1)} %get-tuple-element.36), channel_id=1, source_target_pairs={{0,2},{1,3},{2,0},{3,1},{4,6},{5,7},{6,4},{7,5},{8,10},{9,11},{10,... | collective-permute-start | bytes 393224 | tf_op jit(solution)/shard_map/sum_down/ppermute | solution.py:29
  160.1 8.2 %collective-permute-start.38 = (bf16[32,2048]{1,0:T(8,128)(2,1)S(1)}, bf16[32,2048]{1,0:T(8,128)(2,1)S(1)}, u32[]{:S(2)}, u32[]{:S(2)}) collective-permute-start(bf16[32,2048]{1,0:T(8,128)(2,1)S(1)} %get-tuple-element.53), channel_id=1, source_target_pairs={{0,12},{1,13},{2,14},{3,15},{4,0},{5,1},{6,2},{7,3},{8,4},{9,5},{1... | collective-permute-start | bytes 393224 | tf_op jit(solution)/shard_map/sum_down/ppermute | solution.py:29
  161.4 7.6 %collective-permute-start.39 = (bf16[32,2048]{1,0:T(8,128)(2,1)S(1)}, bf16[32,2048]{1,0:T(8,128)(2,1)S(1)}, u32[]{:S(2)}, u32[]{:S(2)}) collective-permute-start(bf16[32,2048]{1,0:T(8,128)(2,1)S(1)} %get-tuple-element.55), channel_id=1, source_target_pairs={{0,4},{1,5},{2,6},{3,7},{4,8},{5,9},{6,10},{7,11},{8,12},{9,13},{1... | collective-permute-start | bytes 393224 | tf_op jit(solution)/shard_map/sum_down/ppermute | solution.py:29
  162.2 6.7 %collective-permute-start.40 = (bf16[32,2048]{1,0:T(8,128)(2,1)S(1)}, bf16[32,2048]{1,0:T(8,128)(2,1)S(1)}, u32[]{:S(2)}, u32[]{:S(2)}) collective-permute-start(bf16[32,2048]{1,0:T(8,128)(2,1)S(1)} %get-tuple-element.54), channel_id=1, source_target_pairs={{0,8},{1,9},{2,10},{3,11},{4,12},{5,13},{6,14},{7,15},{8,0},{9,1},... | collective-permute-start | bytes 393224 | tf_op jit(solution)/shard_map/sum_down/ppermute | solution.py:29
  (2 other events, 13.9 us)

commit v3 on v2

--- a/solution.py
+++ b/solution.py
@@ -10,6 +10,7 @@
 D = 16384
 HEAD_SIZE = 128
 ATTEND_VMEM = 62 << 20
+EARLY = 2
 AXES = ("attn", "ffn")
 BF16 = jnp.bfloat16
 F32 = jnp.float32
@@ -64,21 +65,39 @@
     return lax.optimization_barrier((value, *others))[0]
 
 
+def stack_kernel(*refs):
+    rows = refs[0].shape[0]
+    for n, ref in enumerate(refs[:-1]):
+        refs[-1][n * rows : (n + 1) * rows, :] = ref[...]
+
+
+def stack(blocks):
+    rows, width = blocks[0].shape
+    return pl.pallas_call(
+        stack_kernel,
+        out_shape=jax.ShapeDtypeStruct((len(blocks) * rows, width), blocks[0].dtype),
+        **COPY,
+    )(*blocks)
+
+
 def gather_rows(block):
     near = {i: along_first(block, i) for i in (1, 3, 2)}
-    chunk = jnp.concatenate([block, near[1], near[2], near[3]], axis=0)
+    chunk = stack([block, near[1], near[2], near[3]])
     far = {j: along_second(chunk, j) for j in (1, 3, 2)}
     return [chunk, far[1], far[2], far[3]]
 
 
-def offsets_of(projected, x, y, z, core, half, low, j):
-    which = (core ^ half) * 2 + low
-    delta = (x - z - which) & 3 if projected else which
-    i = jnp.where(core == 0, j + delta, j - delta) & 3
-    x_off = jnp.where(core == 0, i, j)
-    if projected:
-        return i, ((x - x_off - y) & 3) * 2 + (low ^ (z & 1))
-    return i, low * 4 + (-(x_off ^ y) & 3)
+def offsets_of(projected, x, y, z, core, half, turn, j):
+    which = core ^ half
+    if not projected:
+        which = which * 2 + turn
+        i = jnp.where(core == 0, j + which, j - which) & 3
+        x_off = jnp.where(core == 0, i, j)
+        return i, turn * 4 + (-(x_off ^ y) & 3)
+    inner = 1 if j in (1, 2) else 0
+    i = jnp.where(core == 0, (which ^ inner) + 2 * turn, (3 + 2 * (which ^ (j & 1)) + turn) & 3)
+    x_off, z_off = jnp.where(core == 0, i, j), jnp.where(core == 0, j, i)
+    return i, ((x + 2 + x_off - y) & 3) * 2 + 1 - (z_off & 1)
 
 
 COPY = dict(
@@ -92,12 +111,12 @@
     rows = chunks[0].shape[0] // 4
     place = my_place()
     for half in range(2):
-        for j in range(4):
-            for low in range(2):
-                i, spot = offsets_of(projected, *place, half, low, j)
+        for j in range(0 if extra else EARLY, 4):
+            for turn in range(2):
+                i, spot = offsets_of(projected, *place, half, turn, j)
                 block = chunks[j].at[pl.ds(pl.multiple_of(i * rows, rows), rows), :]
-                if j:
-                    at = ((j - 1) * 2 + low) * rows
+                if j >= EARLY:
+                    at = ((j - EARLY) * 2 + turn) * rows
                     rest[half][at : at + rows, :] = block[:, :width]
                 if extra:
                     start = pl.multiple_of(spot * rows, rows)
@@ -107,7 +126,7 @@
 def split(chunks, projected, width):
     rows, extra = chunks[0].shape[0] // 4, chunks[0].shape[1] - width
     kind = chunks[0].dtype
-    shapes = [jax.ShapeDtypeStruct((6 * rows, width), kind)] * 2
+    shapes = [jax.ShapeDtypeStruct(((4 - EARLY) * 2 * rows, width), kind)] * 2
     if extra:
         shapes += [jax.ShapeDtypeStruct((8 * rows, extra), kind)] * 2
     return pl.pallas_call(
@@ -117,33 +136,41 @@
     )(*chunks)
 
 
-def place_kernel(projected, half, first, rest, out):
-    rows = first.shape[0] // 4
+def place_kernel(projected, half, *refs):
+    early, rest, out = refs[:EARLY], refs[EARLY], refs[EARLY + 1]
+    rows = out.shape[0] // 8
     place = my_place()
     for j in range(4):
-        for low in range(2):
-            i, spot = offsets_of(projected, *place, half, low, j)
+        for turn in range(2):
+            i, spot = offsets_of(projected, *place, half, turn, j)
             start = pl.multiple_of(spot * rows, rows)
-            at = ((j - 1) * 2 + low) * rows
-            if j:
+            if j < EARLY:
+                out[pl.ds(start, rows), :] = early[j][pl.ds(pl.multiple_of(i * rows, rows), rows), :]
+            else:
+                at = ((j - EARLY) * 2 + turn) * rows
                 out[pl.ds(start, rows), :] = rest[at : at + rows, :]
-            else:
-                out[pl.ds(start, rows), :] = first[pl.ds(pl.multiple_of(i * rows, rows), rows), :]
-
-
-def in_place(first, rest, projected, half):
-    rows, width = first.shape[0] // 4, first.shape[1]
+
+
+def in_place(early, rest, projected, half):
+    rows, width = early[0].shape[0] // 4, early[0].shape[1]
     return pl.pallas_call(
         functools.partial(place_kernel, projected, half),
-        out_shape=jax.ShapeDtypeStruct((8 * rows, width), first.dtype),
+        out_shape=jax.ShapeDtypeStruct((8 * rows, width), rest.dtype),
         **COPY,
-    )(first, rest)
+    )(*early, rest)
+
+
+def early_products(chunks, weights):
+    width = weights[0].shape[0]
+    found = [[dot(chunk[:, :width], w) for chunk in chunks[:EARLY]] for w in weights]
+    ready = [f[-1] for f in found]
+    return found, chunks[:EARLY] + [after(chunk, *ready) for chunk in chunks[EARLY:]]
 
 
 def products(chunks, weight, projected):
-    first = dot(chunks[0], weight)
+    (early,), chunks = early_products(chunks, [weight])
     own_rows, away_rows = split(chunks, projected, weight.shape[0])
-    return shares(first, own_rows, away_rows, weight, projected)
+    return shares(early, own_rows, away_rows, weight, projected)
 
 
 def shares(first, own_rows, away_rows, weight, projected):
@@ -219,7 +246,7 @@
     sources = (queries, new_key, key_cache, token_value, cached_value_rows)
     return pl.pallas_call(
         attend_kernel,
-        out_shape=jax.ShapeDtypeStruct(queries.shape, BF16),
+        out_shape=pltpu.VMEM(queries.shape, BF16),
         in_specs=[pl.BlockSpec(memory_space=pltpu.SMEM)]
         + [pl.BlockSpec(memory_space=pl.ANY)] * 5,
         out_specs=pl.BlockSpec(memory_space=pltpu.VMEM),
@@ -270,17 +297,17 @@
 def to_owners(summed):
     with jax.named_scope("to_owners"):
         rows = summed.shape[0] // 2
-        blocks = [
-            send(
-                summed[s * rows : (s + 1) * rows],
-                lambda x, y, z, core, s=s: (y, x, (y - core * 2 - (s ^ (z & 1))) & 3, z >> 1),
-            )
-            for s in range(2)
-        ]
-        x, _, z, _ = my_place()
-        odd = ((x - z) & 1) == 1
+
+        def first(x, y, z, core):
+            return 2 * x - y + 2, x, z + (-1 if core ^ ((y - x) & 1) else 1), z >> 1
+
+        def second(x, y, z, core):
+            return 2 * x - y + 2, x, z + (2 if core ^ ((y - x) & 1) else 0), z >> 1
+
+        blocks = [send(summed[:rows], first), send(summed[rows:], second)]
+        odd = (my_place()[2] & 1) == 1
         return jnp.concatenate(
-            [jnp.where(odd, blocks[1], blocks[0]), jnp.where(odd, blocks[0], blocks[1])], axis=1
+            [jnp.where(odd, blocks[0], blocks[1]), jnp.where(odd, blocks[1], blocks[0])], axis=1
         )
 
 
@@ -296,7 +323,7 @@
     width, cols = gate_weight.shape
     rows = chunks[0].shape[0] // 4
     with jax.named_scope("gate_up"):
-        first_gate, first_up = [dot(chunks[0][:, :width], w) for w in (gate_weight, up_weight)]
+        (first_gate, first_up), chunks = early_products(chunks, [gate_weight, up_weight])
         own_rows, away_rows, own_squares, away_squares = split(chunks, False, width)
         away_gate = in_place(first_gate, dot(away_rows, gate_weight), False, 1)
         away_up = in_place(first_up, dot(away_rows, up_weight), False, 1)
@@ -350,16 +377,13 @@
 def sum_down(down):
     with jax.named_scope("sum_down"):
         rows, chunk = down.shape[0] // 16, down.shape[0] // 4
-        far = {j: along_second(down[j * chunk + rows : (j + 1) * chunk], -j) for j in (1, 3, 2)}
-        near = []
-        for i in (1, 3, 2):
-            cut = slice((i - 1) * rows, i * rows)
-            total = add(down[i * rows : (i + 1) * rows], *[far[j][cut] for j in (1, 2, 3)])
-            near.append(along_first(total.astype(BF16), -i))
-        side = [
-            along_second(after(down[j * chunk : j * chunk + rows], far[1]), -j) for j in (1, 3, 2)
-        ]
-        return add(down[:rows], *side, *near)
+        far = [along_second(down[j * chunk : (j + 1) * chunk], -j) for j in (1, 3, 2)]
+
+        def total(i):
+            cut = slice(i * rows, (i + 1) * rows)
+            return add(down[cut], *[f[cut] for f in far])
+
+        return add(total(0), *[along_first(total(i).astype(BF16), -i) for i in (1, 3, 2)])
 
 
 def local(

time: 171 us -> 162 us (0.947)
  starting transfers between devices: 62.7 us -> 50.8 us
  waiting for transfers between devices: 75.5 us -> 80.2 us
    ppermute x41 -> x38, starting transfers between devices: 62.7 us -> 50.8 us  [send(): return lax.ppermute(value, AXES, pairs)]
    ppermute x41 -> x38, waiting for transfers between devices: 75.5 us -> 80.2 us  [send(): return lax.ppermute(value, AXES, pairs)]
    pallas_call x1 -> x3, Pallas kernels: 3.92 us -> 3.34 us  [the longest x1 3.26 us: attend(): pl.pallas_call(attend_kernel, out_shape=pltpu.VMEM(queries.shape, BF16),...]
    dot_general x11 -> x14, matrix products: 21.2 us -> 21.2 us  [dot(): return jnp.dot(left, right, preferred_element_type=F32).astype(BF16)]
  transfers between devices with their start and end apart: 41 -> 38, of which waited for: 25 -> 27; matrix products, arithmetic and copies ran while one was open for 9% -> 10% of each run, Pallas kernels for 0% -> 0%
where the time goes in v3:
time: 162 us
  waiting for transfers between devices  80.2 us (50%)
  starting transfers between devices  50.8 us (31%)
  matrix products  21.2 us (13%)
  Pallas kernels  4.16 us (3%)
  other arithmetic  3.72 us (2%)
    ppermute x38, waiting for transfers between devices, send(): return lax.ppermute(value, AXES, pairs)  80.2 us
    ppermute x38, starting transfers between devices, send(): return lax.ppermute(value, AXES, pairs)  50.8 us
    dot_general x14, matrix products, dot(): return jnp.dot(left, right, preferred_element_type=F32).astype(BF16)  21.2 us
    pallas_call x1, Pallas kernels, attend(): pl.pallas_call(attend_kernel, out_shape=pltpu.VMEM(queries.shape, BF16),...  3.26 us
  transfers between devices with their start and end apart: 38, of which 27 were waited for; matrix products, arithmetic and copies ran while one was open for 10% of the time, Pallas kernels for 0%

profile of v3, /device:TPU:0, one launch (start us, length us, event | category | flops | bytes accessed | tf_op | source)
XLA Modules:
  0.0 162.0 jit_solution(15999155809966607285)
XLA Ops:
  0.0 3.3 %attention.1.refs_0_ = bf16[32,2048]{1,0:T(8,128)(2,1)S(1)} custom-call(s32[32]{0:T(128)} %lengths.1, bf16[32,2048]{1,0:T(8,128)(2,1)} %refs_0_.1, bf16[32,128]{1,0:T(8,128)(2,1)} %refs_1_.1, bf16[32,128,128]{2,1,0:T(8,128)(2,1)} %refs_2_.1, bf16[32,128]{1,0:T(8,128)(2,1)} %refs_3_.1, bf16[32,128,128]{2,1,0:T(8,128)(2,1)} %refs_4_.1), custom_call_target="tpu_custom_call" | custom-call | tf_op jit(solution)/shard_map/attention/pallas_call | solution.py:247
  3.3 1.6 %collective-permute-start = (bf16[32,2048]{1,0:T(8,128)(2,1)S(1)}, bf16[32,2048]{1,0:T(8,128)(2,1)S(1)}, u32[]{:S(2)}, u32[]{:S(2)}) collective-permute-start(bf16[32,2048]{1,0:T(8,128)(2,1)S(1)} %attention.1.refs_0_), channel_id=1, source_target_pairs={{0,4},{1,5},{2,6},{3,7},{4,8},{5,9},{6,10},{7,11},{8,12},{9,13},{1... | collective-permute-start | bytes 393224 | tf_op jit(solution)/shard_map/gather_attended/ppermute | solution.py:30
  4.9 2.7 %collective-permute-start.1 = (bf16[32,2048]{1,0:T(8,128)(2,1)S(1)}, bf16[32,2048]{1,0:T(8,128)(2,1)S(1)}, u32[]{:S(2)}, u32[]{:S(2)}) collective-permute-start(bf16[32,2048]{1,0:T(8,128)(2,1)S(1)} %attention.1.refs_0_), channel_id=1, source_target_pairs={{0,8},{1,9},{2,10},{3,11},{4,12},{5,13},{6,14},{7,15},{8,0},{9,1},... | collective-permute-start | bytes 393224 | tf_op jit(solution)/shard_map/gather_attended/ppermute | solution.py:30
  7.7 1.4 collective-permute-start.2
  9.5 2.5 %collective-permute-done.1.refs_2_ = bf16[32,2048]{1,0:T(8,128)(2,1)S(1)} collective-permute-done((bf16[32,2048]{1,0:T(8,128)(2,1)S(1)}, bf16[32,2048]{1,0:T(8,128)(2,1)S(1)}, u32[]{:S(2)}, u32[]{:S(2)}) %collective-permute-start.1) | collective-permute-done | bytes 131104 | tf_op jit(solution)/shard_map/gather_attended/ppermute | solution.py:30
  12.7 2.0 %collective-permute-start.3 = (bf16[128,2048]{1,0:T(8,128)(2,1)S(1)}, bf16[128,2048]{1,0:T(8,128)(2,1)S(1)}, u32[]{:S(2)}, u32[]{:S(2)}) collective-permute-start(bf16[128,2048]{1,0:T(8,128)(2,1)S(1)} %gather_attended.1.refs_0_), channel_id=1, source_target_pairs={{0,1},{1,2},{2,3},{3,0},{4,5},{5,6},{6,7},{7,4},{8,9},{9,10},{10,1... | collective-permute-start | bytes 1572872 | tf_op jit(solution)/shard_map/gather_attended/ppermute | solution.py:30
  14.7 2.2 %collective-permute-start.5 = (bf16[128,2048]{1,0:T(8,128)(2,1)S(1)}, bf16[128,2048]{1,0:T(8,128)(2,1)S(1)}, u32[]{:S(2)}, u32[]{:S(2)}) collective-permute-start(bf16[128,2048]{1,0:T(8,128)(2,1)S(1)} %gather_attended.1.refs_0_), channel_id=1, source_target_pairs={{0,3},{1,0},{2,1},{3,2},{4,7},{5,4},{6,5},{7,6},{8,11},{9,8},{10,9... | collective-permute-start | bytes 1572872 | tf_op jit(solution)/shard_map/gather_attended/ppermute | solution.py:30
  16.9 1.8 %collective-permute-start.4 = (bf16[128,2048]{1,0:T(8,128)(2,1)S(1)}, bf16[128,2048]{1,0:T(8,128)(2,1)S(1)}, u32[]{:S(2)}, u32[]{:S(2)}) collective-permute-start(bf16[128,2048]{1,0:T(8,128)(2,1)S(1)} %gather_attended.1.refs_0_), channel_id=1, source_target_pairs={{0,2},{1,3},{2,0},{3,1},{4,6},{5,7},{6,4},{7,5},{8,10},{9,11},{10,... | collective-permute-start | bytes 1572872 | tf_op jit(solution)/shard_map/gather_attended/ppermute | solution.py:30
  18.6 2.9 %convolution_convert_fusion.13.refs_0_ = bf16[128,1024]{1,0:T(8,128)(2,1)S(1)} fusion(bf16[128,2048]{1,0:T(8,128)(2,1)S(1)} %gather_attended.1.refs_0_, bf16[2048,1024]{1,0:T(8,128)(2,1)} %param.19), kind=kOutput, calls=%fused_computation.13 | convolution fusion | flops 537001984 | bytes 4980736 | tf_op jit(solution)/shard_map/projection/dot_general | solution.py:260
  21.6 2.3 %collective-permute-done.3.refs_1_ = bf16[128,2048]{1,0:T(8,128)(2,1)S(1)} collective-permute-done((bf16[128,2048]{1,0:T(8,128)(2,1)S(1)}, bf16[128,2048]{1,0:T(8,128)(2,1)S(1)}, u32[]{:S(2)}, u32[]{:S(2)}) %collective-permute-start.3) | collective-permute-done | bytes 524320 | tf_op jit(solution)/shard_map/gather_attended/ppermute | solution.py:30
  24.7 4.5 %collective-permute-done.5.refs_3_ = bf16[128,2048]{1,0:T(8,128)(2,1)S(1)} collective-permute-done((bf16[128,2048]{1,0:T(8,128)(2,1)S(1)}, bf16[128,2048]{1,0:T(8,128)(2,1)S(1)}, u32[]{:S(2)}, u32[]{:S(2)}) %collective-permute-start.5) | collective-permute-done | bytes 524320 | tf_op jit(solution)/shard_map/gather_attended/ppermute | solution.py:30
  29.2 1.8 %collective-permute-done.4.refs_2_ = bf16[128,2048]{1,0:T(8,128)(2,1)S(1)} collective-permute-done((bf16[128,2048]{1,0:T(8,128)(2,1)S(1)}, bf16[128,2048]{1,0:T(8,128)(2,1)S(1)}, u32[]{:S(2)}, u32[]{:S(2)}) %collective-permute-start.4) | collective-permute-done | bytes 524320 | tf_op jit(solution)/shard_map/gather_attended/ppermute | solution.py:30
  34.0 1.6 %collective-permute-start.7 = (bf16[64,1024]{1,0:T(8,128)(2,1)S(1)}, bf16[64,1024]{1,0:T(8,128)(2,1)S(1)}, u32[]{:S(2)}, u32[]{:S(2)}) collective-permute-start(bf16[64,1024]{1,0:T(8,128)(2,1)S(1)} %get-tuple-element.79), channel_id=1, source_target_pairs={{0,32},{1,33},{2,34},{3,35},{4,36},{5,37},{6,38},{7,39},{8,40},{9,... | collective-permute-start | bytes 393224 | tf_op jit(solution)/shard_map/sum_projected/ppermute | solution.py:30
  35.7 1.7 %collective-permute-start.8 = (bf16[64,1024]{1,0:T(8,128)(2,1)S(1)}, bf16[64,1024]{1,0:T(8,128)(2,1)S(1)}, u32[]{:S(2)}, u32[]{:S(2)}) collective-permute-start(bf16[64,1024]{1,0:T(8,128)(2,1)S(1)} %get-tuple-element.81), channel_id=1, source_target_pairs={{0,96},{1,97},{2,98},{3,99},{4,100},{5,101},{6,102},{7,103},{8,104... | collective-permute-start | bytes 393224 | tf_op jit(solution)/shard_map/sum_projected/ppermute | solution.py:30
  37.3 2.0 %collective-permute-start.9 = (bf16[64,1024]{1,0:T(8,128)(2,1)S(1)}, bf16[64,1024]{1,0:T(8,128)(2,1)S(1)}, u32[]{:S(2)}, u32[]{:S(2)}) collective-permute-start(bf16[64,1024]{1,0:T(8,128)(2,1)S(1)} %get-tuple-element.80), channel_id=1, source_target_pairs={{0,64},{1,65},{2,66},{3,67},{4,68},{5,69},{6,70},{7,71},{8,72},{9,... | collective-permute-start | bytes 393224 | tf_op jit(solution)/shard_map/sum_projected/ppermute | solution.py:30
  39.3 1.6 collective-permute-done.7
  40.9 2.2 %collective-permute-done.8 = bf16[64,1024]{1,0:T(8,128)(2,1)S(1)} collective-permute-done((bf16[64,1024]{1,0:T(8,128)(2,1)S(1)}, bf16[64,1024]{1,0:T(8,128)(2,1)S(1)}, u32[]{:S(2)}, u32[]{:S(2)}) %collective-permute-start.8) | collective-permute-done | bytes 131104 | tf_op jit(solution)/shard_map/sum_projected/ppermute | solution.py:30
  43.1 1.8 %collective-permute-done.9 = bf16[64,1024]{1,0:T(8,128)(2,1)S(1)} collective-permute-done((bf16[64,1024]{1,0:T(8,128)(2,1)S(1)}, bf16[64,1024]{1,0:T(8,128)(2,1)S(1)}, u32[]{:S(2)}, u32[]{:S(2)}) %collective-permute-start.9) | collective-permute-done | bytes 131104 | tf_op jit(solution)/shard_map/sum_projected/ppermute | solution.py:30
  45.0 3.3 %collective-permute-start.10 = (bf16[32,1024]{1,0:T(8,128)(2,1)S(1)}, bf16[32,1024]{1,0:T(8,128)(2,1)S(1)}, u32[]{:S(2)}, u32[]{:S(2)}) collective-permute-start(bf16[32,1024]{1,0:T(8,128)(2,1)S(1)} %get-tuple-element.88), channel_id=1, source_target_pairs={{0,9},{1,10},{2,27},{3,24},{4,35},{5,32},{6,49},{7,50},{8,73},{9,7... | collective-permute-start | bytes 196616 | tf_op jit(solution)/shard_map/to_owners/ppermute | solution.py:30
  49.2 2.4 %collective-permute-done.10 = bf16[32,1024]{1,0:T(8,128)(2,1)S(1)} collective-permute-done((bf16[32,1024]{1,0:T(8,128)(2,1)S(1)}, bf16[32,1024]{1,0:T(8,128)(2,1)S(1)}, u32[]{:S(2)}, u32[]{:S(2)}) %collective-permute-start.10) | collective-permute-done | bytes 65568 | tf_op jit(solution)/shard_map/to_owners/ppermute | solution.py:30
  51.6 2.8 %collective-permute-done.11 = bf16[32,1024]{1,0:T(8,128)(2,1)S(1)} collective-permute-done((bf16[32,1024]{1,0:T(8,128)(2,1)S(1)}, bf16[32,1024]{1,0:T(8,128)(2,1)S(1)}, u32[]{:S(2)}, u32[]{:S(2)}) %collective-permute-start.11) | collective-permute-done | bytes 65568 | tf_op jit(solution)/shard_map/to_owners/ppermute | solution.py:30
  54.8 5.5 %collective-permute-start.13 = (bf16[32,2176]{1,0:T(8,128)(2,1)S(1)}, bf16[32,2176]{1,0:T(8,128)(2,1)S(1)}, u32[]{:S(2)}, u32[]{:S(2)}) collective-permute-start(bf16[32,2176]{1,0:T(8,128)(2,1)S(1)} %pad_maximum_fusion.4.refs_0_), channel_id=1, source_target_pairs={{0,8},{1,9},{2,10},{3,11},{4,12},{5,13},{6,14},{7,15},{8,0},{9,1},... | collective-permute-start | bytes 417800 | tf_op jit(solution)/shard_map/gather_scaled/ppermute | solution.py:30
  60.3 1.6 collective-permute-done.12.refs_1_
  61.8 2.9 %collective-permute-done.13.refs_2_ = bf16[32,2176]{1,0:T(8,128)(2,1)S(1)} collective-permute-done((bf16[32,2176]{1,0:T(8,128)(2,1)S(1)}, bf16[32,2176]{1,0:T(8,128)(2,1)S(1)}, u32[]{:S(2)}, u32[]{:S(2)}) %collective-permute-start.13) | collective-permute-done | bytes 139296 | tf_op jit(solution)/shard_map/gather_scaled/ppermute | solution.py:30
  65.5 3.2 %collective-permute-start.17 = (bf16[128,2176]{1,0:T(8,128)(2,1)S(1)}, bf16[128,2176]{1,0:T(8,128)(2,1)S(1)}, u32[]{:S(2)}, u32[]{:S(2)}) collective-permute-start(bf16[128,2176]{1,0:T(8,128)(2,1)S(1)} %gather_scaled.1.refs_0_), channel_id=1, source_target_pairs={{0,3},{1,0},{2,1},{3,2},{4,7},{5,4},{6,5},{7,6},{8,11},{9,8},{10,9... | collective-permute-start | bytes 1671176 | tf_op jit(solution)/shard_map/gather_scaled/ppermute | solution.py:30
  68.7 3.1 %collective-permute-start.16 = (bf16[128,2176]{1,0:T(8,128)(2,1)S(1)}, bf16[128,2176]{1,0:T(8,128)(2,1)S(1)}, u32[]{:S(2)}, u32[]{:S(2)}) collective-permute-start(bf16[128,2176]{1,0:T(8,128)(2,1)S(1)} %gather_scaled.1.refs_0_), channel_id=1, source_target_pairs={{0,2},{1,3},{2,0},{3,1},{4,6},{5,7},{6,4},{7,5},{8,10},{9,11},{10,... | collective-permute-start | bytes 1671176 | tf_op jit(solution)/shard_map/gather_scaled/ppermute | solution.py:30
  71.8 4.1 %convolution_convert_fusion.7.refs_0_ = bf16[128,1664]{1,0:T(8,128)(2,1)S(1)} fusion(bf16[2048,1664]{1,0:T(8,128)(2,1)} %param.21, bf16[128,2176]{1,0:T(8,128)(2,1)S(1)} %gather_scaled.1.refs_0_), kind=kOutput, calls=%fused_computation.7 | convolution fusion | flops 872628224 | bytes 7766016 | tf_op jit(solution)/shard_map/gate_up/dot_general | solution.py:260
  77.1 1.1 convolution_convert_fusion.8.refs_1_
  80.3 3.0 %collective-permute-done.16.refs_2_ = bf16[128,2176]{1,0:T(8,128)(2,1)S(1)} collective-permute-done((bf16[128,2176]{1,0:T(8,128)(2,1)S(1)}, bf16[128,2176]{1,0:T(8,128)(2,1)S(1)}, u32[]{:S(2)}, u32[]{:S(2)}) %collective-permute-start.16) | collective-permute-done | bytes 557088 | tf_op jit(solution)/shard_map/gather_scaled/ppermute | solution.py:30
  83.4 1.1 convolution_convert_fusion.6.refs_2_
  84.5 1.1 convolution_convert_fusion.4.refs_2_
  87.8 1.7 %collective-permute-done.18 = bf16[256,128]{1,0:T(8,128)(2,1)S(1)} collective-permute-done((bf16[256,128]{1,0:T(8,128)(2,1)S(1)}, bf16[256,128]{1,0:T(8,128)(2,1)S(1)}, u32[]{:S(2)}, u32[]{:S(2)}) %collective-permute-start.18) | collective-permute-done | bytes 65568 | tf_op jit(solution)/shard_map/gate_up/ppermute | solution.py:30
  91.6 3.2 %collective-permute-start.22 = (bf16[64,3456]{1,0:T(8,128)(2,1)S(1)}, bf16[64,3456]{1,0:T(8,128)(2,1)S(1)}, u32[]{:S(2)}, u32[]{:S(2)}) collective-permute-start(bf16[64,3456]{1,0:T(8,128)(2,1)S(1)} %pad_maximum_fusion.1), channel_id=1, source_target_pairs={{0,96},{1,97},{2,98},{3,99},{4,100},{5,101},{6,102},{7,103},{8,104... | collective-permute-start | bytes 1327112 | tf_op jit(solution)/shard_map/sum_terms/ppermute | solution.py:30
  94.9 10.6 %collective-permute-done.22 = bf16[64,3456]{1,0:T(8,128)(2,1)S(1)} collective-permute-done((bf16[64,3456]{1,0:T(8,128)(2,1)S(1)}, bf16[64,3456]{1,0:T(8,128)(2,1)S(1)}, u32[]{:S(2)}, u32[]{:S(2)}) %collective-permute-start.22) | collective-permute-done | bytes 442400 | tf_op jit(solution)/shard_map/sum_terms/ppermute | solution.py:30
  105.5 1.6 collective-permute-done.21
  108.0 1.2 collective-permute-start.23
  109.2 5.1 %collective-permute-done.24 = bf16[32,3456]{1,0:T(8,128)(2,1)S(1)} collective-permute-done((bf16[32,3456]{1,0:T(8,128)(2,1)S(1)}, bf16[32,3456]{1,0:T(8,128)(2,1)S(1)}, u32[]{:S(2)}, u32[]{:S(2)}) %collective-permute-start.24) | collective-permute-done | bytes 221216 | tf_op jit(solution)/shard_map/sum_terms/ppermute | solution.py:30
  114.3 1.6 %collective-permute-done.23 = bf16[32,3456]{1,0:T(8,128)(2,1)S(1)} collective-permute-done((bf16[32,3456]{1,0:T(8,128)(2,1)S(1)}, bf16[32,3456]{1,0:T(8,128)(2,1)S(1)}, u32[]{:S(2)}, u32[]{:S(2)}) %collective-permute-start.23) | collective-permute-done | bytes 221216 | tf_op jit(solution)/shard_map/sum_terms/ppermute | solution.py:30
  117.2 2.6 %collective-permute-start.28 = (bf16[64,1664]{1,0:T(8,128)(2,1)S(1)}, bf16[64,1664]{1,0:T(8,128)(2,1)S(1)}, u32[]{:S(2)}, u32[]{:S(2)}) collective-permute-start(bf16[64,1664]{1,0:T(8,128)(2,1)S(1)} %fusion.5), channel_id=1, source_target_pairs={{0,64},{1,65},{2,66},{3,67},{4,68},{5,69},{6,70},{7,71},{8,72},{9,... | collective-permute-start | bytes 638984 | tf_op jit(solution)/shard_map/gather_hidden/ppermute | solution.py:30
  121.0 7.4 %collective-permute-done.26 = bf16[64,1664]{1,0:T(8,128)(2,1)S(1)} collective-permute-done((bf16[64,1664]{1,0:T(8,128)(2,1)S(1)}, bf16[64,1664]{1,0:T(8,128)(2,1)S(1)}, u32[]{:S(2)}, u32[]{:S(2)}) %collective-permute-start.26) | collective-permute-done | bytes 213024 | tf_op jit(solution)/shard_map/gather_hidden/ppermute | solution.py:30
  130.4 3.0 %convolution_convert_fusion.rest = bf16[384,2048]{1,0:T(8,128)(2,1)S(1)} fusion(bf16[384,1664]{1,0:T(8,128)(2,1)S(1)} %constant_dynamic-update-slice_fusion, bf16[1664,2048]{1,0:T(8,128)(2,1)S(1)} %bitcast.28), kind=kOutput, calls=%fused_computation | convolution fusion | flops 2618032128 | bytes 9666560 | tf_op jit(solution)/shard_map/down/dot_general | solution.py:260
  133.8 2.4 %collective-permute-start.32 = (bf16[128,2048]{1,0:T(8,128)(2,1)S(1)}, bf16[128,2048]{1,0:T(8,128)(2,1)S(1)}, u32[]{:S(2)}, u32[]{:S(2)}) collective-permute-start(bf16[128,2048]{1,0:T(8,128)(2,1)S(1)} %get-tuple-element.58), channel_id=1, source_target_pairs={{0,3},{1,0},{2,1},{3,2},{4,7},{5,4},{6,5},{7,6},{8,11},{9,8},{10,9... | collective-permute-start | bytes 1572872 | tf_op jit(solution)/shard_map/sum_down/ppermute | solution.py:30
  136.2 1.9 %collective-permute-start.34 = (bf16[128,2048]{1,0:T(8,128)(2,1)S(1)}, bf16[128,2048]{1,0:T(8,128)(2,1)S(1)}, u32[]{:S(2)}, u32[]{:S(2)}) collective-permute-start(bf16[128,2048]{1,0:T(8,128)(2,1)S(1)} %get-tuple-element.59), channel_id=1, source_target_pairs={{0,2},{1,3},{2,0},{3,1},{4,6},{5,7},{6,4},{7,5},{8,10},{9,11},{10,... | collective-permute-start | bytes 1572872 | tf_op jit(solution)/shard_map/sum_down/ppermute | solution.py:30
  138.1 10.4 %collective-permute-done.32 = bf16[128,2048]{1,0:T(8,128)(2,1)S(1)} collective-permute-done((bf16[128,2048]{1,0:T(8,128)(2,1)S(1)}, bf16[128,2048]{1,0:T(8,128)(2,1)S(1)}, u32[]{:S(2)}, u32[]{:S(2)}) %collective-permute-start.32) | collective-permute-done | bytes 524320 | tf_op jit(solution)/shard_map/sum_down/ppermute | solution.py:30
  148.5 3.7 %collective-permute-done.33 = bf16[128,2048]{1,0:T(8,128)(2,1)S(1)} collective-permute-done((bf16[128,2048]{1,0:T(8,128)(2,1)S(1)}, bf16[128,2048]{1,0:T(8,128)(2,1)S(1)}, u32[]{:S(2)}, u32[]{:S(2)}) %collective-permute-start.33) | collective-permute-done | bytes 524320 | tf_op jit(solution)/shard_map/sum_down/ppermute | solution.py:30
  152.5 1.2 collective-permute-start.35
  155.3 2.2 %collective-permute-done.35 = bf16[32,2048]{1,0:T(8,128)(2,1)S(1)} collective-permute-done((bf16[32,2048]{1,0:T(8,128)(2,1)S(1)}, bf16[32,2048]{1,0:T(8,128)(2,1)S(1)}, u32[]{:S(2)}, u32[]{:S(2)}) %collective-permute-start.35) | collective-permute-done | bytes 131104 | tf_op jit(solution)/shard_map/sum_down/ppermute | solution.py:30
  157.5 3.7 %collective-permute-done.36 = bf16[32,2048]{1,0:T(8,128)(2,1)S(1)} collective-permute-done((bf16[32,2048]{1,0:T(8,128)(2,1)S(1)}, bf16[32,2048]{1,0:T(8,128)(2,1)S(1)}, u32[]{:S(2)}, u32[]{:S(2)}) %collective-permute-start.36) | collective-permute-done | bytes 131104 | tf_op jit(solution)/shard_map/sum_down/ppermute | solution.py:30
  (120 shorter events, 22.8 us)
Async XLA Ops:
  3.3 20.7 %copy-start = (bf16[2048,1024]{1,0:T(8,128)(2,1)S(1)}, bf16[2048,1024]{1,0:T(8,128)(2,1)}, u32[]{:S(2)}) copy-start(bf16[2048,1024]{1,0:T(8,128)(2,1)} %param.19) | copy-start | bytes 12582916
  3.3 6.2 %collective-permute-start = (bf16[32,2048]{1,0:T(8,128)(2,1)S(1)}, bf16[32,2048]{1,0:T(8,128)(2,1)S(1)}, u32[]{:S(2)}, u32[]{:S(2)}) collective-permute-start(bf16[32,2048]{1,0:T(8,128)(2,1)S(1)} %attention.1.refs_0_), channel_id=1, source_target_pairs={{0,4},{1,5},{2,6},{3,7},{4,8},{5,9},{6,10},{7,11},{8,12},{9,13},{1... | collective-permute-start | bytes 393224 | tf_op jit(solution)/shard_map/gather_attended/ppermute | solution.py:30
  4.9 7.1 %collective-permute-start.1 = (bf16[32,2048]{1,0:T(8,128)(2,1)S(1)}, bf16[32,2048]{1,0:T(8,128)(2,1)S(1)}, u32[]{:S(2)}, u32[]{:S(2)}) collective-permute-start(bf16[32,2048]{1,0:T(8,128)(2,1)S(1)} %attention.1.refs_0_), channel_id=1, source_target_pairs={{0,8},{1,9},{2,10},{3,11},{4,12},{5,13},{6,14},{7,15},{8,0},{9,1},... | collective-permute-start | bytes 393224 | tf_op jit(solution)/shard_map/gather_attended/ppermute | solution.py:30
  7.7 5.0 %collective-permute-start.2 = (bf16[32,2048]{1,0:T(8,128)(2,1)S(1)}, bf16[32,2048]{1,0:T(8,128)(2,1)S(1)}, u32[]{:S(2)}, u32[]{:S(2)}) collective-permute-start(bf16[32,2048]{1,0:T(8,128)(2,1)S(1)} %attention.1.refs_0_), channel_id=1, source_target_pairs={{0,12},{1,13},{2,14},{3,15},{4,0},{5,1},{6,2},{7,3},{8,4},{9,5},{1... | collective-permute-start | bytes 393224 | tf_op jit(solution)/shard_map/gather_attended/ppermute | solution.py:30
  12.7 11.3 %collective-permute-start.3 = (bf16[128,2048]{1,0:T(8,128)(2,1)S(1)}, bf16[128,2048]{1,0:T(8,128)(2,1)S(1)}, u32[]{:S(2)}, u32[]{:S(2)}) collective-permute-start(bf16[128,2048]{1,0:T(8,128)(2,1)S(1)} %gather_attended.1.refs_0_), channel_id=1, source_target_pairs={{0,1},{1,2},{2,3},{3,0},{4,5},{5,6},{6,7},{7,4},{8,9},{9,10},{10,1... | collective-permute-start | bytes 1572872 | tf_op jit(solution)/shard_map/gather_attended/ppermute | solution.py:30
  14.7 14.6 %collective-permute-start.5 = (bf16[128,2048]{1,0:T(8,128)(2,1)S(1)}, bf16[128,2048]{1,0:T(8,128)(2,1)S(1)}, u32[]{:S(2)}, u32[]{:S(2)}) collective-permute-start(bf16[128,2048]{1,0:T(8,128)(2,1)S(1)} %gather_attended.1.refs_0_), channel_id=1, source_target_pairs={{0,3},{1,0},{2,1},{3,2},{4,7},{5,4},{6,5},{7,6},{8,11},{9,8},{10,9... | collective-permute-start | bytes 1572872 | tf_op jit(solution)/shard_map/gather_attended/ppermute | solution.py:30
  16.9 14.2 %collective-permute-start.4 = (bf16[128,2048]{1,0:T(8,128)(2,1)S(1)}, bf16[128,2048]{1,0:T(8,128)(2,1)S(1)}, u32[]{:S(2)}, u32[]{:S(2)}) collective-permute-start(bf16[128,2048]{1,0:T(8,128)(2,1)S(1)} %gather_attended.1.refs_0_), channel_id=1, source_target_pairs={{0,2},{1,3},{2,0},{3,1},{4,6},{5,7},{6,4},{7,5},{8,10},{9,11},{10,... | collective-permute-start | bytes 1572872 | tf_op jit(solution)/shard_map/gather_attended/ppermute | solution.py:30
  31.8 7.5 %copy-start.2 = (bf16[2048]{0:T(1024)(128)(2,1)S(1)}, bf16[2048]{0:T(1024)(128)(2,1)}, u32[]{:S(2)}) copy-start(bf16[2048]{0:T(1024)(128)(2,1)} %param.20) | copy-start | bytes 12292
  31.9 2.0 %collective-permute-start.6 = (bf16[256,1024]{1,0:T(8,128)(2,1)S(1)}, bf16[256,1024]{1,0:T(8,128)(2,1)S(1)}, u32[]{:S(2)}, u32[]{:S(2)}) collective-permute-start(bf16[256,1024]{1,0:T(8,128)(2,1)S(1)} %projection.4), channel_id=1, source_target_pairs={{0,16},{1,17},{2,18},{3,19},{4,20},{5,21},{6,22},{7,23},{8,24},{9,... | collective-permute-start | bytes 1572872 | tf_op jit(solution)/shard_map/projection/ppermute | solution.py:30
  32.0 22.4 %copy-start.1 = (f32[32,2048]{1,0:T(8,128)S(1)}, f32[32,2048]{1,0:T(8,128)}, u32[]{:S(2)}) copy-start(f32[32,2048]{1,0:T(8,128)} %param.18) | copy-start | bytes 786436
  34.0 6.9 %collective-permute-start.7 = (bf16[64,1024]{1,0:T(8,128)(2,1)S(1)}, bf16[64,1024]{1,0:T(8,128)(2,1)S(1)}, u32[]{:S(2)}, u32[]{:S(2)}) collective-permute-start(bf16[64,1024]{1,0:T(8,128)(2,1)S(1)} %get-tuple-element.79), channel_id=1, source_target_pairs={{0,32},{1,33},{2,34},{3,35},{4,36},{5,37},{6,38},{7,39},{8,40},{9,... | collective-permute-start | bytes 393224 | tf_op jit(solution)/shard_map/sum_projected/ppermute | solution.py:30
  35.7 7.4 %collective-permute-start.8 = (bf16[64,1024]{1,0:T(8,128)(2,1)S(1)}, bf16[64,1024]{1,0:T(8,128)(2,1)S(1)}, u32[]{:S(2)}, u32[]{:S(2)}) collective-permute-start(bf16[64,1024]{1,0:T(8,128)(2,1)S(1)} %get-tuple-element.81), channel_id=1, source_target_pairs={{0,96},{1,97},{2,98},{3,99},{4,100},{5,101},{6,102},{7,103},{8,104... | collective-permute-start | bytes 393224 | tf_op jit(solution)/shard_map/sum_projected/ppermute | solution.py:30
  37.3 7.6 %collective-permute-start.9 = (bf16[64,1024]{1,0:T(8,128)(2,1)S(1)}, bf16[64,1024]{1,0:T(8,128)(2,1)S(1)}, u32[]{:S(2)}, u32[]{:S(2)}) collective-permute-start(bf16[64,1024]{1,0:T(8,128)(2,1)S(1)} %get-tuple-element.80), channel_id=1, source_target_pairs={{0,64},{1,65},{2,66},{3,67},{4,68},{5,69},{6,70},{7,71},{8,72},{9,... | collective-permute-start | bytes 393224 | tf_op jit(solution)/shard_map/sum_projected/ppermute | solution.py:30
  45.0 6.6 %collective-permute-start.10 = (bf16[32,1024]{1,0:T(8,128)(2,1)S(1)}, bf16[32,1024]{1,0:T(8,128)(2,1)S(1)}, u32[]{:S(2)}, u32[]{:S(2)}) collective-permute-start(bf16[32,1024]{1,0:T(8,128)(2,1)S(1)} %get-tuple-element.88), channel_id=1, source_target_pairs={{0,9},{1,10},{2,27},{3,24},{4,35},{5,32},{6,49},{7,50},{8,73},{9,7... | collective-permute-start | bytes 196616 | tf_op jit(solution)/shard_map/to_owners/ppermute | solution.py:30
  48.3 6.2 %collective-permute-start.11 = (bf16[32,1024]{1,0:T(8,128)(2,1)S(1)}, bf16[32,1024]{1,0:T(8,128)(2,1)S(1)}, u32[]{:S(2)}, u32[]{:S(2)}) collective-permute-start(bf16[32,1024]{1,0:T(8,128)(2,1)S(1)} %get-tuple-element.89), channel_id=1, source_target_pairs={{0,8},{1,9},{2,26},{3,27},{4,34},{5,35},{6,48},{7,49},{8,72},{9,73... | collective-permute-start | bytes 196616 | tf_op jit(solution)/shard_map/to_owners/ppermute | solution.py:30
  54.7 7.1 %collective-permute-start.12 = (bf16[32,2176]{1,0:T(8,128)(2,1)S(1)}, bf16[32,2176]{1,0:T(8,128)(2,1)S(1)}, u32[]{:S(2)}, u32[]{:S(2)}) collective-permute-start(bf16[32,2176]{1,0:T(8,128)(2,1)S(1)} %pad_maximum_fusion.4.refs_0_), channel_id=1, source_target_pairs={{0,4},{1,5},{2,6},{3,7},{4,8},{5,9},{6,10},{7,11},{8,12},{9,13},{1... | collective-permute-start | bytes 417800 | tf_op jit(solution)/shard_map/gather_scaled/ppermute | solution.py:30
  54.8 10.0 %collective-permute-start.13 = (bf16[32,2176]{1,0:T(8,128)(2,1)S(1)}, bf16[32,2176]{1,0:T(8,128)(2,1)S(1)}, u32[]{:S(2)}, u32[]{:S(2)}) collective-permute-start(bf16[32,2176]{1,0:T(8,128)(2,1)S(1)} %pad_maximum_fusion.4.refs_0_), channel_id=1, source_target_pairs={{0,8},{1,9},{2,10},{3,11},{4,12},{5,13},{6,14},{7,15},{8,0},{9,1},... | collective-permute-start | bytes 417800 | tf_op jit(solution)/shard_map/gather_scaled/ppermute | solution.py:30
  60.3 5.1 %collective-permute-start.14 = (bf16[32,2176]{1,0:T(8,128)(2,1)S(1)}, bf16[32,2176]{1,0:T(8,128)(2,1)S(1)}, u32[]{:S(2)}, u32[]{:S(2)}) collective-permute-start(bf16[32,2176]{1,0:T(8,128)(2,1)S(1)} %pad_maximum_fusion.4.refs_0_), channel_id=1, source_target_pairs={{0,12},{1,13},{2,14},{3,15},{4,0},{5,1},{6,2},{7,3},{8,4},{9,5},{1... | collective-permute-start | bytes 417800 | tf_op jit(solution)/shard_map/gather_scaled/ppermute | solution.py:30
  65.3 10.6 %slice-start.2 = ((s8[6815744]{0:T(1024)(128)(4,1)}), s8[4194304]{0:T(1024)(128)(4,1)S(1)}, s32[]{:S(2)}) async-start(s8[6815744]{0:T(1024)(128)(4,1)} %bitcast.25), calls=%async_computation.2 | async-start | bytes 8388608
  65.4 10.5 %slice-start.3 = ((s8[6815744]{0:T(1024)(128)(4,1)}), s8[2621440]{0:T(1024)(128)(4,1)S(1)}, s32[]{:S(2)}) async-start(s8[6815744]{0:T(1024)(128)(4,1)} %bitcast.25), calls=%async_computation.3 | async-start | bytes 5242880
  65.4 11.7 %collective-permute-start.15 = (bf16[128,2176]{1,0:T(8,128)(2,1)S(1)}, bf16[128,2176]{1,0:T(8,128)(2,1)S(1)}, u32[]{:S(2)}, u32[]{:S(2)}) collective-permute-start(bf16[128,2176]{1,0:T(8,128)(2,1)S(1)} %gather_scaled.1.refs_0_), channel_id=1, source_target_pairs={{0,1},{1,2},{2,3},{3,0},{4,5},{5,6},{6,7},{7,4},{8,9},{9,10},{10,1... | collective-permute-start | bytes 1671176 | tf_op jit(solution)/shard_map/gather_scaled/ppermute | solution.py:30
  65.5 14.8 %collective-permute-start.17 = (bf16[128,2176]{1,0:T(8,128)(2,1)S(1)}, bf16[128,2176]{1,0:T(8,128)(2,1)S(1)}, u32[]{:S(2)}, u32[]{:S(2)}) collective-permute-start(bf16[128,2176]{1,0:T(8,128)(2,1)S(1)} %gather_scaled.1.refs_0_), channel_id=1, source_target_pairs={{0,3},{1,0},{2,1},{3,2},{4,7},{5,4},{6,5},{7,6},{8,11},{9,8},{10,9... | collective-permute-start | bytes 1671176 | tf_op jit(solution)/shard_map/gather_scaled/ppermute | solution.py:30
  68.7 14.6 %collective-permute-start.16 = (bf16[128,2176]{1,0:T(8,128)(2,1)S(1)}, bf16[128,2176]{1,0:T(8,128)(2,1)S(1)}, u32[]{:S(2)}, u32[]{:S(2)}) collective-permute-start(bf16[128,2176]{1,0:T(8,128)(2,1)S(1)} %gather_scaled.1.refs_0_), channel_id=1, source_target_pairs={{0,2},{1,3},{2,0},{3,1},{4,6},{5,7},{6,4},{7,5},{8,10},{9,11},{10,... | collective-permute-start | bytes 1671176 | tf_op jit(solution)/shard_map/gather_scaled/ppermute | solution.py:30
  75.9 2.3 %slice-start = ((s8[6815744]{0:T(1024)(128)(4,1)}), s8[4194304]{0:T(1024)(128)(4,1)S(1)}, s32[]{:S(2)}) async-start(s8[6815744]{0:T(1024)(128)(4,1)} %bitcast.23), calls=%async_computation | async-start | bytes 8388608
  77.1 2.1 %slice-start.1 = ((s8[6815744]{0:T(1024)(128)(4,1)}), s8[2621440]{0:T(1024)(128)(4,1)S(1)}, s32[]{:S(2)}) async-start(s8[6815744]{0:T(1024)(128)(4,1)} %bitcast.23), calls=%async_computation.1 | async-start | bytes 5242880
  85.7 4.3 %collective-permute-start.19 = (bf16[256,1664]{1,0:T(8,128)(2,1)S(1)}, bf16[256,1664]{1,0:T(8,128)(2,1)S(1)}, u32[]{:S(2)}, u32[]{:S(2)}) collective-permute-start(bf16[256,1664]{1,0:T(8,128)(2,1)S(1)} %gate_up.6), channel_id=1, source_target_pairs={{0,16},{1,17},{2,18},{3,19},{4,20},{5,21},{6,22},{7,23},{8,24},{9,... | collective-permute-start | bytes 2555912 | tf_op jit(solution)/shard_map/gate_up/ppermute | solution.py:30
  85.9 5.5 %collective-permute-start.20 = (bf16[256,1664]{1,0:T(8,128)(2,1)S(1)}, bf16[256,1664]{1,0:T(8,128)(2,1)S(1)}, u32[]{:S(2)}, u32[]{:S(2)}) collective-permute-start(bf16[256,1664]{1,0:T(8,128)(2,1)S(1)} %gate_up.7), channel_id=1, source_target_pairs={{0,16},{1,17},{2,18},{3,19},{4,20},{5,21},{6,22},{7,23},{8,24},{9,... | collective-permute-start | bytes 2555912 | tf_op jit(solution)/shard_map/gate_up/ppermute | solution.py:30
  86.5 3.0 %collective-permute-start.18 = (bf16[256,128]{1,0:T(8,128)(2,1)S(1)}, bf16[256,128]{1,0:T(8,128)(2,1)S(1)}, u32[]{:S(2)}, u32[]{:S(2)}) collective-permute-start(bf16[256,128]{1,0:T(8,128)(2,1)S(1)} %get-tuple-element.30), channel_id=1, source_target_pairs={{0,16},{1,17},{2,18},{3,19},{4,20},{5,21},{6,22},{7,23},{8,24},{9,... | collective-permute-start | bytes 196616 | tf_op jit(solution)/shard_map/gate_up/ppermute | solution.py:30
  89.9 39.0 %slice-start.4 = ((s8[6815744]{0:T(1024)(128)(4,1)}), s8[4194304]{0:T(1024)(128)(4,1)S(1)}, s32[]{:S(2)}) async-start(s8[6815744]{0:T(1024)(128)(4,1)} %bitcast.27), calls=%async_computation.4 | async-start | bytes 8388608
  90.1 38.9 %slice-start.5 = ((s8[6815744]{0:T(1024)(128)(4,1)}), s8[2621440]{0:T(1024)(128)(4,1)S(1)}, s32[]{:S(2)}) async-start(s8[6815744]{0:T(1024)(128)(4,1)} %bitcast.27), calls=%async_computation.5 | async-start | bytes 5242880
  91.6 13.9 %collective-permute-start.22 = (bf16[64,3456]{1,0:T(8,128)(2,1)S(1)}, bf16[64,3456]{1,0:T(8,128)(2,1)S(1)}, u32[]{:S(2)}, u32[]{:S(2)}) collective-permute-start(bf16[64,3456]{1,0:T(8,128)(2,1)S(1)} %pad_maximum_fusion.1), channel_id=1, source_target_pairs={{0,96},{1,97},{2,98},{3,99},{4,100},{5,101},{6,102},{7,103},{8,104... | collective-permute-start | bytes 1327112 | tf_op jit(solution)/shard_map/sum_terms/ppermute | solution.py:30
  94.8 12.2 %collective-permute-start.21 = (bf16[64,3456]{1,0:T(8,128)(2,1)S(1)}, bf16[64,3456]{1,0:T(8,128)(2,1)S(1)}, u32[]{:S(2)}, u32[]{:S(2)}) collective-permute-start(bf16[64,3456]{1,0:T(8,128)(2,1)S(1)} %pad_maximum_fusion), channel_id=1, source_target_pairs={{0,32},{1,33},{2,34},{3,35},{4,36},{5,37},{6,38},{7,39},{8,40},{9,... | collective-permute-start | bytes 1327112 | tf_op jit(solution)/shard_map/sum_terms/ppermute | solution.py:30
  107.6 6.7 %collective-permute-start.24 = (bf16[32,3456]{1,0:T(8,128)(2,1)S(1)}, bf16[32,3456]{1,0:T(8,128)(2,1)S(1)}, u32[]{:S(2)}, u32[]{:S(2)}) collective-permute-start(bf16[32,3456]{1,0:T(8,128)(2,1)S(1)} %pad_maximum_fusion.3), channel_id=1, source_target_pairs={{0,32},{1,33},{2,34},{3,35},{4,36},{5,37},{6,38},{7,39},{8,40},{9,... | collective-permute-start | bytes 663560 | tf_op jit(solution)/shard_map/sum_terms/ppermute | solution.py:30
  108.0 7.9 %collective-permute-start.23 = (bf16[32,3456]{1,0:T(8,128)(2,1)S(1)}, bf16[32,3456]{1,0:T(8,128)(2,1)S(1)}, u32[]{:S(2)}, u32[]{:S(2)}) collective-permute-start(bf16[32,3456]{1,0:T(8,128)(2,1)S(1)} %pad_maximum_fusion.2), channel_id=1, source_target_pairs={{0,96},{1,97},{2,98},{3,99},{4,100},{5,101},{6,102},{7,103},{8,104... | collective-permute-start | bytes 663560 | tf_op jit(solution)/shard_map/sum_terms/ppermute | solution.py:30
  116.7 11.7 %collective-permute-start.26 = (bf16[64,1664]{1,0:T(8,128)(2,1)S(1)}, bf16[64,1664]{1,0:T(8,128)(2,1)S(1)}, u32[]{:S(2)}, u32[]{:S(2)}) collective-permute-start(bf16[64,1664]{1,0:T(8,128)(2,1)S(1)} %fusion.5), channel_id=1, source_target_pairs={{0,32},{1,33},{2,34},{3,35},{4,36},{5,37},{6,38},{7,39},{8,40},{9,... | collective-permute-start | bytes 638984 | tf_op jit(solution)/shard_map/gather_hidden/ppermute | solution.py:30
  117.2 11.2 %collective-permute-start.28 = (bf16[64,1664]{1,0:T(8,128)(2,1)S(1)}, bf16[64,1664]{1,0:T(8,128)(2,1)S(1)}, u32[]{:S(2)}, u32[]{:S(2)}) collective-permute-start(bf16[64,1664]{1,0:T(8,128)(2,1)S(1)} %fusion.5), channel_id=1, source_target_pairs={{0,64},{1,65},{2,66},{3,67},{4,68},{5,69},{6,70},{7,71},{8,72},{9,... | collective-permute-start | bytes 638984 | tf_op jit(solution)/shard_map/gather_hidden/ppermute | solution.py:30
  119.8 9.1 %collective-permute-start.30 = (bf16[64,1664]{1,0:T(8,128)(2,1)S(1)}, bf16[64,1664]{1,0:T(8,128)(2,1)S(1)}, u32[]{:S(2)}, u32[]{:S(2)}) collective-permute-start(bf16[64,1664]{1,0:T(8,128)(2,1)S(1)} %fusion.5), channel_id=1, source_target_pairs={{0,96},{1,97},{2,98},{3,99},{4,100},{5,101},{6,102},{7,103},{8,104... | collective-permute-start | bytes 638984 | tf_op jit(solution)/shard_map/gather_hidden/ppermute | solution.py:30
  121.0 8.0 %collective-permute-start.25 = (bf16[64,1664]{1,0:T(8,128)(2,1)S(1)}, bf16[64,1664]{1,0:T(8,128)(2,1)S(1)}, u32[]{:S(2)}, u32[]{:S(2)}) collective-permute-start(bf16[64,1664]{1,0:T(8,128)(2,1)S(1)} %fusion.5), channel_id=1, source_target_pairs={{0,16},{1,17},{2,18},{3,19},{4,20},{5,21},{6,22},{7,23},{8,24},{9,... | collective-permute-start | bytes 638984 | tf_op jit(solution)/shard_map/gather_hidden/ppermute | solution.py:30
  128.3 1.8 %collective-permute-start.27 = (bf16[64,1664]{1,0:T(8,128)(2,1)S(1)}, bf16[64,1664]{1,0:T(8,128)(2,1)S(1)}, u32[]{:S(2)}, u32[]{:S(2)}) collective-permute-start(bf16[64,1664]{1,0:T(8,128)(2,1)S(1)} %collective-permute-done.26), channel_id=1, source_target_pairs={{0,16},{1,17},{2,18},{3,19},{4,20},{5,21},{6,22},{7,23},{8,24},{9,... | collective-permute-start | bytes 638984 | tf_op jit(solution)/shard_map/down/ppermute | solution.py:30
  128.4 1.8 %collective-permute-start.29 = (bf16[64,1664]{1,0:T(8,128)(2,1)S(1)}, bf16[64,1664]{1,0:T(8,128)(2,1)S(1)}, u32[]{:S(2)}, u32[]{:S(2)}) collective-permute-start(bf16[64,1664]{1,0:T(8,128)(2,1)S(1)} %collective-permute-done.28), channel_id=1, source_target_pairs={{0,16},{1,17},{2,18},{3,19},{4,20},{5,21},{6,22},{7,23},{8,24},{9,... | collective-permute-start | bytes 638984 | tf_op jit(solution)/shard_map/down/ppermute | solution.py:30
  128.9 1.5 collective-permute-start.31
  133.8 14.7 %collective-permute-start.32 = (bf16[128,2048]{1,0:T(8,128)(2,1)S(1)}, bf16[128,2048]{1,0:T(8,128)(2,1)S(1)}, u32[]{:S(2)}, u32[]{:S(2)}) collective-permute-start(bf16[128,2048]{1,0:T(8,128)(2,1)S(1)} %get-tuple-element.58), channel_id=1, source_target_pairs={{0,3},{1,0},{2,1},{3,2},{4,7},{5,4},{6,5},{7,6},{8,11},{9,8},{10,9... | collective-permute-start | bytes 1572872 | tf_op jit(solution)/shard_map/sum_down/ppermute | solution.py:30
  136.2 16.0 %collective-permute-start.33 = (bf16[128,2048]{1,0:T(8,128)(2,1)S(1)}, bf16[128,2048]{1,0:T(8,128)(2,1)S(1)}, u32[]{:S(2)}, u32[]{:S(2)}) collective-permute-start(bf16[128,2048]{1,0:T(8,128)(2,1)S(1)} %get-tuple-element.60), channel_id=1, source_target_pairs={{0,1},{1,2},{2,3},{3,0},{4,5},{5,6},{6,7},{7,4},{8,9},{9,10},{10,1... | collective-permute-start | bytes 1572872 | tf_op jit(solution)/shard_map/sum_down/ppermute | solution.py:30
  136.2 16.0 %collective-permute-start.34 = (bf16[128,2048]{1,0:T(8,128)(2,1)S(1)}, bf16[128,2048]{1,0:T(8,128)(2,1)S(1)}, u32[]{:S(2)}, u32[]{:S(2)}) collective-permute-start(bf16[128,2048]{1,0:T(8,128)(2,1)S(1)} %get-tuple-element.59), channel_id=1, source_target_pairs={{0,2},{1,3},{2,0},{3,1},{4,6},{5,7},{6,4},{7,5},{8,10},{9,11},{10,... | collective-permute-start | bytes 1572872 | tf_op jit(solution)/shard_map/sum_down/ppermute | solution.py:30
  152.5 5.0 %collective-permute-start.35 = (bf16[32,2048]{1,0:T(8,128)(2,1)S(1)}, bf16[32,2048]{1,0:T(8,128)(2,1)S(1)}, u32[]{:S(2)}, u32[]{:S(2)}) collective-permute-start(bf16[32,2048]{1,0:T(8,128)(2,1)S(1)} %get-tuple-element.55), channel_id=1, source_target_pairs={{0,12},{1,13},{2,14},{3,15},{4,0},{5,1},{6,2},{7,3},{8,4},{9,5},{1... | collective-permute-start | bytes 393224 | tf_op jit(solution)/shard_map/sum_down/ppermute | solution.py:30
  153.6 7.6 %collective-permute-start.36 = (bf16[32,2048]{1,0:T(8,128)(2,1)S(1)}, bf16[32,2048]{1,0:T(8,128)(2,1)S(1)}, u32[]{:S(2)}, u32[]{:S(2)}) collective-permute-start(bf16[32,2048]{1,0:T(8,128)(2,1)S(1)} %get-tuple-element.57), channel_id=1, source_target_pairs={{0,4},{1,5},{2,6},{3,7},{4,8},{5,9},{6,10},{7,11},{8,12},{9,13},{1... | collective-permute-start | bytes 393224 | tf_op jit(solution)/shard_map/sum_down/ppermute | solution.py:30
  154.5 6.6 %collective-permute-start.37 = (bf16[32,2048]{1,0:T(8,128)(2,1)S(1)}, bf16[32,2048]{1,0:T(8,128)(2,1)S(1)}, u32[]{:S(2)}, u32[]{:S(2)}) collective-permute-start(bf16[32,2048]{1,0:T(8,128)(2,1)S(1)} %get-tuple-element.56), channel_id=1, source_target_pairs={{0,8},{1,9},{2,10},{3,11},{4,12},{5,13},{6,14},{7,15},{8,0},{9,1},... | collective-permute-start | bytes 393224 | tf_op jit(solution)/shard_map/sum_down/ppermute | solution.py:30

commit v4 on v3

--- a/solution.py
+++ b/solution.py
@@ -326,40 +326,65 @@
         (first_gate, first_up), chunks = early_products(chunks, [gate_weight, up_weight])
         own_rows, away_rows, own_squares, away_squares = split(chunks, False, width)
         away_gate = in_place(first_gate, dot(away_rows, gate_weight), False, 1)
+        gate_shares = to_other_core(away_gate)
+        square_shares = own_squares, to_other_core(away_squares)
+        own_rows = after(own_rows, away_gate)
+        own_gate = in_place(first_gate, dot(own_rows, gate_weight), False, 0)
+        gate_shares = own_gate, gate_shares
+
+    def cut(terms, low, xor):
+        at = (low * 4 + (-xor & 3)) * rows
+        return add(*[t[at : at + rows] for t in terms])
+
+    def gate_of(low, xor):
+        return cut(gate_shares, low, xor), jnp.sum(cut(square_shares, low, xor), axis=1)
+
+    def up_of(low, xor):
+        return cut(up_shares, low, xor)
+
+    def gate_message(*totals):
+        gate, square = zip(*totals)
+        square = in_three(jnp.concatenate(square))
+        return jnp.concatenate([jnp.concatenate(gate, axis=0).astype(BF16), square], axis=1)
+
+    def up_message(*totals):
+        return jnp.concatenate(totals, axis=0).astype(BF16)
+
+    def gate_plus(total, message):
+        more = jnp.sum(message[:, cols:].astype(F32), axis=1)
+        return add(total[0], message[:, :cols]), total[1] + more
+
+    with jax.named_scope("sum_gate"):
+        low = gate_message(gate_of(0, 2), gate_of(0, 1))
+        high = gate_message(gate_of(1, 3), gate_of(1, 2))
+        gates = [across_y(low, 1), across_y(high, 3)]
+        away_rows = after(away_rows, low, high)
+    with jax.named_scope("sum_up"):
         away_up = in_place(first_up, dot(away_rows, up_weight), False, 1)
-        away = [to_other_core(t) for t in (away_gate, away_up, away_squares)]
-        own_rows = after(own_rows, away_gate, away_up)
-        own_gate = in_place(first_gate, dot(own_rows, gate_weight), False, 0)
-        own_rows = after(own_rows, away[0])
-        own_up = in_place(first_up, dot(own_rows, up_weight), False, 0)
-        own = [own_gate, own_up, own_squares]
-
-    def piece(low, xor):
-        at = (low * 4 + (-xor & 3)) * rows
-        gate, up, square = [add(o[at : at + rows], a[at : at + rows]) for o, a in zip(own, away)]
-        return gate, up, jnp.sum(square, axis=1)
-
-    def plus(total, message):
-        gate, up, square = total
-        more = jnp.sum(message[:, 2 * cols :].astype(F32), axis=1)
-        return add(gate, message[:, :cols]), add(up, message[:, cols : 2 * cols]), square + more
-
-    def message(*totals):
-        gate, up, square = [jnp.concatenate(t, axis=0) for t in zip(*totals)]
-        return jnp.concatenate([gate.astype(BF16), up.astype(BF16), in_three(square)], axis=1)
-
+        own_rows = after(own_rows, away_up)
+        up_shares = in_place(first_up, dot(own_rows, up_weight), False, 0), to_other_core(away_up)
+        ups = [
+            across_y(up_message(up_of(0, 2), up_of(0, 1)), 1),
+            across_y(up_message(up_of(1, 3), up_of(1, 2)), 3),
+        ]
+        gates, ups = lax.optimization_barrier((gates, ups))
     with jax.named_scope("sum_terms"):
-        low = across_y(message(piece(0, 2), piece(0, 1)), 1)
-        high = across_y(message(piece(1, 3), piece(1, 2)), 3)
-        low, high = lax.optimization_barrier((low, high))
-        low_last = across_y(message(plus(piece(0, 3), low[:rows])), 3)
-        high_last = across_y(message(plus(piece(1, 1), high[rows:])), 1)
-        low_last, high_last = lax.optimization_barrier((low_last, high_last))
-        sums = [
-            plus(plus(piece(0, 0), low[rows:]), low_last),
-            plus(plus(piece(1, 0), high[:rows]), high_last),
+
+        def passed_on(low, xor, at):
+            gate = gate_plus(gate_of(low, xor), gates[low][at : at + rows])
+            up = add(up_of(low, xor), ups[low][at : at + rows])
+            return jnp.concatenate([up_message(up), gate_message(gate)], axis=1)
+
+        last = [across_y(passed_on(0, 3, 0), 3), across_y(passed_on(1, 1, rows), 1)]
+        last = lax.optimization_barrier(last)
+        kept = [slice(rows, 2 * rows), slice(0, rows)]
+        gates = [
+            gate_plus(gate_plus(gate_of(n, 0), gates[n][kept[n]]), last[n][:, cols:])
+            for n in range(2)
         ]
-        gate, up, square = [jnp.concatenate(t, axis=0) for t in zip(*sums)]
+        ups = [add(up_of(n, 0), ups[n][kept[n]], last[n][:, :cols]) for n in range(2)]
+        gate, square = [jnp.concatenate(t, axis=0) for t in zip(*gates)]
+        up = jnp.concatenate(ups, axis=0)
         inv_rms = lax.rsqrt(square / D + 1e-05)[:, None]
         return (jax.nn.silu(inv_rms * gate) * (inv_rms * up)).astype(BF16)
 

time: 162 us -> 161 us (level)
  waiting for transfers between devices: 80.2 us -> 73.8 us
  starting transfers between devices: 50.8 us -> 55.4 us
    ppermute x38 -> x40, waiting for transfers between devices: 80.2 us -> 73.8 us  [send(): return lax.ppermute(value, AXES, pairs)]
    ppermute x38 -> x40, starting transfers between devices: 50.8 us -> 55.4 us  [send(): return lax.ppermute(value, AXES, pairs)]
  transfers between devices with their start and end apart: 38 -> 40, of which waited for: 27 -> 31; matrix products, arithmetic and copies ran while one was open for 10% -> 10% of each run, Pallas kernels for 0% -> 0%
where the time goes in v4:
time: 161 us; the launch traced here: 160 us
  waiting for transfers between devices  73.8 us (46%)
  starting transfers between devices  55.4 us (34%)
  matrix products  21.4 us (13%)
  Pallas kernels  4.16 us (3%)
  other arithmetic  3.71 us (2%)
    ppermute x40, waiting for transfers between devices, send(): return lax.ppermute(value, AXES, pairs)  73.8 us
    ppermute x40, starting transfers between devices, send(): return lax.ppermute(value, AXES, pairs)  55.4 us
    dot_general x14, matrix products, dot(): return jnp.dot(left, right, preferred_element_type=F32).astype(BF16)  21.4 us
    pallas_call x1, Pallas kernels, attend(): pl.pallas_call(attend_kernel, out_shape=pltpu.VMEM(queries.shape, BF16),...  3.26 us
  transfers between devices with their start and end apart: 40, of which 31 were waited for; matrix products, arithmetic and copies ran while one was open for 10% of the time, Pallas kernels for 0%

profile of v4, /device:TPU:0, one launch (start us, length us, event | category | flops | bytes accessed | tf_op | source)
XLA Modules:
  0.0 160.4 jit_solution(886392638013595721)
XLA Ops:
  0.0 3.3 %attention.1.refs_0_ = bf16[32,2048]{1,0:T(8,128)(2,1)S(1)} custom-call(s32[32]{0:T(128)} %lengths.1, bf16[32,2048]{1,0:T(8,128)(2,1)} %refs_0_.1, bf16[32,128]{1,0:T(8,128)(2,1)} %refs_1_.1, bf16[32,128,128]{2,1,0:T(8,128)(2,1)} %refs_2_.1, bf16[32,128]{1,0:T(8,128)(2,1)} %refs_3_.1, bf16[32,128,128]{2,1,0:T(8,128)(2,1)} %refs_4_.1), custom_call_target="tpu_custom_call" | custom-call | tf_op jit(solution)/shard_map/attention/pallas_call | solution.py:247
  3.3 1.6 %collective-permute-start = (bf16[32,2048]{1,0:T(8,128)(2,1)S(1)}, bf16[32,2048]{1,0:T(8,128)(2,1)S(1)}, u32[]{:S(2)}, u32[]{:S(2)}) collective-permute-start(bf16[32,2048]{1,0:T(8,128)(2,1)S(1)} %attention.1.refs_0_), channel_id=1, source_target_pairs={{0,4},{1,5},{2,6},{3,7},{4,8},{5,9},{6,10},{7,11},{8,12},{9,13},{1... | collective-permute-start | bytes 393224 | tf_op jit(solution)/shard_map/gather_attended/ppermute | solution.py:30
  4.9 2.7 %collective-permute-start.1 = (bf16[32,2048]{1,0:T(8,128)(2,1)S(1)}, bf16[32,2048]{1,0:T(8,128)(2,1)S(1)}, u32[]{:S(2)}, u32[]{:S(2)}) collective-permute-start(bf16[32,2048]{1,0:T(8,128)(2,1)S(1)} %attention.1.refs_0_), channel_id=1, source_target_pairs={{0,8},{1,9},{2,10},{3,11},{4,12},{5,13},{6,14},{7,15},{8,0},{9,1},... | collective-permute-start | bytes 393224 | tf_op jit(solution)/shard_map/gather_attended/ppermute | solution.py:30
  7.7 1.4 collective-permute-start.2
  9.5 2.5 %collective-permute-done.1.refs_2_ = bf16[32,2048]{1,0:T(8,128)(2,1)S(1)} collective-permute-done((bf16[32,2048]{1,0:T(8,128)(2,1)S(1)}, bf16[32,2048]{1,0:T(8,128)(2,1)S(1)}, u32[]{:S(2)}, u32[]{:S(2)}) %collective-permute-start.1) | collective-permute-done | bytes 131104 | tf_op jit(solution)/shard_map/gather_attended/ppermute | solution.py:30
  12.7 2.0 %collective-permute-start.3 = (bf16[128,2048]{1,0:T(8,128)(2,1)S(1)}, bf16[128,2048]{1,0:T(8,128)(2,1)S(1)}, u32[]{:S(2)}, u32[]{:S(2)}) collective-permute-start(bf16[128,2048]{1,0:T(8,128)(2,1)S(1)} %gather_attended.1.refs_0_), channel_id=1, source_target_pairs={{0,1},{1,2},{2,3},{3,0},{4,5},{5,6},{6,7},{7,4},{8,9},{9,10},{10,1... | collective-permute-start | bytes 1572872 | tf_op jit(solution)/shard_map/gather_attended/ppermute | solution.py:30
  14.7 2.2 %collective-permute-start.5 = (bf16[128,2048]{1,0:T(8,128)(2,1)S(1)}, bf16[128,2048]{1,0:T(8,128)(2,1)S(1)}, u32[]{:S(2)}, u32[]{:S(2)}) collective-permute-start(bf16[128,2048]{1,0:T(8,128)(2,1)S(1)} %gather_attended.1.refs_0_), channel_id=1, source_target_pairs={{0,3},{1,0},{2,1},{3,2},{4,7},{5,4},{6,5},{7,6},{8,11},{9,8},{10,9... | collective-permute-start | bytes 1572872 | tf_op jit(solution)/shard_map/gather_attended/ppermute | solution.py:30
  16.9 1.8 %collective-permute-start.4 = (bf16[128,2048]{1,0:T(8,128)(2,1)S(1)}, bf16[128,2048]{1,0:T(8,128)(2,1)S(1)}, u32[]{:S(2)}, u32[]{:S(2)}) collective-permute-start(bf16[128,2048]{1,0:T(8,128)(2,1)S(1)} %gather_attended.1.refs_0_), channel_id=1, source_target_pairs={{0,2},{1,3},{2,0},{3,1},{4,6},{5,7},{6,4},{7,5},{8,10},{9,11},{10,... | collective-permute-start | bytes 1572872 | tf_op jit(solution)/shard_map/gather_attended/ppermute | solution.py:30
  18.6 2.9 %convolution_convert_fusion.13.refs_0_ = bf16[128,1024]{1,0:T(8,128)(2,1)S(1)} fusion(bf16[128,2048]{1,0:T(8,128)(2,1)S(1)} %gather_attended.1.refs_0_, bf16[2048,1024]{1,0:T(8,128)(2,1)} %param.19), kind=kOutput, calls=%fused_computation.13 | convolution fusion | flops 537001984 | bytes 4980736 | tf_op jit(solution)/shard_map/projection/dot_general | solution.py:260
  21.6 2.3 %collective-permute-done.3.refs_1_ = bf16[128,2048]{1,0:T(8,128)(2,1)S(1)} collective-permute-done((bf16[128,2048]{1,0:T(8,128)(2,1)S(1)}, bf16[128,2048]{1,0:T(8,128)(2,1)S(1)}, u32[]{:S(2)}, u32[]{:S(2)}) %collective-permute-start.3) | collective-permute-done | bytes 524320 | tf_op jit(solution)/shard_map/gather_attended/ppermute | solution.py:30
  24.7 4.5 %collective-permute-done.5.refs_3_ = bf16[128,2048]{1,0:T(8,128)(2,1)S(1)} collective-permute-done((bf16[128,2048]{1,0:T(8,128)(2,1)S(1)}, bf16[128,2048]{1,0:T(8,128)(2,1)S(1)}, u32[]{:S(2)}, u32[]{:S(2)}) %collective-permute-start.5) | collective-permute-done | bytes 524320 | tf_op jit(solution)/shard_map/gather_attended/ppermute | solution.py:30
  29.2 1.8 %collective-permute-done.4.refs_2_ = bf16[128,2048]{1,0:T(8,128)(2,1)S(1)} collective-permute-done((bf16[128,2048]{1,0:T(8,128)(2,1)S(1)}, bf16[128,2048]{1,0:T(8,128)(2,1)S(1)}, u32[]{:S(2)}, u32[]{:S(2)}) %collective-permute-start.4) | collective-permute-done | bytes 524320 | tf_op jit(solution)/shard_map/gather_attended/ppermute | solution.py:30
  34.0 1.6 %collective-permute-start.7 = (bf16[64,1024]{1,0:T(8,128)(2,1)S(1)}, bf16[64,1024]{1,0:T(8,128)(2,1)S(1)}, u32[]{:S(2)}, u32[]{:S(2)}) collective-permute-start(bf16[64,1024]{1,0:T(8,128)(2,1)S(1)} %get-tuple-element.83), channel_id=1, source_target_pairs={{0,32},{1,33},{2,34},{3,35},{4,36},{5,37},{6,38},{7,39},{8,40},{9,... | collective-permute-start | bytes 393224 | tf_op jit(solution)/shard_map/sum_projected/ppermute | solution.py:30
  35.7 1.7 %collective-permute-start.8 = (bf16[64,1024]{1,0:T(8,128)(2,1)S(1)}, bf16[64,1024]{1,0:T(8,128)(2,1)S(1)}, u32[]{:S(2)}, u32[]{:S(2)}) collective-permute-start(bf16[64,1024]{1,0:T(8,128)(2,1)S(1)} %get-tuple-element.85), channel_id=1, source_target_pairs={{0,96},{1,97},{2,98},{3,99},{4,100},{5,101},{6,102},{7,103},{8,104... | collective-permute-start | bytes 393224 | tf_op jit(solution)/shard_map/sum_projected/ppermute | solution.py:30
  37.3 2.0 %collective-permute-start.9 = (bf16[64,1024]{1,0:T(8,128)(2,1)S(1)}, bf16[64,1024]{1,0:T(8,128)(2,1)S(1)}, u32[]{:S(2)}, u32[]{:S(2)}) collective-permute-start(bf16[64,1024]{1,0:T(8,128)(2,1)S(1)} %get-tuple-element.84), channel_id=1, source_target_pairs={{0,64},{1,65},{2,66},{3,67},{4,68},{5,69},{6,70},{7,71},{8,72},{9,... | collective-permute-start | bytes 393224 | tf_op jit(solution)/shard_map/sum_projected/ppermute | solution.py:30
  39.3 1.6 collective-permute-done.7
  40.9 2.2 %collective-permute-done.8 = bf16[64,1024]{1,0:T(8,128)(2,1)S(1)} collective-permute-done((bf16[64,1024]{1,0:T(8,128)(2,1)S(1)}, bf16[64,1024]{1,0:T(8,128)(2,1)S(1)}, u32[]{:S(2)}, u32[]{:S(2)}) %collective-permute-start.8) | collective-permute-done | bytes 131104 | tf_op jit(solution)/shard_map/sum_projected/ppermute | solution.py:30
  43.1 1.8 %collective-permute-done.9 = bf16[64,1024]{1,0:T(8,128)(2,1)S(1)} collective-permute-done((bf16[64,1024]{1,0:T(8,128)(2,1)S(1)}, bf16[64,1024]{1,0:T(8,128)(2,1)S(1)}, u32[]{:S(2)}, u32[]{:S(2)}) %collective-permute-start.9) | collective-permute-done | bytes 131104 | tf_op jit(solution)/shard_map/sum_projected/ppermute | solution.py:30
  45.0 3.3 %collective-permute-start.10 = (bf16[32,1024]{1,0:T(8,128)(2,1)S(1)}, bf16[32,1024]{1,0:T(8,128)(2,1)S(1)}, u32[]{:S(2)}, u32[]{:S(2)}) collective-permute-start(bf16[32,1024]{1,0:T(8,128)(2,1)S(1)} %get-tuple-element.92), channel_id=1, source_target_pairs={{0,9},{1,10},{2,27},{3,24},{4,35},{5,32},{6,49},{7,50},{8,73},{9,7... | collective-permute-start | bytes 196616 | tf_op jit(solution)/shard_map/to_owners/ppermute | solution.py:30
  49.2 2.4 %collective-permute-done.10 = bf16[32,1024]{1,0:T(8,128)(2,1)S(1)} collective-permute-done((bf16[32,1024]{1,0:T(8,128)(2,1)S(1)}, bf16[32,1024]{1,0:T(8,128)(2,1)S(1)}, u32[]{:S(2)}, u32[]{:S(2)}) %collective-permute-start.10) | collective-permute-done | bytes 65568 | tf_op jit(solution)/shard_map/to_owners/ppermute | solution.py:30
  51.6 2.8 %collective-permute-done.11 = bf16[32,1024]{1,0:T(8,128)(2,1)S(1)} collective-permute-done((bf16[32,1024]{1,0:T(8,128)(2,1)S(1)}, bf16[32,1024]{1,0:T(8,128)(2,1)S(1)}, u32[]{:S(2)}, u32[]{:S(2)}) %collective-permute-start.11) | collective-permute-done | bytes 65568 | tf_op jit(solution)/shard_map/to_owners/ppermute | solution.py:30
  54.8 5.5 %collective-permute-start.13 = (bf16[32,2176]{1,0:T(8,128)(2,1)S(1)}, bf16[32,2176]{1,0:T(8,128)(2,1)S(1)}, u32[]{:S(2)}, u32[]{:S(2)}) collective-permute-start(bf16[32,2176]{1,0:T(8,128)(2,1)S(1)} %pad_maximum_fusion.6.refs_0_), channel_id=1, source_target_pairs={{0,8},{1,9},{2,10},{3,11},{4,12},{5,13},{6,14},{7,15},{8,0},{9,1},... | collective-permute-start | bytes 417800 | tf_op jit(solution)/shard_map/gather_scaled/ppermute | solution.py:30
  60.3 1.6 collective-permute-done.12.refs_1_
  61.8 2.9 %collective-permute-done.13.refs_2_ = bf16[32,2176]{1,0:T(8,128)(2,1)S(1)} collective-permute-done((bf16[32,2176]{1,0:T(8,128)(2,1)S(1)}, bf16[32,2176]{1,0:T(8,128)(2,1)S(1)}, u32[]{:S(2)}, u32[]{:S(2)}) %collective-permute-start.13) | collective-permute-done | bytes 139296 | tf_op jit(solution)/shard_map/gather_scaled/ppermute | solution.py:30
  65.5 3.2 %collective-permute-start.17 = (bf16[128,2176]{1,0:T(8,128)(2,1)S(1)}, bf16[128,2176]{1,0:T(8,128)(2,1)S(1)}, u32[]{:S(2)}, u32[]{:S(2)}) collective-permute-start(bf16[128,2176]{1,0:T(8,128)(2,1)S(1)} %gather_scaled.1.refs_0_), channel_id=1, source_target_pairs={{0,3},{1,0},{2,1},{3,2},{4,7},{5,4},{6,5},{7,6},{8,11},{9,8},{10,9... | collective-permute-start | bytes 1671176 | tf_op jit(solution)/shard_map/gather_scaled/ppermute | solution.py:30
  68.7 3.1 %collective-permute-start.16 = (bf16[128,2176]{1,0:T(8,128)(2,1)S(1)}, bf16[128,2176]{1,0:T(8,128)(2,1)S(1)}, u32[]{:S(2)}, u32[]{:S(2)}) collective-permute-start(bf16[128,2176]{1,0:T(8,128)(2,1)S(1)} %gather_scaled.1.refs_0_), channel_id=1, source_target_pairs={{0,2},{1,3},{2,0},{3,1},{4,6},{5,7},{6,4},{7,5},{8,10},{9,11},{10,... | collective-permute-start | bytes 1671176 | tf_op jit(solution)/shard_map/gather_scaled/ppermute | solution.py:30
  71.8 4.1 %convolution_convert_fusion.7.refs_0_ = bf16[128,1664]{1,0:T(8,128)(2,1)S(1)} fusion(bf16[2048,1664]{1,0:T(8,128)(2,1)} %param.21, bf16[128,2176]{1,0:T(8,128)(2,1)S(1)} %gather_scaled.1.refs_0_), kind=kOutput, calls=%fused_computation.7 | convolution fusion | flops 872628224 | bytes 7766016 | tf_op jit(solution)/shard_map/gate_up/dot_general | solution.py:260
  80.3 3.0 %collective-permute-done.16.refs_2_ = bf16[128,2176]{1,0:T(8,128)(2,1)S(1)} collective-permute-done((bf16[128,2176]{1,0:T(8,128)(2,1)S(1)}, bf16[128,2176]{1,0:T(8,128)(2,1)S(1)}, u32[]{:S(2)}, u32[]{:S(2)}) %collective-permute-start.16) | collective-permute-done | bytes 557088 | tf_op jit(solution)/shard_map/gather_scaled/ppermute | solution.py:30
  89.3 3.3 %collective-permute-start.21 = (bf16[64,1792]{1,0:T(8,128)(2,1)S(1)}, bf16[64,1792]{1,0:T(8,128)(2,1)S(1)}, u32[]{:S(2)}, u32[]{:S(2)}) collective-permute-start(bf16[64,1792]{1,0:T(8,128)(2,1)S(1)} %pad_maximum_fusion.1), channel_id=1, source_target_pairs={{0,96},{1,97},{2,98},{3,99},{4,100},{5,101},{6,102},{7,103},{8,104... | collective-permute-start | bytes 688136 | tf_op jit(solution)/shard_map/sum_gate/ppermute | solution.py:30
  94.9 1.3 collective-permute-start.23
  96.3 2.8 %collective-permute-done.21 = bf16[64,1792]{1,0:T(8,128)(2,1)S(1)} collective-permute-done((bf16[64,1792]{1,0:T(8,128)(2,1)S(1)}, bf16[64,1792]{1,0:T(8,128)(2,1)S(1)}, u32[]{:S(2)}, u32[]{:S(2)}) %collective-permute-start.21) | collective-permute-done | bytes 229408 | tf_op jit(solution)/shard_map/sum_gate/ppermute | solution.py:30
  99.1 2.1 %collective-permute-done.20 = bf16[64,1792]{1,0:T(8,128)(2,1)S(1)} collective-permute-done((bf16[64,1792]{1,0:T(8,128)(2,1)S(1)}, bf16[64,1792]{1,0:T(8,128)(2,1)S(1)}, u32[]{:S(2)}, u32[]{:S(2)}) %collective-permute-start.20) | collective-permute-done | bytes 229408 | tf_op jit(solution)/shard_map/sum_gate/ppermute | solution.py:30
  101.2 2.0 %collective-permute-done.24 = bf16[64,1664]{1,0:T(8,128)(2,1)S(1)} collective-permute-done((bf16[64,1664]{1,0:T(8,128)(2,1)S(1)}, bf16[64,1664]{1,0:T(8,128)(2,1)S(1)}, u32[]{:S(2)}, u32[]{:S(2)}) %collective-permute-start.24) | collective-permute-done | bytes 213024 | tf_op jit(solution)/shard_map/sum_up/ppermute | solution.py:30
  103.1 1.5 collective-permute-done.23
  105.5 1.5 collective-permute-start.25
  107.1 4.5 %collective-permute-done.26 = bf16[32,3456]{1,0:T(8,128)(2,1)S(1)} collective-permute-done((bf16[32,3456]{1,0:T(8,128)(2,1)S(1)}, bf16[32,3456]{1,0:T(8,128)(2,1)S(1)}, u32[]{:S(2)}, u32[]{:S(2)}) %collective-permute-start.26) | collective-permute-done | bytes 221216 | tf_op jit(solution)/shard_map/sum_terms/ppermute | solution.py:30
  111.5 1.9 %collective-permute-done.25 = bf16[32,3456]{1,0:T(8,128)(2,1)S(1)} collective-permute-done((bf16[32,3456]{1,0:T(8,128)(2,1)S(1)}, bf16[32,3456]{1,0:T(8,128)(2,1)S(1)}, u32[]{:S(2)}, u32[]{:S(2)}) %collective-permute-start.25) | collective-permute-done | bytes 221216 | tf_op jit(solution)/shard_map/sum_terms/ppermute | solution.py:30
  114.5 2.8 %collective-permute-start.30 = (bf16[64,1664]{1,0:T(8,128)(2,1)S(1)}, bf16[64,1664]{1,0:T(8,128)(2,1)S(1)}, u32[]{:S(2)}, u32[]{:S(2)}) collective-permute-start(bf16[64,1664]{1,0:T(8,128)(2,1)S(1)} %fusion.5), channel_id=1, source_target_pairs={{0,64},{1,65},{2,66},{3,67},{4,68},{5,69},{6,70},{7,71},{8,72},{9,... | collective-permute-start | bytes 638984 | tf_op jit(solution)/shard_map/gather_hidden/ppermute | solution.py:30
  118.3 4.8 %collective-permute-done.28 = bf16[64,1664]{1,0:T(8,128)(2,1)S(1)} collective-permute-done((bf16[64,1664]{1,0:T(8,128)(2,1)S(1)}, bf16[64,1664]{1,0:T(8,128)(2,1)S(1)}, u32[]{:S(2)}, u32[]{:S(2)}) %collective-permute-start.28) | collective-permute-done | bytes 213024 | tf_op jit(solution)/shard_map/gather_hidden/ppermute | solution.py:30
  123.1 2.3 %collective-permute-done.30 = bf16[64,1664]{1,0:T(8,128)(2,1)S(1)} collective-permute-done((bf16[64,1664]{1,0:T(8,128)(2,1)S(1)}, bf16[64,1664]{1,0:T(8,128)(2,1)S(1)}, u32[]{:S(2)}, u32[]{:S(2)}) %collective-permute-start.30) | collective-permute-done | bytes 213024 | tf_op jit(solution)/shard_map/gather_hidden/ppermute | solution.py:30
  127.4 3.1 %convolution_convert_fusion.rest = bf16[384,2048]{1,0:T(8,128)(2,1)S(1)} fusion(bf16[384,1664]{1,0:T(8,128)(2,1)S(1)} %constant_dynamic-update-slice_fusion, bf16[1664,2048]{1,0:T(8,128)(2,1)S(1)} %bitcast.28), kind=kOutput, calls=%fused_computation | convolution fusion | flops 2618032128 | bytes 9666560 | tf_op jit(solution)/shard_map/down/dot_general | solution.py:260
  130.9 2.4 %collective-permute-start.34 = (bf16[128,2048]{1,0:T(8,128)(2,1)S(1)}, bf16[128,2048]{1,0:T(8,128)(2,1)S(1)}, u32[]{:S(2)}, u32[]{:S(2)}) collective-permute-start(bf16[128,2048]{1,0:T(8,128)(2,1)S(1)} %get-tuple-element.64), channel_id=1, source_target_pairs={{0,3},{1,0},{2,1},{3,2},{4,7},{5,4},{6,5},{7,6},{8,11},{9,8},{10,9... | collective-permute-start | bytes 1572872 | tf_op jit(solution)/shard_map/sum_down/ppermute | solution.py:30
  133.3 3.2 %collective-permute-start.36 = (bf16[128,2048]{1,0:T(8,128)(2,1)S(1)}, bf16[128,2048]{1,0:T(8,128)(2,1)S(1)}, u32[]{:S(2)}, u32[]{:S(2)}) collective-permute-start(bf16[128,2048]{1,0:T(8,128)(2,1)S(1)} %get-tuple-element.65), channel_id=1, source_target_pairs={{0,2},{1,3},{2,0},{3,1},{4,6},{5,7},{6,4},{7,5},{8,10},{9,11},{10,... | collective-permute-start | bytes 1572872 | tf_op jit(solution)/shard_map/sum_down/ppermute | solution.py:30
  136.5 9.1 %collective-permute-done.34 = bf16[128,2048]{1,0:T(8,128)(2,1)S(1)} collective-permute-done((bf16[128,2048]{1,0:T(8,128)(2,1)S(1)}, bf16[128,2048]{1,0:T(8,128)(2,1)S(1)}, u32[]{:S(2)}, u32[]{:S(2)}) %collective-permute-start.34) | collective-permute-done | bytes 524320 | tf_op jit(solution)/shard_map/sum_down/ppermute | solution.py:30
  145.6 3.7 %collective-permute-done.36 = bf16[128,2048]{1,0:T(8,128)(2,1)S(1)} collective-permute-done((bf16[128,2048]{1,0:T(8,128)(2,1)S(1)}, bf16[128,2048]{1,0:T(8,128)(2,1)S(1)}, u32[]{:S(2)}, u32[]{:S(2)}) %collective-permute-start.36) | collective-permute-done | bytes 524320 | tf_op jit(solution)/shard_map/sum_down/ppermute | solution.py:30
  149.5 2.4 %collective-permute-start.37 = (bf16[32,2048]{1,0:T(8,128)(2,1)S(1)}, bf16[32,2048]{1,0:T(8,128)(2,1)S(1)}, u32[]{:S(2)}, u32[]{:S(2)}) collective-permute-start(bf16[32,2048]{1,0:T(8,128)(2,1)S(1)} %get-tuple-element.61), channel_id=1, source_target_pairs={{0,12},{1,13},{2,14},{3,15},{4,0},{5,1},{6,2},{7,3},{8,4},{9,5},{1... | collective-permute-start | bytes 393224 | tf_op jit(solution)/shard_map/sum_down/ppermute | solution.py:30
  151.9 1.7 %collective-permute-start.39 = (bf16[32,2048]{1,0:T(8,128)(2,1)S(1)}, bf16[32,2048]{1,0:T(8,128)(2,1)S(1)}, u32[]{:S(2)}, u32[]{:S(2)}) collective-permute-start(bf16[32,2048]{1,0:T(8,128)(2,1)S(1)} %get-tuple-element.62), channel_id=1, source_target_pairs={{0,8},{1,9},{2,10},{3,11},{4,12},{5,13},{6,14},{7,15},{8,0},{9,1},... | collective-permute-start | bytes 393224 | tf_op jit(solution)/shard_map/sum_down/ppermute | solution.py:30
  154.6 5.0 %collective-permute-done.38 = bf16[32,2048]{1,0:T(8,128)(2,1)S(1)} collective-permute-done((bf16[32,2048]{1,0:T(8,128)(2,1)S(1)}, bf16[32,2048]{1,0:T(8,128)(2,1)S(1)}, u32[]{:S(2)}, u32[]{:S(2)}) %collective-permute-start.38) | collective-permute-done | bytes 131104 | tf_op jit(solution)/shard_map/sum_down/ppermute | solution.py:30
  (127 shorter events, 26.7 us)
Async XLA Ops:
  3.3 20.7 %copy-start = (bf16[2048,1024]{1,0:T(8,128)(2,1)S(1)}, bf16[2048,1024]{1,0:T(8,128)(2,1)}, u32[]{:S(2)}) copy-start(bf16[2048,1024]{1,0:T(8,128)(2,1)} %param.19) | copy-start | bytes 12582916
  3.3 6.2 %collective-permute-start = (bf16[32,2048]{1,0:T(8,128)(2,1)S(1)}, bf16[32,2048]{1,0:T(8,128)(2,1)S(1)}, u32[]{:S(2)}, u32[]{:S(2)}) collective-permute-start(bf16[32,2048]{1,0:T(8,128)(2,1)S(1)} %attention.1.refs_0_), channel_id=1, source_target_pairs={{0,4},{1,5},{2,6},{3,7},{4,8},{5,9},{6,10},{7,11},{8,12},{9,13},{1... | collective-permute-start | bytes 393224 | tf_op jit(solution)/shard_map/gather_attended/ppermute | solution.py:30
  4.9 7.1 %collective-permute-start.1 = (bf16[32,2048]{1,0:T(8,128)(2,1)S(1)}, bf16[32,2048]{1,0:T(8,128)(2,1)S(1)}, u32[]{:S(2)}, u32[]{:S(2)}) collective-permute-start(bf16[32,2048]{1,0:T(8,128)(2,1)S(1)} %attention.1.refs_0_), channel_id=1, source_target_pairs={{0,8},{1,9},{2,10},{3,11},{4,12},{5,13},{6,14},{7,15},{8,0},{9,1},... | collective-permute-start | bytes 393224 | tf_op jit(solution)/shard_map/gather_attended/ppermute | solution.py:30
  7.7 5.0 %collective-permute-start.2 = (bf16[32,2048]{1,0:T(8,128)(2,1)S(1)}, bf16[32,2048]{1,0:T(8,128)(2,1)S(1)}, u32[]{:S(2)}, u32[]{:S(2)}) collective-permute-start(bf16[32,2048]{1,0:T(8,128)(2,1)S(1)} %attention.1.refs_0_), channel_id=1, source_target_pairs={{0,12},{1,13},{2,14},{3,15},{4,0},{5,1},{6,2},{7,3},{8,4},{9,5},{1... | collective-permute-start | bytes 393224 | tf_op jit(solution)/shard_map/gather_attended/ppermute | solution.py:30
  12.7 11.3 %collective-permute-start.3 = (bf16[128,2048]{1,0:T(8,128)(2,1)S(1)}, bf16[128,2048]{1,0:T(8,128)(2,1)S(1)}, u32[]{:S(2)}, u32[]{:S(2)}) collective-permute-start(bf16[128,2048]{1,0:T(8,128)(2,1)S(1)} %gather_attended.1.refs_0_), channel_id=1, source_target_pairs={{0,1},{1,2},{2,3},{3,0},{4,5},{5,6},{6,7},{7,4},{8,9},{9,10},{10,1... | collective-permute-start | bytes 1572872 | tf_op jit(solution)/shard_map/gather_attended/ppermute | solution.py:30
  14.7 14.6 %collective-permute-start.5 = (bf16[128,2048]{1,0:T(8,128)(2,1)S(1)}, bf16[128,2048]{1,0:T(8,128)(2,1)S(1)}, u32[]{:S(2)}, u32[]{:S(2)}) collective-permute-start(bf16[128,2048]{1,0:T(8,128)(2,1)S(1)} %gather_attended.1.refs_0_), channel_id=1, source_target_pairs={{0,3},{1,0},{2,1},{3,2},{4,7},{5,4},{6,5},{7,6},{8,11},{9,8},{10,9... | collective-permute-start | bytes 1572872 | tf_op jit(solution)/shard_map/gather_attended/ppermute | solution.py:30
  16.9 14.2 %collective-permute-start.4 = (bf16[128,2048]{1,0:T(8,128)(2,1)S(1)}, bf16[128,2048]{1,0:T(8,128)(2,1)S(1)}, u32[]{:S(2)}, u32[]{:S(2)}) collective-permute-start(bf16[128,2048]{1,0:T(8,128)(2,1)S(1)} %gather_attended.1.refs_0_), channel_id=1, source_target_pairs={{0,2},{1,3},{2,0},{3,1},{4,6},{5,7},{6,4},{7,5},{8,10},{9,11},{10,... | collective-permute-start | bytes 1572872 | tf_op jit(solution)/shard_map/gather_attended/ppermute | solution.py:30
  31.8 7.5 %copy-start.2 = (bf16[2048]{0:T(1024)(128)(2,1)S(1)}, bf16[2048]{0:T(1024)(128)(2,1)}, u32[]{:S(2)}) copy-start(bf16[2048]{0:T(1024)(128)(2,1)} %param.20) | copy-start | bytes 12292
  31.9 2.0 %collective-permute-start.6 = (bf16[256,1024]{1,0:T(8,128)(2,1)S(1)}, bf16[256,1024]{1,0:T(8,128)(2,1)S(1)}, u32[]{:S(2)}, u32[]{:S(2)}) collective-permute-start(bf16[256,1024]{1,0:T(8,128)(2,1)S(1)} %projection.4), channel_id=1, source_target_pairs={{0,16},{1,17},{2,18},{3,19},{4,20},{5,21},{6,22},{7,23},{8,24},{9,... | collective-permute-start | bytes 1572872 | tf_op jit(solution)/shard_map/projection/ppermute | solution.py:30
  32.0 22.4 %copy-start.1 = (f32[32,2048]{1,0:T(8,128)S(1)}, f32[32,2048]{1,0:T(8,128)}, u32[]{:S(2)}) copy-start(f32[32,2048]{1,0:T(8,128)} %param.18) | copy-start | bytes 786436
  34.0 6.9 %collective-permute-start.7 = (bf16[64,1024]{1,0:T(8,128)(2,1)S(1)}, bf16[64,1024]{1,0:T(8,128)(2,1)S(1)}, u32[]{:S(2)}, u32[]{:S(2)}) collective-permute-start(bf16[64,1024]{1,0:T(8,128)(2,1)S(1)} %get-tuple-element.83), channel_id=1, source_target_pairs={{0,32},{1,33},{2,34},{3,35},{4,36},{5,37},{6,38},{7,39},{8,40},{9,... | collective-permute-start | bytes 393224 | tf_op jit(solution)/shard_map/sum_projected/ppermute | solution.py:30
  35.7 7.4 %collective-permute-start.8 = (bf16[64,1024]{1,0:T(8,128)(2,1)S(1)}, bf16[64,1024]{1,0:T(8,128)(2,1)S(1)}, u32[]{:S(2)}, u32[]{:S(2)}) collective-permute-start(bf16[64,1024]{1,0:T(8,128)(2,1)S(1)} %get-tuple-element.85), channel_id=1, source_target_pairs={{0,96},{1,97},{2,98},{3,99},{4,100},{5,101},{6,102},{7,103},{8,104... | collective-permute-start | bytes 393224 | tf_op jit(solution)/shard_map/sum_projected/ppermute | solution.py:30
  37.3 7.6 %collective-permute-start.9 = (bf16[64,1024]{1,0:T(8,128)(2,1)S(1)}, bf16[64,1024]{1,0:T(8,128)(2,1)S(1)}, u32[]{:S(2)}, u32[]{:S(2)}) collective-permute-start(bf16[64,1024]{1,0:T(8,128)(2,1)S(1)} %get-tuple-element.84), channel_id=1, source_target_pairs={{0,64},{1,65},{2,66},{3,67},{4,68},{5,69},{6,70},{7,71},{8,72},{9,... | collective-permute-start | bytes 393224 | tf_op jit(solution)/shard_map/sum_projected/ppermute | solution.py:30
  45.0 6.6 %collective-permute-start.10 = (bf16[32,1024]{1,0:T(8,128)(2,1)S(1)}, bf16[32,1024]{1,0:T(8,128)(2,1)S(1)}, u32[]{:S(2)}, u32[]{:S(2)}) collective-permute-start(bf16[32,1024]{1,0:T(8,128)(2,1)S(1)} %get-tuple-element.92), channel_id=1, source_target_pairs={{0,9},{1,10},{2,27},{3,24},{4,35},{5,32},{6,49},{7,50},{8,73},{9,7... | collective-permute-start | bytes 196616 | tf_op jit(solution)/shard_map/to_owners/ppermute | solution.py:30
  48.3 6.2 %collective-permute-start.11 = (bf16[32,1024]{1,0:T(8,128)(2,1)S(1)}, bf16[32,1024]{1,0:T(8,128)(2,1)S(1)}, u32[]{:S(2)}, u32[]{:S(2)}) collective-permute-start(bf16[32,1024]{1,0:T(8,128)(2,1)S(1)} %get-tuple-element.93), channel_id=1, source_target_pairs={{0,8},{1,9},{2,26},{3,27},{4,34},{5,35},{6,48},{7,49},{8,72},{9,73... | collective-permute-start | bytes 196616 | tf_op jit(solution)/shard_map/to_owners/ppermute | solution.py:30
  54.7 7.1 %collective-permute-start.12 = (bf16[32,2176]{1,0:T(8,128)(2,1)S(1)}, bf16[32,2176]{1,0:T(8,128)(2,1)S(1)}, u32[]{:S(2)}, u32[]{:S(2)}) collective-permute-start(bf16[32,2176]{1,0:T(8,128)(2,1)S(1)} %pad_maximum_fusion.6.refs_0_), channel_id=1, source_target_pairs={{0,4},{1,5},{2,6},{3,7},{4,8},{5,9},{6,10},{7,11},{8,12},{9,13},{1... | collective-permute-start | bytes 417800 | tf_op jit(solution)/shard_map/gather_scaled/ppermute | solution.py:30
  54.8 10.0 %collective-permute-start.13 = (bf16[32,2176]{1,0:T(8,128)(2,1)S(1)}, bf16[32,2176]{1,0:T(8,128)(2,1)S(1)}, u32[]{:S(2)}, u32[]{:S(2)}) collective-permute-start(bf16[32,2176]{1,0:T(8,128)(2,1)S(1)} %pad_maximum_fusion.6.refs_0_), channel_id=1, source_target_pairs={{0,8},{1,9},{2,10},{3,11},{4,12},{5,13},{6,14},{7,15},{8,0},{9,1},... | collective-permute-start | bytes 417800 | tf_op jit(solution)/shard_map/gather_scaled/ppermute | solution.py:30
  60.3 5.1 %collective-permute-start.14 = (bf16[32,2176]{1,0:T(8,128)(2,1)S(1)}, bf16[32,2176]{1,0:T(8,128)(2,1)S(1)}, u32[]{:S(2)}, u32[]{:S(2)}) collective-permute-start(bf16[32,2176]{1,0:T(8,128)(2,1)S(1)} %pad_maximum_fusion.6.refs_0_), channel_id=1, source_target_pairs={{0,12},{1,13},{2,14},{3,15},{4,0},{5,1},{6,2},{7,3},{8,4},{9,5},{1... | collective-permute-start | bytes 417800 | tf_op jit(solution)/shard_map/gather_scaled/ppermute | solution.py:30
  65.3 10.6 %slice-start.2 = ((s8[6815744]{0:T(1024)(128)(4,1)}), s8[4194304]{0:T(1024)(128)(4,1)S(1)}, s32[]{:S(2)}) async-start(s8[6815744]{0:T(1024)(128)(4,1)} %bitcast.25), calls=%async_computation.2 | async-start | bytes 8388608
  65.4 10.5 %slice-start.3 = ((s8[6815744]{0:T(1024)(128)(4,1)}), s8[2621440]{0:T(1024)(128)(4,1)S(1)}, s32[]{:S(2)}) async-start(s8[6815744]{0:T(1024)(128)(4,1)} %bitcast.25), calls=%async_computation.3 | async-start | bytes 5242880
  65.4 11.7 %collective-permute-start.15 = (bf16[128,2176]{1,0:T(8,128)(2,1)S(1)}, bf16[128,2176]{1,0:T(8,128)(2,1)S(1)}, u32[]{:S(2)}, u32[]{:S(2)}) collective-permute-start(bf16[128,2176]{1,0:T(8,128)(2,1)S(1)} %gather_scaled.1.refs_0_), channel_id=1, source_target_pairs={{0,1},{1,2},{2,3},{3,0},{4,5},{5,6},{6,7},{7,4},{8,9},{9,10},{10,1... | collective-permute-start | bytes 1671176 | tf_op jit(solution)/shard_map/gather_scaled/ppermute | solution.py:30
  65.5 14.8 %collective-permute-start.17 = (bf16[128,2176]{1,0:T(8,128)(2,1)S(1)}, bf16[128,2176]{1,0:T(8,128)(2,1)S(1)}, u32[]{:S(2)}, u32[]{:S(2)}) collective-permute-start(bf16[128,2176]{1,0:T(8,128)(2,1)S(1)} %gather_scaled.1.refs_0_), channel_id=1, source_target_pairs={{0,3},{1,0},{2,1},{3,2},{4,7},{5,4},{6,5},{7,6},{8,11},{9,8},{10,9... | collective-permute-start | bytes 1671176 | tf_op jit(solution)/shard_map/gather_scaled/ppermute | solution.py:30
  68.7 14.6 %collective-permute-start.16 = (bf16[128,2176]{1,0:T(8,128)(2,1)S(1)}, bf16[128,2176]{1,0:T(8,128)(2,1)S(1)}, u32[]{:S(2)}, u32[]{:S(2)}) collective-permute-start(bf16[128,2176]{1,0:T(8,128)(2,1)S(1)} %gather_scaled.1.refs_0_), channel_id=1, source_target_pairs={{0,2},{1,3},{2,0},{3,1},{4,6},{5,7},{6,4},{7,5},{8,10},{9,11},{10,... | collective-permute-start | bytes 1671176 | tf_op jit(solution)/shard_map/gather_scaled/ppermute | solution.py:30
  75.9 2.3 %slice-start = ((s8[6815744]{0:T(1024)(128)(4,1)}), s8[4194304]{0:T(1024)(128)(4,1)S(1)}, s32[]{:S(2)}) async-start(s8[6815744]{0:T(1024)(128)(4,1)} %bitcast.23), calls=%async_computation | async-start | bytes 8388608
  84.6 3.1 %collective-permute-start.19 = (bf16[256,1664]{1,0:T(8,128)(2,1)S(1)}, bf16[256,1664]{1,0:T(8,128)(2,1)S(1)}, u32[]{:S(2)}, u32[]{:S(2)}) collective-permute-start(bf16[256,1664]{1,0:T(8,128)(2,1)S(1)} %gate_up.4), channel_id=1, source_target_pairs={{0,16},{1,17},{2,18},{3,19},{4,20},{5,21},{6,22},{7,23},{8,24},{9,... | collective-permute-start | bytes 2555912 | tf_op jit(solution)/shard_map/gate_up/ppermute | solution.py:30
  84.7 2.5 %collective-permute-start.18 = (bf16[256,128]{1,0:T(8,128)(2,1)S(1)}, bf16[256,128]{1,0:T(8,128)(2,1)S(1)}, u32[]{:S(2)}, u32[]{:S(2)}) collective-permute-start(bf16[256,128]{1,0:T(8,128)(2,1)S(1)} %get-tuple-element.33), channel_id=1, source_target_pairs={{0,16},{1,17},{2,18},{3,19},{4,20},{5,21},{6,22},{7,23},{8,24},{9,... | collective-permute-start | bytes 196616 | tf_op jit(solution)/shard_map/gate_up/ppermute | solution.py:30
  89.0 36.9 %slice-start.4 = ((s8[6815744]{0:T(1024)(128)(4,1)}), s8[4194304]{0:T(1024)(128)(4,1)S(1)}, s32[]{:S(2)}) async-start(s8[6815744]{0:T(1024)(128)(4,1)} %bitcast.27), calls=%async_computation.4 | async-start | bytes 8388608
  89.1 36.8 %slice-start.5 = ((s8[6815744]{0:T(1024)(128)(4,1)}), s8[2621440]{0:T(1024)(128)(4,1)S(1)}, s32[]{:S(2)}) async-start(s8[6815744]{0:T(1024)(128)(4,1)} %bitcast.27), calls=%async_computation.5 | async-start | bytes 5242880
  89.1 4.8 %collective-permute-start.22 = (bf16[256,1664]{1,0:T(8,128)(2,1)S(1)}, bf16[256,1664]{1,0:T(8,128)(2,1)S(1)}, u32[]{:S(2)}, u32[]{:S(2)}) collective-permute-start(bf16[256,1664]{1,0:T(8,128)(2,1)S(1)} %sum_up.2), channel_id=1, source_target_pairs={{0,16},{1,17},{2,18},{3,19},{4,20},{5,21},{6,22},{7,23},{8,24},{9,... | collective-permute-start | bytes 2555912 | tf_op jit(solution)/shard_map/sum_up/ppermute | solution.py:30
  89.3 9.7 %collective-permute-start.21 = (bf16[64,1792]{1,0:T(8,128)(2,1)S(1)}, bf16[64,1792]{1,0:T(8,128)(2,1)S(1)}, u32[]{:S(2)}, u32[]{:S(2)}) collective-permute-start(bf16[64,1792]{1,0:T(8,128)(2,1)S(1)} %pad_maximum_fusion.1), channel_id=1, source_target_pairs={{0,96},{1,97},{2,98},{3,99},{4,100},{5,101},{6,102},{7,103},{8,104... | collective-permute-start | bytes 688136 | tf_op jit(solution)/shard_map/sum_gate/ppermute | solution.py:30
  92.7 8.5 %collective-permute-start.20 = (bf16[64,1792]{1,0:T(8,128)(2,1)S(1)}, bf16[64,1792]{1,0:T(8,128)(2,1)S(1)}, u32[]{:S(2)}, u32[]{:S(2)}) collective-permute-start(bf16[64,1792]{1,0:T(8,128)(2,1)S(1)} %pad_maximum_fusion), channel_id=1, source_target_pairs={{0,32},{1,33},{2,34},{3,35},{4,36},{5,37},{6,38},{7,39},{8,40},{9,... | collective-permute-start | bytes 688136 | tf_op jit(solution)/shard_map/sum_gate/ppermute | solution.py:30
  94.1 9.1 %collective-permute-start.24 = (bf16[64,1664]{1,0:T(8,128)(2,1)S(1)}, bf16[64,1664]{1,0:T(8,128)(2,1)S(1)}, u32[]{:S(2)}, u32[]{:S(2)}) collective-permute-start(bf16[64,1664]{1,0:T(8,128)(2,1)S(1)} %pad_maximum_fusion.5), channel_id=1, source_target_pairs={{0,96},{1,97},{2,98},{3,99},{4,100},{5,101},{6,102},{7,103},{8,104... | collective-permute-start | bytes 638984 | tf_op jit(solution)/shard_map/sum_up/ppermute | solution.py:30
  94.9 9.7 %collective-permute-start.23 = (bf16[64,1664]{1,0:T(8,128)(2,1)S(1)}, bf16[64,1664]{1,0:T(8,128)(2,1)S(1)}, u32[]{:S(2)}, u32[]{:S(2)}) collective-permute-start(bf16[64,1664]{1,0:T(8,128)(2,1)S(1)} %pad_maximum_fusion.4), channel_id=1, source_target_pairs={{0,32},{1,33},{2,34},{3,35},{4,36},{5,37},{6,38},{7,39},{8,40},{9,... | collective-permute-start | bytes 638984 | tf_op jit(solution)/shard_map/sum_up/ppermute | solution.py:30
  105.2 6.4 %collective-permute-start.26 = (bf16[32,3456]{1,0:T(8,128)(2,1)S(1)}, bf16[32,3456]{1,0:T(8,128)(2,1)S(1)}, u32[]{:S(2)}, u32[]{:S(2)}) collective-permute-start(bf16[32,3456]{1,0:T(8,128)(2,1)S(1)} %pad_maximum_fusion.3), channel_id=1, source_target_pairs={{0,32},{1,33},{2,34},{3,35},{4,36},{5,37},{6,38},{7,39},{8,40},{9,... | collective-permute-start | bytes 663560 | tf_op jit(solution)/shard_map/sum_terms/ppermute | solution.py:30
  105.5 7.9 %collective-permute-start.25 = (bf16[32,3456]{1,0:T(8,128)(2,1)S(1)}, bf16[32,3456]{1,0:T(8,128)(2,1)S(1)}, u32[]{:S(2)}, u32[]{:S(2)}) collective-permute-start(bf16[32,3456]{1,0:T(8,128)(2,1)S(1)} %pad_maximum_fusion.2), channel_id=1, source_target_pairs={{0,96},{1,97},{2,98},{3,99},{4,100},{5,101},{6,102},{7,103},{8,104... | collective-permute-start | bytes 663560 | tf_op jit(solution)/shard_map/sum_terms/ppermute | solution.py:30
  114.2 8.9 %collective-permute-start.28 = (bf16[64,1664]{1,0:T(8,128)(2,1)S(1)}, bf16[64,1664]{1,0:T(8,128)(2,1)S(1)}, u32[]{:S(2)}, u32[]{:S(2)}) collective-permute-start(bf16[64,1664]{1,0:T(8,128)(2,1)S(1)} %fusion.5), channel_id=1, source_target_pairs={{0,32},{1,33},{2,34},{3,35},{4,36},{5,37},{6,38},{7,39},{8,40},{9,... | collective-permute-start | bytes 638984 | tf_op jit(solution)/shard_map/gather_hidden/ppermute | solution.py:30
  114.5 10.9 %collective-permute-start.30 = (bf16[64,1664]{1,0:T(8,128)(2,1)S(1)}, bf16[64,1664]{1,0:T(8,128)(2,1)S(1)}, u32[]{:S(2)}, u32[]{:S(2)}) collective-permute-start(bf16[64,1664]{1,0:T(8,128)(2,1)S(1)} %fusion.5), channel_id=1, source_target_pairs={{0,64},{1,65},{2,66},{3,67},{4,68},{5,69},{6,70},{7,71},{8,72},{9,... | collective-permute-start | bytes 638984 | tf_op jit(solution)/shard_map/gather_hidden/ppermute | solution.py:30
  117.2 8.7 %collective-permute-start.32 = (bf16[64,1664]{1,0:T(8,128)(2,1)S(1)}, bf16[64,1664]{1,0:T(8,128)(2,1)S(1)}, u32[]{:S(2)}, u32[]{:S(2)}) collective-permute-start(bf16[64,1664]{1,0:T(8,128)(2,1)S(1)} %fusion.5), channel_id=1, source_target_pairs={{0,96},{1,97},{2,98},{3,99},{4,100},{5,101},{6,102},{7,103},{8,104... | collective-permute-start | bytes 638984 | tf_op jit(solution)/shard_map/gather_hidden/ppermute | solution.py:30
  118.3 7.6 %collective-permute-start.27 = (bf16[64,1664]{1,0:T(8,128)(2,1)S(1)}, bf16[64,1664]{1,0:T(8,128)(2,1)S(1)}, u32[]{:S(2)}, u32[]{:S(2)}) collective-permute-start(bf16[64,1664]{1,0:T(8,128)(2,1)S(1)} %fusion.5), channel_id=1, source_target_pairs={{0,16},{1,17},{2,18},{3,19},{4,20},{5,21},{6,22},{7,23},{8,24},{9,... | collective-permute-start | bytes 638984 | tf_op jit(solution)/shard_map/gather_hidden/ppermute | solution.py:30
  123.1 4.0 %collective-permute-start.29 = (bf16[64,1664]{1,0:T(8,128)(2,1)S(1)}, bf16[64,1664]{1,0:T(8,128)(2,1)S(1)}, u32[]{:S(2)}, u32[]{:S(2)}) collective-permute-start(bf16[64,1664]{1,0:T(8,128)(2,1)S(1)} %collective-permute-done.28), channel_id=1, source_target_pairs={{0,16},{1,17},{2,18},{3,19},{4,20},{5,21},{6,22},{7,23},{8,24},{9,... | collective-permute-start | bytes 638984 | tf_op jit(solution)/shard_map/down/ppermute | solution.py:30
  125.4 1.8 %collective-permute-start.31 = (bf16[64,1664]{1,0:T(8,128)(2,1)S(1)}, bf16[64,1664]{1,0:T(8,128)(2,1)S(1)}, u32[]{:S(2)}, u32[]{:S(2)}) collective-permute-start(bf16[64,1664]{1,0:T(8,128)(2,1)S(1)} %collective-permute-done.30), channel_id=1, source_target_pairs={{0,16},{1,17},{2,18},{3,19},{4,20},{5,21},{6,22},{7,23},{8,24},{9,... | collective-permute-start | bytes 638984 | tf_op jit(solution)/shard_map/down/ppermute | solution.py:30
  125.9 1.5 collective-permute-start.33
  130.9 14.8 %collective-permute-start.34 = (bf16[128,2048]{1,0:T(8,128)(2,1)S(1)}, bf16[128,2048]{1,0:T(8,128)(2,1)S(1)}, u32[]{:S(2)}, u32[]{:S(2)}) collective-permute-start(bf16[128,2048]{1,0:T(8,128)(2,1)S(1)} %get-tuple-element.64), channel_id=1, source_target_pairs={{0,3},{1,0},{2,1},{3,2},{4,7},{5,4},{6,5},{7,6},{8,11},{9,8},{10,9... | collective-permute-start | bytes 1572872 | tf_op jit(solution)/shard_map/sum_down/ppermute | solution.py:30
  133.3 12.4 %collective-permute-start.35 = (bf16[128,2048]{1,0:T(8,128)(2,1)S(1)}, bf16[128,2048]{1,0:T(8,128)(2,1)S(1)}, u32[]{:S(2)}, u32[]{:S(2)}) collective-permute-start(bf16[128,2048]{1,0:T(8,128)(2,1)S(1)} %get-tuple-element.66), channel_id=1, source_target_pairs={{0,1},{1,2},{2,3},{3,0},{4,5},{5,6},{6,7},{7,4},{8,9},{9,10},{10,1... | collective-permute-start | bytes 1572872 | tf_op jit(solution)/shard_map/sum_down/ppermute | solution.py:30
  133.3 16.0 %collective-permute-start.36 = (bf16[128,2048]{1,0:T(8,128)(2,1)S(1)}, bf16[128,2048]{1,0:T(8,128)(2,1)S(1)}, u32[]{:S(2)}, u32[]{:S(2)}) collective-permute-start(bf16[128,2048]{1,0:T(8,128)(2,1)S(1)} %get-tuple-element.65), channel_id=1, source_target_pairs={{0,2},{1,3},{2,0},{3,1},{4,6},{5,7},{6,4},{7,5},{8,10},{9,11},{10,... | collective-permute-start | bytes 1572872 | tf_op jit(solution)/shard_map/sum_down/ppermute | solution.py:30
  149.5 5.0 %collective-permute-start.37 = (bf16[32,2048]{1,0:T(8,128)(2,1)S(1)}, bf16[32,2048]{1,0:T(8,128)(2,1)S(1)}, u32[]{:S(2)}, u32[]{:S(2)}) collective-permute-start(bf16[32,2048]{1,0:T(8,128)(2,1)S(1)} %get-tuple-element.61), channel_id=1, source_target_pairs={{0,12},{1,13},{2,14},{3,15},{4,0},{5,1},{6,2},{7,3},{8,4},{9,5},{1... | collective-permute-start | bytes 393224 | tf_op jit(solution)/shard_map/sum_down/ppermute | solution.py:30
  151.9 7.6 %collective-permute-start.38 = (bf16[32,2048]{1,0:T(8,128)(2,1)S(1)}, bf16[32,2048]{1,0:T(8,128)(2,1)S(1)}, u32[]{:S(2)}, u32[]{:S(2)}) collective-permute-start(bf16[32,2048]{1,0:T(8,128)(2,1)S(1)} %get-tuple-element.63), channel_id=1, source_target_pairs={{0,4},{1,5},{2,6},{3,7},{4,8},{5,9},{6,10},{7,11},{8,12},{9,13},{1... | collective-permute-start | bytes 393224 | tf_op jit(solution)/shard_map/sum_down/ppermute | solution.py:30
  151.9 7.6 %collective-permute-start.39 = (bf16[32,2048]{1,0:T(8,128)(2,1)S(1)}, bf16[32,2048]{1,0:T(8,128)(2,1)S(1)}, u32[]{:S(2)}, u32[]{:S(2)}) collective-permute-start(bf16[32,2048]{1,0:T(8,128)(2,1)S(1)} %get-tuple-element.62), channel_id=1, source_target_pairs={{0,8},{1,9},{2,10},{3,11},{4,12},{5,13},{6,14},{7,15},{8,0},{9,1},... | collective-permute-start | bytes 393224 | tf_op jit(solution)/shard_map/sum_down/ppermute | solution.py:30
  (1 other events, 2.1 us)

commit v5 on v4

--- a/solution.py
+++ b/solution.py
@@ -399,7 +399,7 @@
         return order_down(first, dot(jnp.concatenate(rest, axis=0), down_weight))
 
 
-def sum_down(down):
+def sum_down(down, middle):
     with jax.named_scope("sum_down"):
         rows, chunk = down.shape[0] // 16, down.shape[0] // 4
         far = [along_second(down[j * chunk : (j + 1) * chunk], -j) for j in (1, 3, 2)]
@@ -408,7 +408,8 @@
             cut = slice(i * rows, (i + 1) * rows)
             return add(down[cut], *[f[cut] for f in far])
 
-        return add(total(0), *[along_first(total(i).astype(BF16), -i) for i in (1, 3, 2)])
+        near = [along_first(total(i).astype(BF16), -i) for i in (1, 3, 2)]
+        return add(lax.optimization_barrier(middle + total(0)), *near)
 
 
 def local(
@@ -434,7 +435,7 @@
     with jax.named_scope("gather_scaled"):
         gathered = gather_rows(message)
     hidden = make_hidden(gathered, gate_weight, up_weight)
-    return middle + sum_down(down_product(hidden, down_weight))
+    return sum_down(down_product(hidden, down_weight), middle)
 
 
 def solution(mesh):

time: 161 us -> 161 us (level)
  no operation moved by 1% of the time
where the time goes in v5:
time: 161 us; the launch traced here: 160 us
  waiting for transfers between devices  73.8 us (46%)
  starting transfers between devices  55.4 us (34%)
  matrix products  21.4 us (13%)
  Pallas kernels  4.16 us (3%)
  other arithmetic  3.75 us (2%)
    ppermute x40, waiting for transfers between devices, send(): return lax.ppermute(value, AXES, pairs)  73.8 us
    ppermute x40, starting transfers between devices, send(): return lax.ppermute(value, AXES, pairs)  55.4 us
    dot_general x14, matrix products, dot(): return jnp.dot(left, right, preferred_element_type=F32).astype(BF16)  21.4 us
    pallas_call x1, Pallas kernels, attend(): pl.pallas_call(attend_kernel, out_shape=pltpu.VMEM(queries.shape, BF16),...  3.26 us
  transfers between devices with their start and end apart: 40, of which 31 were waited for; matrix products, arithmetic and copies ran while one was open for 10% of the time, Pallas kernels for 0%

profile of v5, /device:TPU:0, one launch (start us, length us, event | category | flops | bytes accessed | tf_op | source)
XLA Modules:
  0.0 160.4 jit_solution(378703740971481069)
XLA Ops:
  0.0 3.3 %attention.1.refs_0_ = bf16[32,2048]{1,0:T(8,128)(2,1)S(1)} custom-call(s32[32]{0:T(128)} %lengths.1, bf16[32,2048]{1,0:T(8,128)(2,1)} %refs_0_.1, bf16[32,128]{1,0:T(8,128)(2,1)} %refs_1_.1, bf16[32,128,128]{2,1,0:T(8,128)(2,1)} %refs_2_.1, bf16[32,128]{1,0:T(8,128)(2,1)} %refs_3_.1, bf16[32,128,128]{2,1,0:T(8,128)(2,1)} %refs_4_.1), custom_call_target="tpu_custom_call" | custom-call | tf_op jit(solution)/shard_map/attention/pallas_call | solution.py:247
  3.3 1.6 %collective-permute-start = (bf16[32,2048]{1,0:T(8,128)(2,1)S(1)}, bf16[32,2048]{1,0:T(8,128)(2,1)S(1)}, u32[]{:S(2)}, u32[]{:S(2)}) collective-permute-start(bf16[32,2048]{1,0:T(8,128)(2,1)S(1)} %attention.1.refs_0_), channel_id=1, source_target_pairs={{0,4},{1,5},{2,6},{3,7},{4,8},{5,9},{6,10},{7,11},{8,12},{9,13},{1... | collective-permute-start | bytes 393224 | tf_op jit(solution)/shard_map/gather_attended/ppermute | solution.py:30
  4.9 2.7 %collective-permute-start.1 = (bf16[32,2048]{1,0:T(8,128)(2,1)S(1)}, bf16[32,2048]{1,0:T(8,128)(2,1)S(1)}, u32[]{:S(2)}, u32[]{:S(2)}) collective-permute-start(bf16[32,2048]{1,0:T(8,128)(2,1)S(1)} %attention.1.refs_0_), channel_id=1, source_target_pairs={{0,8},{1,9},{2,10},{3,11},{4,12},{5,13},{6,14},{7,15},{8,0},{9,1},... | collective-permute-start | bytes 393224 | tf_op jit(solution)/shard_map/gather_attended/ppermute | solution.py:30
  7.7 1.4 collective-permute-start.2
  9.5 2.5 %collective-permute-done.1.refs_2_ = bf16[32,2048]{1,0:T(8,128)(2,1)S(1)} collective-permute-done((bf16[32,2048]{1,0:T(8,128)(2,1)S(1)}, bf16[32,2048]{1,0:T(8,128)(2,1)S(1)}, u32[]{:S(2)}, u32[]{:S(2)}) %collective-permute-start.1) | collective-permute-done | bytes 131104 | tf_op jit(solution)/shard_map/gather_attended/ppermute | solution.py:30
  12.7 2.0 %collective-permute-start.3 = (bf16[128,2048]{1,0:T(8,128)(2,1)S(1)}, bf16[128,2048]{1,0:T(8,128)(2,1)S(1)}, u32[]{:S(2)}, u32[]{:S(2)}) collective-permute-start(bf16[128,2048]{1,0:T(8,128)(2,1)S(1)} %gather_attended.1.refs_0_), channel_id=1, source_target_pairs={{0,1},{1,2},{2,3},{3,0},{4,5},{5,6},{6,7},{7,4},{8,9},{9,10},{10,1... | collective-permute-start | bytes 1572872 | tf_op jit(solution)/shard_map/gather_attended/ppermute | solution.py:30
  14.7 2.2 %collective-permute-start.5 = (bf16[128,2048]{1,0:T(8,128)(2,1)S(1)}, bf16[128,2048]{1,0:T(8,128)(2,1)S(1)}, u32[]{:S(2)}, u32[]{:S(2)}) collective-permute-start(bf16[128,2048]{1,0:T(8,128)(2,1)S(1)} %gather_attended.1.refs_0_), channel_id=1, source_target_pairs={{0,3},{1,0},{2,1},{3,2},{4,7},{5,4},{6,5},{7,6},{8,11},{9,8},{10,9... | collective-permute-start | bytes 1572872 | tf_op jit(solution)/shard_map/gather_attended/ppermute | solution.py:30
  16.9 1.8 %collective-permute-start.4 = (bf16[128,2048]{1,0:T(8,128)(2,1)S(1)}, bf16[128,2048]{1,0:T(8,128)(2,1)S(1)}, u32[]{:S(2)}, u32[]{:S(2)}) collective-permute-start(bf16[128,2048]{1,0:T(8,128)(2,1)S(1)} %gather_attended.1.refs_0_), channel_id=1, source_target_pairs={{0,2},{1,3},{2,0},{3,1},{4,6},{5,7},{6,4},{7,5},{8,10},{9,11},{10,... | collective-permute-start | bytes 1572872 | tf_op jit(solution)/shard_map/gather_attended/ppermute | solution.py:30
  18.6 2.9 %convolution_convert_fusion.13.refs_0_ = bf16[128,1024]{1,0:T(8,128)(2,1)S(1)} fusion(bf16[128,2048]{1,0:T(8,128)(2,1)S(1)} %gather_attended.1.refs_0_, bf16[2048,1024]{1,0:T(8,128)(2,1)} %param.19), kind=kOutput, calls=%fused_computation.13 | convolution fusion | flops 537001984 | bytes 4980736 | tf_op jit(solution)/shard_map/projection/dot_general | solution.py:260
  21.6 2.3 %collective-permute-done.3.refs_1_ = bf16[128,2048]{1,0:T(8,128)(2,1)S(1)} collective-permute-done((bf16[128,2048]{1,0:T(8,128)(2,1)S(1)}, bf16[128,2048]{1,0:T(8,128)(2,1)S(1)}, u32[]{:S(2)}, u32[]{:S(2)}) %collective-permute-start.3) | collective-permute-done | bytes 524320 | tf_op jit(solution)/shard_map/gather_attended/ppermute | solution.py:30
  24.7 4.5 %collective-permute-done.5.refs_3_ = bf16[128,2048]{1,0:T(8,128)(2,1)S(1)} collective-permute-done((bf16[128,2048]{1,0:T(8,128)(2,1)S(1)}, bf16[128,2048]{1,0:T(8,128)(2,1)S(1)}, u32[]{:S(2)}, u32[]{:S(2)}) %collective-permute-start.5) | collective-permute-done | bytes 524320 | tf_op jit(solution)/shard_map/gather_attended/ppermute | solution.py:30
  29.2 1.8 %collective-permute-done.4.refs_2_ = bf16[128,2048]{1,0:T(8,128)(2,1)S(1)} collective-permute-done((bf16[128,2048]{1,0:T(8,128)(2,1)S(1)}, bf16[128,2048]{1,0:T(8,128)(2,1)S(1)}, u32[]{:S(2)}, u32[]{:S(2)}) %collective-permute-start.4) | collective-permute-done | bytes 524320 | tf_op jit(solution)/shard_map/gather_attended/ppermute | solution.py:30
  34.0 1.6 %collective-permute-start.7 = (bf16[64,1024]{1,0:T(8,128)(2,1)S(1)}, bf16[64,1024]{1,0:T(8,128)(2,1)S(1)}, u32[]{:S(2)}, u32[]{:S(2)}) collective-permute-start(bf16[64,1024]{1,0:T(8,128)(2,1)S(1)} %get-tuple-element.84), channel_id=1, source_target_pairs={{0,32},{1,33},{2,34},{3,35},{4,36},{5,37},{6,38},{7,39},{8,40},{9,... | collective-permute-start | bytes 393224 | tf_op jit(solution)/shard_map/sum_projected/ppermute | solution.py:30
  35.7 1.7 %collective-permute-start.8 = (bf16[64,1024]{1,0:T(8,128)(2,1)S(1)}, bf16[64,1024]{1,0:T(8,128)(2,1)S(1)}, u32[]{:S(2)}, u32[]{:S(2)}) collective-permute-start(bf16[64,1024]{1,0:T(8,128)(2,1)S(1)} %get-tuple-element.86), channel_id=1, source_target_pairs={{0,96},{1,97},{2,98},{3,99},{4,100},{5,101},{6,102},{7,103},{8,104... | collective-permute-start | bytes 393224 | tf_op jit(solution)/shard_map/sum_projected/ppermute | solution.py:30
  37.3 2.0 %collective-permute-start.9 = (bf16[64,1024]{1,0:T(8,128)(2,1)S(1)}, bf16[64,1024]{1,0:T(8,128)(2,1)S(1)}, u32[]{:S(2)}, u32[]{:S(2)}) collective-permute-start(bf16[64,1024]{1,0:T(8,128)(2,1)S(1)} %get-tuple-element.85), channel_id=1, source_target_pairs={{0,64},{1,65},{2,66},{3,67},{4,68},{5,69},{6,70},{7,71},{8,72},{9,... | collective-permute-start | bytes 393224 | tf_op jit(solution)/shard_map/sum_projected/ppermute | solution.py:30
  39.3 1.6 collective-permute-done.7
  40.9 2.2 %collective-permute-done.8 = bf16[64,1024]{1,0:T(8,128)(2,1)S(1)} collective-permute-done((bf16[64,1024]{1,0:T(8,128)(2,1)S(1)}, bf16[64,1024]{1,0:T(8,128)(2,1)S(1)}, u32[]{:S(2)}, u32[]{:S(2)}) %collective-permute-start.8) | collective-permute-done | bytes 131104 | tf_op jit(solution)/shard_map/sum_projected/ppermute | solution.py:30
  43.1 1.8 %collective-permute-done.9 = bf16[64,1024]{1,0:T(8,128)(2,1)S(1)} collective-permute-done((bf16[64,1024]{1,0:T(8,128)(2,1)S(1)}, bf16[64,1024]{1,0:T(8,128)(2,1)S(1)}, u32[]{:S(2)}, u32[]{:S(2)}) %collective-permute-start.9) | collective-permute-done | bytes 131104 | tf_op jit(solution)/shard_map/sum_projected/ppermute | solution.py:30
  45.0 3.3 %collective-permute-start.10 = (bf16[32,1024]{1,0:T(8,128)(2,1)S(1)}, bf16[32,1024]{1,0:T(8,128)(2,1)S(1)}, u32[]{:S(2)}, u32[]{:S(2)}) collective-permute-start(bf16[32,1024]{1,0:T(8,128)(2,1)S(1)} %get-tuple-element.93), channel_id=1, source_target_pairs={{0,9},{1,10},{2,27},{3,24},{4,35},{5,32},{6,49},{7,50},{8,73},{9,7... | collective-permute-start | bytes 196616 | tf_op jit(solution)/shard_map/to_owners/ppermute | solution.py:30
  49.2 2.4 %collective-permute-done.10 = bf16[32,1024]{1,0:T(8,128)(2,1)S(1)} collective-permute-done((bf16[32,1024]{1,0:T(8,128)(2,1)S(1)}, bf16[32,1024]{1,0:T(8,128)(2,1)S(1)}, u32[]{:S(2)}, u32[]{:S(2)}) %collective-permute-start.10) | collective-permute-done | bytes 65568 | tf_op jit(solution)/shard_map/to_owners/ppermute | solution.py:30
  51.6 2.8 %collective-permute-done.11 = bf16[32,1024]{1,0:T(8,128)(2,1)S(1)} collective-permute-done((bf16[32,1024]{1,0:T(8,128)(2,1)S(1)}, bf16[32,1024]{1,0:T(8,128)(2,1)S(1)}, u32[]{:S(2)}, u32[]{:S(2)}) %collective-permute-start.11) | collective-permute-done | bytes 65568 | tf_op jit(solution)/shard_map/to_owners/ppermute | solution.py:30
  54.8 5.5 %collective-permute-start.13 = (bf16[32,2176]{1,0:T(8,128)(2,1)S(1)}, bf16[32,2176]{1,0:T(8,128)(2,1)S(1)}, u32[]{:S(2)}, u32[]{:S(2)}) collective-permute-start(bf16[32,2176]{1,0:T(8,128)(2,1)S(1)} %pad_maximum_fusion.6.refs_0_), channel_id=1, source_target_pairs={{0,8},{1,9},{2,10},{3,11},{4,12},{5,13},{6,14},{7,15},{8,0},{9,1},... | collective-permute-start | bytes 417800 | tf_op jit(solution)/shard_map/gather_scaled/ppermute | solution.py:30
  60.3 1.6 collective-permute-done.12.refs_1_
  61.8 2.9 %collective-permute-done.13.refs_2_ = bf16[32,2176]{1,0:T(8,128)(2,1)S(1)} collective-permute-done((bf16[32,2176]{1,0:T(8,128)(2,1)S(1)}, bf16[32,2176]{1,0:T(8,128)(2,1)S(1)}, u32[]{:S(2)}, u32[]{:S(2)}) %collective-permute-start.13) | collective-permute-done | bytes 139296 | tf_op jit(solution)/shard_map/gather_scaled/ppermute | solution.py:30
  65.5 3.2 %collective-permute-start.17 = (bf16[128,2176]{1,0:T(8,128)(2,1)S(1)}, bf16[128,2176]{1,0:T(8,128)(2,1)S(1)}, u32[]{:S(2)}, u32[]{:S(2)}) collective-permute-start(bf16[128,2176]{1,0:T(8,128)(2,1)S(1)} %gather_scaled.1.refs_0_), channel_id=1, source_target_pairs={{0,3},{1,0},{2,1},{3,2},{4,7},{5,4},{6,5},{7,6},{8,11},{9,8},{10,9... | collective-permute-start | bytes 1671176 | tf_op jit(solution)/shard_map/gather_scaled/ppermute | solution.py:30
  68.7 3.1 %collective-permute-start.16 = (bf16[128,2176]{1,0:T(8,128)(2,1)S(1)}, bf16[128,2176]{1,0:T(8,128)(2,1)S(1)}, u32[]{:S(2)}, u32[]{:S(2)}) collective-permute-start(bf16[128,2176]{1,0:T(8,128)(2,1)S(1)} %gather_scaled.1.refs_0_), channel_id=1, source_target_pairs={{0,2},{1,3},{2,0},{3,1},{4,6},{5,7},{6,4},{7,5},{8,10},{9,11},{10,... | collective-permute-start | bytes 1671176 | tf_op jit(solution)/shard_map/gather_scaled/ppermute | solution.py:30
  71.8 4.1 %convolution_convert_fusion.7.refs_0_ = bf16[128,1664]{1,0:T(8,128)(2,1)S(1)} fusion(bf16[2048,1664]{1,0:T(8,128)(2,1)} %param.21, bf16[128,2176]{1,0:T(8,128)(2,1)S(1)} %gather_scaled.1.refs_0_), kind=kOutput, calls=%fused_computation.7 | convolution fusion | flops 872628224 | bytes 7766016 | tf_op jit(solution)/shard_map/gate_up/dot_general | solution.py:260
  80.3 3.0 %collective-permute-done.16.refs_2_ = bf16[128,2176]{1,0:T(8,128)(2,1)S(1)} collective-permute-done((bf16[128,2176]{1,0:T(8,128)(2,1)S(1)}, bf16[128,2176]{1,0:T(8,128)(2,1)S(1)}, u32[]{:S(2)}, u32[]{:S(2)}) %collective-permute-start.16) | collective-permute-done | bytes 557088 | tf_op jit(solution)/shard_map/gather_scaled/ppermute | solution.py:30
  89.3 3.3 %collective-permute-start.21 = (bf16[64,1792]{1,0:T(8,128)(2,1)S(1)}, bf16[64,1792]{1,0:T(8,128)(2,1)S(1)}, u32[]{:S(2)}, u32[]{:S(2)}) collective-permute-start(bf16[64,1792]{1,0:T(8,128)(2,1)S(1)} %pad_maximum_fusion.1), channel_id=1, source_target_pairs={{0,96},{1,97},{2,98},{3,99},{4,100},{5,101},{6,102},{7,103},{8,104... | collective-permute-start | bytes 688136 | tf_op jit(solution)/shard_map/sum_gate/ppermute | solution.py:30
  94.9 1.3 collective-permute-start.23
  96.3 2.8 %collective-permute-done.21 = bf16[64,1792]{1,0:T(8,128)(2,1)S(1)} collective-permute-done((bf16[64,1792]{1,0:T(8,128)(2,1)S(1)}, bf16[64,1792]{1,0:T(8,128)(2,1)S(1)}, u32[]{:S(2)}, u32[]{:S(2)}) %collective-permute-start.21) | collective-permute-done | bytes 229408 | tf_op jit(solution)/shard_map/sum_gate/ppermute | solution.py:30
  99.1 2.1 %collective-permute-done.20 = bf16[64,1792]{1,0:T(8,128)(2,1)S(1)} collective-permute-done((bf16[64,1792]{1,0:T(8,128)(2,1)S(1)}, bf16[64,1792]{1,0:T(8,128)(2,1)S(1)}, u32[]{:S(2)}, u32[]{:S(2)}) %collective-permute-start.20) | collective-permute-done | bytes 229408 | tf_op jit(solution)/shard_map/sum_gate/ppermute | solution.py:30
  101.2 2.0 %collective-permute-done.24 = bf16[64,1664]{1,0:T(8,128)(2,1)S(1)} collective-permute-done((bf16[64,1664]{1,0:T(8,128)(2,1)S(1)}, bf16[64,1664]{1,0:T(8,128)(2,1)S(1)}, u32[]{:S(2)}, u32[]{:S(2)}) %collective-permute-start.24) | collective-permute-done | bytes 213024 | tf_op jit(solution)/shard_map/sum_up/ppermute | solution.py:30
  103.1 1.5 collective-permute-done.23
  105.5 1.5 collective-permute-start.25
  107.1 4.5 %collective-permute-done.26 = bf16[32,3456]{1,0:T(8,128)(2,1)S(1)} collective-permute-done((bf16[32,3456]{1,0:T(8,128)(2,1)S(1)}, bf16[32,3456]{1,0:T(8,128)(2,1)S(1)}, u32[]{:S(2)}, u32[]{:S(2)}) %collective-permute-start.26) | collective-permute-done | bytes 221216 | tf_op jit(solution)/shard_map/sum_terms/ppermute | solution.py:30
  111.5 1.9 %collective-permute-done.25 = bf16[32,3456]{1,0:T(8,128)(2,1)S(1)} collective-permute-done((bf16[32,3456]{1,0:T(8,128)(2,1)S(1)}, bf16[32,3456]{1,0:T(8,128)(2,1)S(1)}, u32[]{:S(2)}, u32[]{:S(2)}) %collective-permute-start.25) | collective-permute-done | bytes 221216 | tf_op jit(solution)/shard_map/sum_terms/ppermute | solution.py:30
  114.5 2.8 %collective-permute-start.30 = (bf16[64,1664]{1,0:T(8,128)(2,1)S(1)}, bf16[64,1664]{1,0:T(8,128)(2,1)S(1)}, u32[]{:S(2)}, u32[]{:S(2)}) collective-permute-start(bf16[64,1664]{1,0:T(8,128)(2,1)S(1)} %fusion.5), channel_id=1, source_target_pairs={{0,64},{1,65},{2,66},{3,67},{4,68},{5,69},{6,70},{7,71},{8,72},{9,... | collective-permute-start | bytes 638984 | tf_op jit(solution)/shard_map/gather_hidden/ppermute | solution.py:30
  118.3 4.8 %collective-permute-done.28 = bf16[64,1664]{1,0:T(8,128)(2,1)S(1)} collective-permute-done((bf16[64,1664]{1,0:T(8,128)(2,1)S(1)}, bf16[64,1664]{1,0:T(8,128)(2,1)S(1)}, u32[]{:S(2)}, u32[]{:S(2)}) %collective-permute-start.28) | collective-permute-done | bytes 213024 | tf_op jit(solution)/shard_map/gather_hidden/ppermute | solution.py:30
  123.1 2.3 %collective-permute-done.30 = bf16[64,1664]{1,0:T(8,128)(2,1)S(1)} collective-permute-done((bf16[64,1664]{1,0:T(8,128)(2,1)S(1)}, bf16[64,1664]{1,0:T(8,128)(2,1)S(1)}, u32[]{:S(2)}, u32[]{:S(2)}) %collective-permute-start.30) | collective-permute-done | bytes 213024 | tf_op jit(solution)/shard_map/gather_hidden/ppermute | solution.py:30
  127.4 3.1 %convolution_convert_fusion.rest = bf16[384,2048]{1,0:T(8,128)(2,1)S(1)} fusion(bf16[384,1664]{1,0:T(8,128)(2,1)S(1)} %constant_dynamic-update-slice_fusion, bf16[1664,2048]{1,0:T(8,128)(2,1)S(1)} %bitcast.28), kind=kOutput, calls=%fused_computation | convolution fusion | flops 2618032128 | bytes 9666560 | tf_op jit(solution)/shard_map/down/dot_general | solution.py:260
  130.9 2.4 %collective-permute-start.34 = (bf16[128,2048]{1,0:T(8,128)(2,1)S(1)}, bf16[128,2048]{1,0:T(8,128)(2,1)S(1)}, u32[]{:S(2)}, u32[]{:S(2)}) collective-permute-start(bf16[128,2048]{1,0:T(8,128)(2,1)S(1)} %get-tuple-element.65), channel_id=1, source_target_pairs={{0,3},{1,0},{2,1},{3,2},{4,7},{5,4},{6,5},{7,6},{8,11},{9,8},{10,9... | collective-permute-start | bytes 1572872 | tf_op jit(solution)/shard_map/sum_down/ppermute | solution.py:30
  133.3 3.2 %collective-permute-start.36 = (bf16[128,2048]{1,0:T(8,128)(2,1)S(1)}, bf16[128,2048]{1,0:T(8,128)(2,1)S(1)}, u32[]{:S(2)}, u32[]{:S(2)}) collective-permute-start(bf16[128,2048]{1,0:T(8,128)(2,1)S(1)} %get-tuple-element.66), channel_id=1, source_target_pairs={{0,2},{1,3},{2,0},{3,1},{4,6},{5,7},{6,4},{7,5},{8,10},{9,11},{10,... | collective-permute-start | bytes 1572872 | tf_op jit(solution)/shard_map/sum_down/ppermute | solution.py:30
  136.5 9.1 %collective-permute-done.34 = bf16[128,2048]{1,0:T(8,128)(2,1)S(1)} collective-permute-done((bf16[128,2048]{1,0:T(8,128)(2,1)S(1)}, bf16[128,2048]{1,0:T(8,128)(2,1)S(1)}, u32[]{:S(2)}, u32[]{:S(2)}) %collective-permute-start.34) | collective-permute-done | bytes 524320 | tf_op jit(solution)/shard_map/sum_down/ppermute | solution.py:30
  145.6 3.7 %collective-permute-done.36 = bf16[128,2048]{1,0:T(8,128)(2,1)S(1)} collective-permute-done((bf16[128,2048]{1,0:T(8,128)(2,1)S(1)}, bf16[128,2048]{1,0:T(8,128)(2,1)S(1)}, u32[]{:S(2)}, u32[]{:S(2)}) %collective-permute-start.36) | collective-permute-done | bytes 524320 | tf_op jit(solution)/shard_map/sum_down/ppermute | solution.py:30
  149.7 2.4 %collective-permute-start.37 = (bf16[32,2048]{1,0:T(8,128)(2,1)S(1)}, bf16[32,2048]{1,0:T(8,128)(2,1)S(1)}, u32[]{:S(2)}, u32[]{:S(2)}) collective-permute-start(bf16[32,2048]{1,0:T(8,128)(2,1)S(1)} %get-tuple-element.61), channel_id=1, source_target_pairs={{0,12},{1,13},{2,14},{3,15},{4,0},{5,1},{6,2},{7,3},{8,4},{9,5},{1... | collective-permute-start | bytes 393224 | tf_op jit(solution)/shard_map/sum_down/ppermute | solution.py:30
  152.1 1.7 %collective-permute-start.39 = (bf16[32,2048]{1,0:T(8,128)(2,1)S(1)}, bf16[32,2048]{1,0:T(8,128)(2,1)S(1)}, u32[]{:S(2)}, u32[]{:S(2)}) collective-permute-start(bf16[32,2048]{1,0:T(8,128)(2,1)S(1)} %get-tuple-element.62), channel_id=1, source_target_pairs={{0,8},{1,9},{2,10},{3,11},{4,12},{5,13},{6,14},{7,15},{8,0},{9,1},... | collective-permute-start | bytes 393224 | tf_op jit(solution)/shard_map/sum_down/ppermute | solution.py:30
  154.7 5.0 %collective-permute-done.38 = bf16[32,2048]{1,0:T(8,128)(2,1)S(1)} collective-permute-done((bf16[32,2048]{1,0:T(8,128)(2,1)S(1)}, bf16[32,2048]{1,0:T(8,128)(2,1)S(1)}, u32[]{:S(2)}, u32[]{:S(2)}) %collective-permute-start.38) | collective-permute-done | bytes 131104 | tf_op jit(solution)/shard_map/sum_down/ppermute | solution.py:30
  (127 shorter events, 26.7 us)
Async XLA Ops:
  3.3 20.7 %copy-start = (bf16[2048,1024]{1,0:T(8,128)(2,1)S(1)}, bf16[2048,1024]{1,0:T(8,128)(2,1)}, u32[]{:S(2)}) copy-start(bf16[2048,1024]{1,0:T(8,128)(2,1)} %param.19) | copy-start | bytes 12582916
  3.3 6.2 %collective-permute-start = (bf16[32,2048]{1,0:T(8,128)(2,1)S(1)}, bf16[32,2048]{1,0:T(8,128)(2,1)S(1)}, u32[]{:S(2)}, u32[]{:S(2)}) collective-permute-start(bf16[32,2048]{1,0:T(8,128)(2,1)S(1)} %attention.1.refs_0_), channel_id=1, source_target_pairs={{0,4},{1,5},{2,6},{3,7},{4,8},{5,9},{6,10},{7,11},{8,12},{9,13},{1... | collective-permute-start | bytes 393224 | tf_op jit(solution)/shard_map/gather_attended/ppermute | solution.py:30
  4.9 7.1 %collective-permute-start.1 = (bf16[32,2048]{1,0:T(8,128)(2,1)S(1)}, bf16[32,2048]{1,0:T(8,128)(2,1)S(1)}, u32[]{:S(2)}, u32[]{:S(2)}) collective-permute-start(bf16[32,2048]{1,0:T(8,128)(2,1)S(1)} %attention.1.refs_0_), channel_id=1, source_target_pairs={{0,8},{1,9},{2,10},{3,11},{4,12},{5,13},{6,14},{7,15},{8,0},{9,1},... | collective-permute-start | bytes 393224 | tf_op jit(solution)/shard_map/gather_attended/ppermute | solution.py:30
  7.7 5.0 %collective-permute-start.2 = (bf16[32,2048]{1,0:T(8,128)(2,1)S(1)}, bf16[32,2048]{1,0:T(8,128)(2,1)S(1)}, u32[]{:S(2)}, u32[]{:S(2)}) collective-permute-start(bf16[32,2048]{1,0:T(8,128)(2,1)S(1)} %attention.1.refs_0_), channel_id=1, source_target_pairs={{0,12},{1,13},{2,14},{3,15},{4,0},{5,1},{6,2},{7,3},{8,4},{9,5},{1... | collective-permute-start | bytes 393224 | tf_op jit(solution)/shard_map/gather_attended/ppermute | solution.py:30
  12.7 11.3 %collective-permute-start.3 = (bf16[128,2048]{1,0:T(8,128)(2,1)S(1)}, bf16[128,2048]{1,0:T(8,128)(2,1)S(1)}, u32[]{:S(2)}, u32[]{:S(2)}) collective-permute-start(bf16[128,2048]{1,0:T(8,128)(2,1)S(1)} %gather_attended.1.refs_0_), channel_id=1, source_target_pairs={{0,1},{1,2},{2,3},{3,0},{4,5},{5,6},{6,7},{7,4},{8,9},{9,10},{10,1... | collective-permute-start | bytes 1572872 | tf_op jit(solution)/shard_map/gather_attended/ppermute | solution.py:30
  14.7 14.6 %collective-permute-start.5 = (bf16[128,2048]{1,0:T(8,128)(2,1)S(1)}, bf16[128,2048]{1,0:T(8,128)(2,1)S(1)}, u32[]{:S(2)}, u32[]{:S(2)}) collective-permute-start(bf16[128,2048]{1,0:T(8,128)(2,1)S(1)} %gather_attended.1.refs_0_), channel_id=1, source_target_pairs={{0,3},{1,0},{2,1},{3,2},{4,7},{5,4},{6,5},{7,6},{8,11},{9,8},{10,9... | collective-permute-start | bytes 1572872 | tf_op jit(solution)/shard_map/gather_attended/ppermute | solution.py:30
  16.9 14.2 %collective-permute-start.4 = (bf16[128,2048]{1,0:T(8,128)(2,1)S(1)}, bf16[128,2048]{1,0:T(8,128)(2,1)S(1)}, u32[]{:S(2)}, u32[]{:S(2)}) collective-permute-start(bf16[128,2048]{1,0:T(8,128)(2,1)S(1)} %gather_attended.1.refs_0_), channel_id=1, source_target_pairs={{0,2},{1,3},{2,0},{3,1},{4,6},{5,7},{6,4},{7,5},{8,10},{9,11},{10,... | collective-permute-start | bytes 1572872 | tf_op jit(solution)/shard_map/gather_attended/ppermute | solution.py:30
  31.8 7.5 %copy-start.2 = (bf16[2048]{0:T(1024)(128)(2,1)S(1)}, bf16[2048]{0:T(1024)(128)(2,1)}, u32[]{:S(2)}) copy-start(bf16[2048]{0:T(1024)(128)(2,1)} %param.20) | copy-start | bytes 12292
  31.9 2.0 %collective-permute-start.6 = (bf16[256,1024]{1,0:T(8,128)(2,1)S(1)}, bf16[256,1024]{1,0:T(8,128)(2,1)S(1)}, u32[]{:S(2)}, u32[]{:S(2)}) collective-permute-start(bf16[256,1024]{1,0:T(8,128)(2,1)S(1)} %projection.4), channel_id=1, source_target_pairs={{0,16},{1,17},{2,18},{3,19},{4,20},{5,21},{6,22},{7,23},{8,24},{9,... | collective-permute-start | bytes 1572872 | tf_op jit(solution)/shard_map/projection/ppermute | solution.py:30
  32.0 22.4 %copy-start.1 = (f32[32,2048]{1,0:T(8,128)S(1)}, f32[32,2048]{1,0:T(8,128)}, u32[]{:S(2)}) copy-start(f32[32,2048]{1,0:T(8,128)} %param.18) | copy-start | bytes 786436
  34.0 6.9 %collective-permute-start.7 = (bf16[64,1024]{1,0:T(8,128)(2,1)S(1)}, bf16[64,1024]{1,0:T(8,128)(2,1)S(1)}, u32[]{:S(2)}, u32[]{:S(2)}) collective-permute-start(bf16[64,1024]{1,0:T(8,128)(2,1)S(1)} %get-tuple-element.84), channel_id=1, source_target_pairs={{0,32},{1,33},{2,34},{3,35},{4,36},{5,37},{6,38},{7,39},{8,40},{9,... | collective-permute-start | bytes 393224 | tf_op jit(solution)/shard_map/sum_projected/ppermute | solution.py:30
  35.7 7.4 %collective-permute-start.8 = (bf16[64,1024]{1,0:T(8,128)(2,1)S(1)}, bf16[64,1024]{1,0:T(8,128)(2,1)S(1)}, u32[]{:S(2)}, u32[]{:S(2)}) collective-permute-start(bf16[64,1024]{1,0:T(8,128)(2,1)S(1)} %get-tuple-element.86), channel_id=1, source_target_pairs={{0,96},{1,97},{2,98},{3,99},{4,100},{5,101},{6,102},{7,103},{8,104... | collective-permute-start | bytes 393224 | tf_op jit(solution)/shard_map/sum_projected/ppermute | solution.py:30
  37.3 7.6 %collective-permute-start.9 = (bf16[64,1024]{1,0:T(8,128)(2,1)S(1)}, bf16[64,1024]{1,0:T(8,128)(2,1)S(1)}, u32[]{:S(2)}, u32[]{:S(2)}) collective-permute-start(bf16[64,1024]{1,0:T(8,128)(2,1)S(1)} %get-tuple-element.85), channel_id=1, source_target_pairs={{0,64},{1,65},{2,66},{3,67},{4,68},{5,69},{6,70},{7,71},{8,72},{9,... | collective-permute-start | bytes 393224 | tf_op jit(solution)/shard_map/sum_projected/ppermute | solution.py:30
  45.0 6.6 %collective-permute-start.10 = (bf16[32,1024]{1,0:T(8,128)(2,1)S(1)}, bf16[32,1024]{1,0:T(8,128)(2,1)S(1)}, u32[]{:S(2)}, u32[]{:S(2)}) collective-permute-start(bf16[32,1024]{1,0:T(8,128)(2,1)S(1)} %get-tuple-element.93), channel_id=1, source_target_pairs={{0,9},{1,10},{2,27},{3,24},{4,35},{5,32},{6,49},{7,50},{8,73},{9,7... | collective-permute-start | bytes 196616 | tf_op jit(solution)/shard_map/to_owners/ppermute | solution.py:30
  48.3 6.2 %collective-permute-start.11 = (bf16[32,1024]{1,0:T(8,128)(2,1)S(1)}, bf16[32,1024]{1,0:T(8,128)(2,1)S(1)}, u32[]{:S(2)}, u32[]{:S(2)}) collective-permute-start(bf16[32,1024]{1,0:T(8,128)(2,1)S(1)} %get-tuple-element.94), channel_id=1, source_target_pairs={{0,8},{1,9},{2,26},{3,27},{4,34},{5,35},{6,48},{7,49},{8,72},{9,73... | collective-permute-start | bytes 196616 | tf_op jit(solution)/shard_map/to_owners/ppermute | solution.py:30
  54.7 7.1 %collective-permute-start.12 = (bf16[32,2176]{1,0:T(8,128)(2,1)S(1)}, bf16[32,2176]{1,0:T(8,128)(2,1)S(1)}, u32[]{:S(2)}, u32[]{:S(2)}) collective-permute-start(bf16[32,2176]{1,0:T(8,128)(2,1)S(1)} %pad_maximum_fusion.6.refs_0_), channel_id=1, source_target_pairs={{0,4},{1,5},{2,6},{3,7},{4,8},{5,9},{6,10},{7,11},{8,12},{9,13},{1... | collective-permute-start | bytes 417800 | tf_op jit(solution)/shard_map/gather_scaled/ppermute | solution.py:30
  54.8 10.0 %collective-permute-start.13 = (bf16[32,2176]{1,0:T(8,128)(2,1)S(1)}, bf16[32,2176]{1,0:T(8,128)(2,1)S(1)}, u32[]{:S(2)}, u32[]{:S(2)}) collective-permute-start(bf16[32,2176]{1,0:T(8,128)(2,1)S(1)} %pad_maximum_fusion.6.refs_0_), channel_id=1, source_target_pairs={{0,8},{1,9},{2,10},{3,11},{4,12},{5,13},{6,14},{7,15},{8,0},{9,1},... | collective-permute-start | bytes 417800 | tf_op jit(solution)/shard_map/gather_scaled/ppermute | solution.py:30
  60.3 5.1 %collective-permute-start.14 = (bf16[32,2176]{1,0:T(8,128)(2,1)S(1)}, bf16[32,2176]{1,0:T(8,128)(2,1)S(1)}, u32[]{:S(2)}, u32[]{:S(2)}) collective-permute-start(bf16[32,2176]{1,0:T(8,128)(2,1)S(1)} %pad_maximum_fusion.6.refs_0_), channel_id=1, source_target_pairs={{0,12},{1,13},{2,14},{3,15},{4,0},{5,1},{6,2},{7,3},{8,4},{9,5},{1... | collective-permute-start | bytes 417800 | tf_op jit(solution)/shard_map/gather_scaled/ppermute | solution.py:30
  65.3 10.6 %slice-start.2 = ((s8[6815744]{0:T(1024)(128)(4,1)}), s8[4194304]{0:T(1024)(128)(4,1)S(1)}, s32[]{:S(2)}) async-start(s8[6815744]{0:T(1024)(128)(4,1)} %bitcast.25), calls=%async_computation.2 | async-start | bytes 8388608
  65.4 10.5 %slice-start.3 = ((s8[6815744]{0:T(1024)(128)(4,1)}), s8[2621440]{0:T(1024)(128)(4,1)S(1)}, s32[]{:S(2)}) async-start(s8[6815744]{0:T(1024)(128)(4,1)} %bitcast.25), calls=%async_computation.3 | async-start | bytes 5242880
  65.4 11.7 %collective-permute-start.15 = (bf16[128,2176]{1,0:T(8,128)(2,1)S(1)}, bf16[128,2176]{1,0:T(8,128)(2,1)S(1)}, u32[]{:S(2)}, u32[]{:S(2)}) collective-permute-start(bf16[128,2176]{1,0:T(8,128)(2,1)S(1)} %gather_scaled.1.refs_0_), channel_id=1, source_target_pairs={{0,1},{1,2},{2,3},{3,0},{4,5},{5,6},{6,7},{7,4},{8,9},{9,10},{10,1... | collective-permute-start | bytes 1671176 | tf_op jit(solution)/shard_map/gather_scaled/ppermute | solution.py:30
  65.5 14.8 %collective-permute-start.17 = (bf16[128,2176]{1,0:T(8,128)(2,1)S(1)}, bf16[128,2176]{1,0:T(8,128)(2,1)S(1)}, u32[]{:S(2)}, u32[]{:S(2)}) collective-permute-start(bf16[128,2176]{1,0:T(8,128)(2,1)S(1)} %gather_scaled.1.refs_0_), channel_id=1, source_target_pairs={{0,3},{1,0},{2,1},{3,2},{4,7},{5,4},{6,5},{7,6},{8,11},{9,8},{10,9... | collective-permute-start | bytes 1671176 | tf_op jit(solution)/shard_map/gather_scaled/ppermute | solution.py:30
  68.7 14.6 %collective-permute-start.16 = (bf16[128,2176]{1,0:T(8,128)(2,1)S(1)}, bf16[128,2176]{1,0:T(8,128)(2,1)S(1)}, u32[]{:S(2)}, u32[]{:S(2)}) collective-permute-start(bf16[128,2176]{1,0:T(8,128)(2,1)S(1)} %gather_scaled.1.refs_0_), channel_id=1, source_target_pairs={{0,2},{1,3},{2,0},{3,1},{4,6},{5,7},{6,4},{7,5},{8,10},{9,11},{10,... | collective-permute-start | bytes 1671176 | tf_op jit(solution)/shard_map/gather_scaled/ppermute | solution.py:30
  75.9 2.3 %slice-start = ((s8[6815744]{0:T(1024)(128)(4,1)}), s8[4194304]{0:T(1024)(128)(4,1)S(1)}, s32[]{:S(2)}) async-start(s8[6815744]{0:T(1024)(128)(4,1)} %bitcast.23), calls=%async_computation | async-start | bytes 8388608
  84.6 3.1 %collective-permute-start.19 = (bf16[256,1664]{1,0:T(8,128)(2,1)S(1)}, bf16[256,1664]{1,0:T(8,128)(2,1)S(1)}, u32[]{:S(2)}, u32[]{:S(2)}) collective-permute-start(bf16[256,1664]{1,0:T(8,128)(2,1)S(1)} %gate_up.4), channel_id=1, source_target_pairs={{0,16},{1,17},{2,18},{3,19},{4,20},{5,21},{6,22},{7,23},{8,24},{9,... | collective-permute-start | bytes 2555912 | tf_op jit(solution)/shard_map/gate_up/ppermute | solution.py:30
  84.7 2.5 %collective-permute-start.18 = (bf16[256,128]{1,0:T(8,128)(2,1)S(1)}, bf16[256,128]{1,0:T(8,128)(2,1)S(1)}, u32[]{:S(2)}, u32[]{:S(2)}) collective-permute-start(bf16[256,128]{1,0:T(8,128)(2,1)S(1)} %get-tuple-element.33), channel_id=1, source_target_pairs={{0,16},{1,17},{2,18},{3,19},{4,20},{5,21},{6,22},{7,23},{8,24},{9,... | collective-permute-start | bytes 196616 | tf_op jit(solution)/shard_map/gate_up/ppermute | solution.py:30
  89.0 36.9 %slice-start.4 = ((s8[6815744]{0:T(1024)(128)(4,1)}), s8[4194304]{0:T(1024)(128)(4,1)S(1)}, s32[]{:S(2)}) async-start(s8[6815744]{0:T(1024)(128)(4,1)} %bitcast.27), calls=%async_computation.4 | async-start | bytes 8388608
  89.1 36.8 %slice-start.5 = ((s8[6815744]{0:T(1024)(128)(4,1)}), s8[2621440]{0:T(1024)(128)(4,1)S(1)}, s32[]{:S(2)}) async-start(s8[6815744]{0:T(1024)(128)(4,1)} %bitcast.27), calls=%async_computation.5 | async-start | bytes 5242880
  89.1 4.8 %collective-permute-start.22 = (bf16[256,1664]{1,0:T(8,128)(2,1)S(1)}, bf16[256,1664]{1,0:T(8,128)(2,1)S(1)}, u32[]{:S(2)}, u32[]{:S(2)}) collective-permute-start(bf16[256,1664]{1,0:T(8,128)(2,1)S(1)} %sum_up.2), channel_id=1, source_target_pairs={{0,16},{1,17},{2,18},{3,19},{4,20},{5,21},{6,22},{7,23},{8,24},{9,... | collective-permute-start | bytes 2555912 | tf_op jit(solution)/shard_map/sum_up/ppermute | solution.py:30
  89.3 9.7 %collective-permute-start.21 = (bf16[64,1792]{1,0:T(8,128)(2,1)S(1)}, bf16[64,1792]{1,0:T(8,128)(2,1)S(1)}, u32[]{:S(2)}, u32[]{:S(2)}) collective-permute-start(bf16[64,1792]{1,0:T(8,128)(2,1)S(1)} %pad_maximum_fusion.1), channel_id=1, source_target_pairs={{0,96},{1,97},{2,98},{3,99},{4,100},{5,101},{6,102},{7,103},{8,104... | collective-permute-start | bytes 688136 | tf_op jit(solution)/shard_map/sum_gate/ppermute | solution.py:30
  92.7 8.5 %collective-permute-start.20 = (bf16[64,1792]{1,0:T(8,128)(2,1)S(1)}, bf16[64,1792]{1,0:T(8,128)(2,1)S(1)}, u32[]{:S(2)}, u32[]{:S(2)}) collective-permute-start(bf16[64,1792]{1,0:T(8,128)(2,1)S(1)} %pad_maximum_fusion), channel_id=1, source_target_pairs={{0,32},{1,33},{2,34},{3,35},{4,36},{5,37},{6,38},{7,39},{8,40},{9,... | collective-permute-start | bytes 688136 | tf_op jit(solution)/shard_map/sum_gate/ppermute | solution.py:30
  94.1 9.1 %collective-permute-start.24 = (bf16[64,1664]{1,0:T(8,128)(2,1)S(1)}, bf16[64,1664]{1,0:T(8,128)(2,1)S(1)}, u32[]{:S(2)}, u32[]{:S(2)}) collective-permute-start(bf16[64,1664]{1,0:T(8,128)(2,1)S(1)} %pad_maximum_fusion.5), channel_id=1, source_target_pairs={{0,96},{1,97},{2,98},{3,99},{4,100},{5,101},{6,102},{7,103},{8,104... | collective-permute-start | bytes 638984 | tf_op jit(solution)/shard_map/sum_up/ppermute | solution.py:30
  94.9 9.7 %collective-permute-start.23 = (bf16[64,1664]{1,0:T(8,128)(2,1)S(1)}, bf16[64,1664]{1,0:T(8,128)(2,1)S(1)}, u32[]{:S(2)}, u32[]{:S(2)}) collective-permute-start(bf16[64,1664]{1,0:T(8,128)(2,1)S(1)} %pad_maximum_fusion.4), channel_id=1, source_target_pairs={{0,32},{1,33},{2,34},{3,35},{4,36},{5,37},{6,38},{7,39},{8,40},{9,... | collective-permute-start | bytes 638984 | tf_op jit(solution)/shard_map/sum_up/ppermute | solution.py:30
  105.2 6.4 %collective-permute-start.26 = (bf16[32,3456]{1,0:T(8,128)(2,1)S(1)}, bf16[32,3456]{1,0:T(8,128)(2,1)S(1)}, u32[]{:S(2)}, u32[]{:S(2)}) collective-permute-start(bf16[32,3456]{1,0:T(8,128)(2,1)S(1)} %pad_maximum_fusion.3), channel_id=1, source_target_pairs={{0,32},{1,33},{2,34},{3,35},{4,36},{5,37},{6,38},{7,39},{8,40},{9,... | collective-permute-start | bytes 663560 | tf_op jit(solution)/shard_map/sum_terms/ppermute | solution.py:30
  105.5 7.9 %collective-permute-start.25 = (bf16[32,3456]{1,0:T(8,128)(2,1)S(1)}, bf16[32,3456]{1,0:T(8,128)(2,1)S(1)}, u32[]{:S(2)}, u32[]{:S(2)}) collective-permute-start(bf16[32,3456]{1,0:T(8,128)(2,1)S(1)} %pad_maximum_fusion.2), channel_id=1, source_target_pairs={{0,96},{1,97},{2,98},{3,99},{4,100},{5,101},{6,102},{7,103},{8,104... | collective-permute-start | bytes 663560 | tf_op jit(solution)/shard_map/sum_terms/ppermute | solution.py:30
  114.2 8.9 %collective-permute-start.28 = (bf16[64,1664]{1,0:T(8,128)(2,1)S(1)}, bf16[64,1664]{1,0:T(8,128)(2,1)S(1)}, u32[]{:S(2)}, u32[]{:S(2)}) collective-permute-start(bf16[64,1664]{1,0:T(8,128)(2,1)S(1)} %fusion.5), channel_id=1, source_target_pairs={{0,32},{1,33},{2,34},{3,35},{4,36},{5,37},{6,38},{7,39},{8,40},{9,... | collective-permute-start | bytes 638984 | tf_op jit(solution)/shard_map/gather_hidden/ppermute | solution.py:30
  114.5 10.9 %collective-permute-start.30 = (bf16[64,1664]{1,0:T(8,128)(2,1)S(1)}, bf16[64,1664]{1,0:T(8,128)(2,1)S(1)}, u32[]{:S(2)}, u32[]{:S(2)}) collective-permute-start(bf16[64,1664]{1,0:T(8,128)(2,1)S(1)} %fusion.5), channel_id=1, source_target_pairs={{0,64},{1,65},{2,66},{3,67},{4,68},{5,69},{6,70},{7,71},{8,72},{9,... | collective-permute-start | bytes 638984 | tf_op jit(solution)/shard_map/gather_hidden/ppermute | solution.py:30
  117.2 8.7 %collective-permute-start.32 = (bf16[64,1664]{1,0:T(8,128)(2,1)S(1)}, bf16[64,1664]{1,0:T(8,128)(2,1)S(1)}, u32[]{:S(2)}, u32[]{:S(2)}) collective-permute-start(bf16[64,1664]{1,0:T(8,128)(2,1)S(1)} %fusion.5), channel_id=1, source_target_pairs={{0,96},{1,97},{2,98},{3,99},{4,100},{5,101},{6,102},{7,103},{8,104... | collective-permute-start | bytes 638984 | tf_op jit(solution)/shard_map/gather_hidden/ppermute | solution.py:30
  118.3 7.6 %collective-permute-start.27 = (bf16[64,1664]{1,0:T(8,128)(2,1)S(1)}, bf16[64,1664]{1,0:T(8,128)(2,1)S(1)}, u32[]{:S(2)}, u32[]{:S(2)}) collective-permute-start(bf16[64,1664]{1,0:T(8,128)(2,1)S(1)} %fusion.5), channel_id=1, source_target_pairs={{0,16},{1,17},{2,18},{3,19},{4,20},{5,21},{6,22},{7,23},{8,24},{9,... | collective-permute-start | bytes 638984 | tf_op jit(solution)/shard_map/gather_hidden/ppermute | solution.py:30
  123.1 4.0 %collective-permute-start.29 = (bf16[64,1664]{1,0:T(8,128)(2,1)S(1)}, bf16[64,1664]{1,0:T(8,128)(2,1)S(1)}, u32[]{:S(2)}, u32[]{:S(2)}) collective-permute-start(bf16[64,1664]{1,0:T(8,128)(2,1)S(1)} %collective-permute-done.28), channel_id=1, source_target_pairs={{0,16},{1,17},{2,18},{3,19},{4,20},{5,21},{6,22},{7,23},{8,24},{9,... | collective-permute-start | bytes 638984 | tf_op jit(solution)/shard_map/down/ppermute | solution.py:30
  125.4 1.8 %collective-permute-start.31 = (bf16[64,1664]{1,0:T(8,128)(2,1)S(1)}, bf16[64,1664]{1,0:T(8,128)(2,1)S(1)}, u32[]{:S(2)}, u32[]{:S(2)}) collective-permute-start(bf16[64,1664]{1,0:T(8,128)(2,1)S(1)} %collective-permute-done.30), channel_id=1, source_target_pairs={{0,16},{1,17},{2,18},{3,19},{4,20},{5,21},{6,22},{7,23},{8,24},{9,... | collective-permute-start | bytes 638984 | tf_op jit(solution)/shard_map/down/ppermute | solution.py:30
  125.9 1.5 collective-permute-start.33
  130.9 14.8 %collective-permute-start.34 = (bf16[128,2048]{1,0:T(8,128)(2,1)S(1)}, bf16[128,2048]{1,0:T(8,128)(2,1)S(1)}, u32[]{:S(2)}, u32[]{:S(2)}) collective-permute-start(bf16[128,2048]{1,0:T(8,128)(2,1)S(1)} %get-tuple-element.65), channel_id=1, source_target_pairs={{0,3},{1,0},{2,1},{3,2},{4,7},{5,4},{6,5},{7,6},{8,11},{9,8},{10,9... | collective-permute-start | bytes 1572872 | tf_op jit(solution)/shard_map/sum_down/ppermute | solution.py:30
  133.3 12.4 %collective-permute-start.35 = (bf16[128,2048]{1,0:T(8,128)(2,1)S(1)}, bf16[128,2048]{1,0:T(8,128)(2,1)S(1)}, u32[]{:S(2)}, u32[]{:S(2)}) collective-permute-start(bf16[128,2048]{1,0:T(8,128)(2,1)S(1)} %get-tuple-element.67), channel_id=1, source_target_pairs={{0,1},{1,2},{2,3},{3,0},{4,5},{5,6},{6,7},{7,4},{8,9},{9,10},{10,1... | collective-permute-start | bytes 1572872 | tf_op jit(solution)/shard_map/sum_down/ppermute | solution.py:30
  133.3 16.0 %collective-permute-start.36 = (bf16[128,2048]{1,0:T(8,128)(2,1)S(1)}, bf16[128,2048]{1,0:T(8,128)(2,1)S(1)}, u32[]{:S(2)}, u32[]{:S(2)}) collective-permute-start(bf16[128,2048]{1,0:T(8,128)(2,1)S(1)} %get-tuple-element.66), channel_id=1, source_target_pairs={{0,2},{1,3},{2,0},{3,1},{4,6},{5,7},{6,4},{7,5},{8,10},{9,11},{10,... | collective-permute-start | bytes 1572872 | tf_op jit(solution)/shard_map/sum_down/ppermute | solution.py:30
  149.7 5.0 %collective-permute-start.37 = (bf16[32,2048]{1,0:T(8,128)(2,1)S(1)}, bf16[32,2048]{1,0:T(8,128)(2,1)S(1)}, u32[]{:S(2)}, u32[]{:S(2)}) collective-permute-start(bf16[32,2048]{1,0:T(8,128)(2,1)S(1)} %get-tuple-element.61), channel_id=1, source_target_pairs={{0,12},{1,13},{2,14},{3,15},{4,0},{5,1},{6,2},{7,3},{8,4},{9,5},{1... | collective-permute-start | bytes 393224 | tf_op jit(solution)/shard_map/sum_down/ppermute | solution.py:30
  152.1 7.6 %collective-permute-start.38 = (bf16[32,2048]{1,0:T(8,128)(2,1)S(1)}, bf16[32,2048]{1,0:T(8,128)(2,1)S(1)}, u32[]{:S(2)}, u32[]{:S(2)}) collective-permute-start(bf16[32,2048]{1,0:T(8,128)(2,1)S(1)} %get-tuple-element.63), channel_id=1, source_target_pairs={{0,4},{1,5},{2,6},{3,7},{4,8},{5,9},{6,10},{7,11},{8,12},{9,13},{1... | collective-permute-start | bytes 393224 | tf_op jit(solution)/shard_map/sum_down/ppermute | solution.py:30
  152.1 7.6 %collective-permute-start.39 = (bf16[32,2048]{1,0:T(8,128)(2,1)S(1)}, bf16[32,2048]{1,0:T(8,128)(2,1)S(1)}, u32[]{:S(2)}, u32[]{:S(2)}) collective-permute-start(bf16[32,2048]{1,0:T(8,128)(2,1)S(1)} %get-tuple-element.62), channel_id=1, source_target_pairs={{0,8},{1,9},{2,10},{3,11},{4,12},{5,13},{6,14},{7,15},{8,0},{9,1},... | collective-permute-start | bytes 393224 | tf_op jit(solution)/shard_map/sum_down/ppermute | solution.py:30
  (1 other events, 2.1 us)
